TPU v7x, 768 devices: a whole 4x8x12 slice. The times are simulated.
768 devices in a mesh: dp: 24 (over z, x_lo), fsdp: 32 (over y, x_hi, core).
Axes of the slice: x: 4 (x_hi: 2, x_lo: 2; x = x_hi * 2 + x_lo), y: 8, z: 12, core: 2. Of those that a mesh axis runs over, the one named last changes fastest.
Arguments:
- tokens: bfloat16 [16384, 6144], P('fsdp'), may hold values from -6 to 6
- routes: int32 [16384, 2], P('fsdp'), may hold values from 0 to 7, as said below
- router_prob: float32 [16384, 2], P('fsdp'), may hold values from 0.1 to 1
- lengths: int32 [32, 8], P('fsdp'), may hold values from 1 to 96, 512 in all within a row
- pair_mask: int32 [32, 4], P('fsdp'), may hold values from 0 to 1, as said below
- margins: float32 [32, 4], P('fsdp'), may hold values from -8 to 8
- hidden_grad: bfloat16 [16384, 9216], P('fsdp', 'dp'), may hold values from -6 to 6
- gate_weight: bfloat16 [6144, 9216], P('fsdp', 'dp'), may hold values from -0.078125 to 0.078125
- up_weight: bfloat16 [6144, 9216], P('fsdp', 'dp'), may hold values from -0.078125 to 0.078125
Outputs:
- slot_grads: float32 [5120, 6144], P('fsdp', 'dp')
Inputs may be any that keep to these rules, and one draw needn't show every extreme that they name: `routes`: no row names one expert twice. Among the 512 rows of one fsdp index, between 80 and 160 rows name expert 0, and on some index exactly 160. `pair_mask`: every fsdp index's row holds at least one 1.
All inputs are finite; a program needn't handle non-finite values.
Results may differ from a plain program's by a relative error of at most 0.0029.
Values may be sent and summed in bfloat16 or wider, within the bound.
No kernel may reach another device: no remote copies, remote signals or barrier semaphores. Data moves between devices by JAX's collectives and lax.ppermute only.
A program may use at most 64 MiB of HBM per device.

v0:
```python
import jax
import jax.numpy as jnp
from jax import lax
from jax.sharding import PartitionSpec as P

CAP = 160


def slot_table(route_rows, capacity):
    count_rows = route_rows.shape[0]
    routed = jnp.any(route_rows == 0, axis=1)
    slot_of = jnp.cumsum(routed.astype(jnp.int32)) - 1
    slots = jnp.arange(capacity, dtype=jnp.int32)
    matches = (slot_of[None, :] == slots[:, None]) & routed[None, :]
    positions = jnp.arange(count_rows, dtype=jnp.int32)
    source_rows = jnp.sum(jnp.where(matches, positions[None, :], 0), axis=1)
    filled = jnp.any(matches, axis=1)
    return (source_rows, filled)


def token_scale(route_rows, prob_rows, length_row, mask_row, margin_row, loss_scale):
    count_rows = route_rows.shape[0]
    seq_count = length_row.shape[0]
    seq_ends = jnp.cumsum(length_row)
    positions = jnp.arange(count_rows, dtype=jnp.int32)
    seq_index = jnp.sum((positions[:, None] >= seq_ends[None, :]).astype(jnp.int32), axis=1)
    pair_weight = mask_row.astype(jnp.float32) * jax.nn.sigmoid(-margin_row) * loss_scale
    per_seq = jnp.stack([-pair_weight, pair_weight], axis=1).reshape(-1)
    seq_ids = jnp.arange(seq_count, dtype=jnp.int32)
    seq_weight = jnp.sum(
        jnp.where(seq_index[:, None] == seq_ids[None, :], per_seq[None, :], jnp.float32(0.0)),
        axis=1,
    )
    router_weight = jnp.sum(jnp.where(route_rows == 0, prob_rows, jnp.float32(0.0)), axis=1)
    return seq_weight * router_weight


def backward(gate_value, up_value, cotangent):
    sigmoid_gate = jax.nn.sigmoid(gate_value)
    grad_up = (cotangent * gate_value * sigmoid_gate).astype(jnp.bfloat16)
    grad_gate = (
        cotangent * up_value * sigmoid_gate * (1.0 + gate_value * (1.0 - sigmoid_gate))
    ).astype(jnp.bfloat16)
    return (grad_gate, grad_up)


def contract_last(left, right):
    return lax.dot_general(
        left, right, (((1,), (1,)), ((), ())), preferred_element_type=jnp.float32
    )


def body(
    tokens, routes, router_prob, lengths, pair_mask, margins, hidden_grad, gate_weight, up_weight
):
    total_pairs = lax.psum(jnp.sum(pair_mask.astype(jnp.float32)), "fsdp")
    loss_scale = lax.axis_size("fsdp") * margins.shape[1] / total_pairs
    coef_tok = token_scale(routes, router_prob, lengths[0], pair_mask[0], margins[0], loss_scale)
    source_rows, filled = slot_table(routes, CAP)
    slot_rows = jnp.where(filled[:, None], tokens[source_rows], jnp.zeros((), jnp.bfloat16))
    coefficient = jnp.where(filled, coef_tok[source_rows], jnp.float32(0.0))
    cotangent = coefficient[:, None] * hidden_grad[source_rows].astype(jnp.float32)
    stacked = jnp.stack([gate_weight, up_weight])
    whole = lax.all_gather(stacked, "fsdp", axis=1, tiled=True)
    gate_value = jnp.dot(slot_rows, whole[0], preferred_element_type=jnp.float32)
    up_value = jnp.dot(slot_rows, whole[1], preferred_element_type=jnp.float32)
    grad_gate, grad_up = backward(gate_value, up_value, cotangent)
    partial_value = contract_last(grad_gate, whole[0]) + contract_last(grad_up, whole[1])
    return lax.psum_scatter(partial_value, "dp", scatter_dimension=1, tiled=True)


def solution(mesh):
    placed = (
        P("fsdp", None),
        P("fsdp", None),
        P("fsdp", None),
        P("fsdp", None),
        P("fsdp", None),
        P("fsdp", None),
        P("fsdp", "dp"),
        P("fsdp", "dp"),
        P("fsdp", "dp"),
    )
    return jax.shard_map(
        body, mesh=mesh, in_specs=placed, out_specs=P("fsdp", "dp"), check_vma=False
    )
```

profile of v0, /device:TPU:32, one launch (start us, length us, event | category | flops | bytes accessed | tf_op | source)
XLA Modules:
  0.0 276.1 jit_solution(3565171545238905303)
XLA Ops:
  6.5 1.8 pad_maximum_fusion
  8.4 1.3 convert_reduce_fusion.1
  9.7 68.0 %psum.7 = f32[]{:T(128)} all-reduce(f32[]{:T(128)} %convert_reduce_fusion.1), channel_id=1, replica_groups=mesh['dp'=24,'fsdp'=32] {'fsdp'}, use_global_device_ids=true, to_apply=%region_7.8 | all-reduce | flops 1 | bytes 8 | tf_op jit(solution)/shard_map/psum | solution.py:56
  78.4 0.7 fusion.22
  79.1 0.1 copy.12
  79.2 0.1 broadcast_in_dim.59
  79.2 0.9 reduce-window.21
  80.1 0.7 fusion.16
  80.8 0.3 reduce-window.19
  81.1 0.1 slice.15
  81.2 0.7 select_reduce_fusion.2
  82.0 0.1 convert_reduce_fusion
  82.0 0.1 select_reduce_fusion.1
  82.1 0.1 slice_reduce_fusion
  82.3 0.2 select_reduce_fusion
  82.5 1.6 gather_fusion
  84.1 0.9 gather_fusion.1
  85.1 7.2 %gather_fusion.2 = bf16[160,6144]{1,0:T(8,128)(2,1)S(1)} fusion(bf16[512,6144]{1,0:T(8,128)(2,1)} %param.9, s32[1024]{0:T(1024)S(1)} %pad_clamp_fusion), kind=kCustom, calls=%fused_computation.2 | custom fusion | bytes 3932800 | tf_op jit(solution)/shard_map/gather | solution.py:60
  92.3 0.1 fusion.8
  92.4 39.1 %all-gather.2.cloned.1.call-done = bf16[2,6144,384]{2,1,0:T(8,128)(2,1)} async-done(((bf16[2,192,384]{2,1,0:T(8,128)(2,1)}), bf16[2,6144,384]{2,1,0:T(8,128)(2,1)}) %all-gather.2.cloned.1.call-update) | async-done | bytes 9437200 | tf_op jit(solution)/shard_map/all_gather | solution.py:64
  131.5 3.6 %fusion.2 = f32[160,384]{1,0:T(8,128)S(1)} fusion(bf16[2,6144,384]{2,1,0:T(8,128)(2,1)} %all-gather.2.cloned.1.call-done, bf16[160,6144]{1,0:T(8,128)(2,1)S(1)} %gather_fusion.2, pred[160]{0:T(512)(128)(4,1)S(1)} %fusion.8), kind=kOutput, calls=%fused_computation.8 | convolution fusion | flops 755957760 | bytes 6930592 | tf_op jit(solution)/shard_map/dot_general | solution.py:65
  135.1 8.6 %fusion.1 = f32[160,6144]{1,0:T(8,128)} fusion(bf16[2,6144,384]{2,1,0:T(8,128)(2,1)} %all-gather.2.cloned.1.call-done, bf16[160,6144]{1,0:T(8,128)(2,1)S(1)} %gather_fusion.2, pred[160]{0:T(512)(128)(4,1)S(1)} %fusion.8, f32[160,384]{1,0:T(8,128)S(1)} %fusion.2, bf16[160,384]{1,0:T(8,128)(2,1)S(1)} %gather_fusion.1, f32[160]{0:T(256)S(1)} %broadcast_select_fusion.4), kind=kOutput, calls=%fused_computation.7 | convolution fusion | flops 1511669760 | bytes 15704864 | tf_op jit(solution)/shard_map/dot_general | solution.py:48
  143.7 7.2 %convolution_add_fusion = f32[160,6144]{1,0:T(8,128)} fusion(f32[160,6144]{1,0:T(8,128)} %fusion.1, bf16[2,6144,384]{2,1,0:T(8,128)(2,1)} %all-gather.2.cloned.1.call-done, f32[160,384]{1,0:T(8,128)S(1)} %fusion.2, bf16[160,384]{1,0:T(8,128)(2,1)S(1)} %gather_fusion.1, f32[160]{0:T(256)S(1)} %broadcast_select_fusion.4), kind=kOutput, calls=%fused_computation.3 | convolution fusion | flops 756449280 | bytes 12952192 | tf_op jit(solution)/shard_map/dot_general | solution.py:48
  150.9 118.3 %reduce-scatter.2.cloned.1.call-done = f32[160,256]{1,0:T(8,128)} async-done(((f32[160,6144]{1,0:T(8,128)}), f32[160,256]{1,0:T(8,128)}) %reduce-scatter.2.cloned.1.call-update) | async-done | bytes 163856 | tf_op jit(solution)/shard_map/reduce_scatter | solution.py:69
  (14 shorter events, 0.2 us)
Async XLA Ops:
  6.5 77.6 %copy-start = (bf16[512,384]{1,0:T(8,128)(2,1)S(1)}, bf16[512,384]{1,0:T(8,128)(2,1)}, u32[]{:S(2)}) copy-start(bf16[512,384]{1,0:T(8,128)(2,1)} %param.15) | copy-start | bytes 1179652
  6.5 125.0 %all-gather.2.cloned.1.call-start = ((), (), s32[]{:S(2)}) async-start(), calls=%async_computation.1 | async-start | bytes 9732096 | tf_op jit(solution)/shard_map/all_gather | solution.py:64
  8.3 260.9 %reduce-scatter.2.cloned.1.call-start = ((), (), s32[]{:S(2)}) async-start(), calls=%async_computation.2 | async-start | bytes 4096000 | tf_op jit(solution)/shard_map/reduce_scatter | solution.py:69
Sparse Core Ops, SparseCore 0:
  11.3 120.1 all-gather.1
  151.1 118.1 reduce-scatter.1
where the time goes:
time: 277 us; the launch traced here: 276 us
  waiting for transfers between devices  157 us (57%)
  blocking collectives  68 us (25%)
  matrix products  19.4 us (7%)
  between operations  14.2 us (5%)
  local copies, waits for them, and re-layouts  10.1 us (4%)
  other arithmetic  6.92 us (2%)
    reduce_scatter x1, waiting for transfers between devices, body(): lax.psum_scatter(partial_value, 'dp', scatter_dimension=1, tiled=True)  118 us
    psum x1, blocking collectives, body(): total_pairs = lax.psum(jnp.sum(pair_mask.astype(jnp.float32)), 'fsdp')  68 us
    all_gather x1, waiting for transfers between devices, body(): whole = lax.all_gather(stacked, 'fsdp', axis=1, tiled=True)  39.1 us
    dot_general x2, matrix products, contract_last(): lax.dot_general(left, right, (((1,), (1,)), ((), ())), preferred_element_...  15.8 us
    gather x1, local copies, waits for them, and re-layouts, body(): tokens[source_rows]  7.22 us
  transfers between devices with their start and end apart: 2, of which 2 were waited for; matrix products, arithmetic and copies ran while one was open for 6% of the time, Pallas kernels for 0%

commit v1 on v0

v1 whole, which is shorter than its diff:
```python
import jax
import jax.numpy as jnp
from jax import lax
from jax.sharding import Mesh, PartitionSpec as P

CAP = 160
SHIFT = 2.0**19


def slot_matrix(route_rows, capacity):
    routed = jnp.any(route_rows == 0, axis=1)
    slot_of = jnp.cumsum(routed.astype(jnp.int32)) - 1
    slots = jnp.arange(capacity, dtype=jnp.int32)
    return (slot_of[None, :] == slots[:, None]) & routed[None, :]


def token_scale(route_rows, prob_rows, length_row, mask_row, margin_row):
    count_rows = route_rows.shape[0]
    seq_count = length_row.shape[0]
    seq_ends = jnp.cumsum(length_row)
    positions = jnp.arange(count_rows, dtype=jnp.int32)
    seq_index = jnp.sum((positions[:, None] >= seq_ends[None, :]).astype(jnp.int32), axis=1)
    pair_weight = mask_row.astype(jnp.float32) * jax.nn.sigmoid(-margin_row)
    per_seq = jnp.stack([-pair_weight, pair_weight], axis=1).reshape(-1)
    seq_ids = jnp.arange(seq_count, dtype=jnp.int32)
    seq_weight = jnp.sum(
        jnp.where(seq_index[:, None] == seq_ids[None, :], per_seq[None, :], jnp.float32(0.0)),
        axis=1,
    )
    router_weight = jnp.sum(jnp.where(route_rows == 0, prob_rows, jnp.float32(0.0)), axis=1)
    return seq_weight * router_weight


def backward(gate_value, up_value, cotangent):
    sigmoid_gate = jax.nn.sigmoid(gate_value)
    grad_up = (cotangent * gate_value * sigmoid_gate).astype(jnp.bfloat16)
    grad_gate = (
        cotangent * up_value * sigmoid_gate * (1.0 + gate_value * (1.0 - sigmoid_gate))
    ).astype(jnp.bfloat16)
    return (grad_gate, grad_up)


def swap(value, axis):
    return lax.ppermute(value, axis, [(0, 1), (1, 0)])


def body(
    tokens, routes, router_prob, lengths, pair_mask, margins, hidden_grad, gate_weight, up_weight
):
    n_y, n_z = lax.axis_size("y"), lax.axis_size("z")
    rows, units = gate_weight.shape
    pairs = margins.shape[1]
    own = jnp.concatenate([gate_weight, up_weight], axis=1).astype(jnp.float32) * SHIFT
    count = jnp.sum(pair_mask.astype(jnp.float32))
    own = jnp.concatenate([own, jnp.broadcast_to(count, (16, 2 * units))]).astype(jnp.float16)
    other = swap(own, "xh")
    first = lax.axis_index("xh") == 0
    both = jnp.stack([jnp.where(first, own, other), jnp.where(first, other, own)])
    whole = lax.all_gather(both, ("y", "core"), axis=0, tiled=False)
    whole = whole.reshape(n_y, 2, 2, rows + 16, 2 * units)
    total_pairs = jnp.sum(whole[:, :, :, rows, 0].astype(jnp.float32))
    loss_scale = whole.shape[0] * 4 * pairs / total_pairs
    weight = whole[:, :, :, :rows].transpose(0, 2, 1, 3, 4).astype(jnp.bfloat16)
    weight = weight.reshape(n_y * 4 * rows, 2 * units)

    taken = slot_matrix(routes, CAP)
    picks = taken.astype(jnp.bfloat16)
    slot_rows = jnp.dot(picks, tokens, preferred_element_type=jnp.float32).astype(jnp.bfloat16)
    grad_rows = jnp.dot(picks, hidden_grad, preferred_element_type=jnp.float32)
    coef_tok = token_scale(routes, router_prob, lengths[0], pair_mask[0], margins[0])
    coefficient = jnp.sum(jnp.where(taken, coef_tok[None, :], jnp.float32(0.0)), axis=1)

    cotangent = (coefficient * loss_scale)[:, None] * grad_rows
    value = jnp.dot(slot_rows, weight, preferred_element_type=jnp.float32) * (1.0 / SHIFT)
    grads = jnp.concatenate(backward(value[:, :units], value[:, units:], cotangent), axis=1)

    mine = lax.axis_index("xl")
    width = weight.shape[0] // (2 * n_z)
    columns = weight.reshape(n_z, 2, width, 2 * units)

    def partial(side):
        part = lax.dynamic_index_in_dim(columns, side, 1, keepdims=False)
        part = part.reshape(n_z * width, 2 * units)
        out = lax.dot_general(
            grads, part, (((1,), (1,)), ((), ())), preferred_element_type=jnp.float32
        )
        return out.reshape(CAP, n_z, width).transpose(1, 0, 2)

    received = swap(partial(1 - mine).astype(jnp.bfloat16), "xl")
    summed = (partial(mine) + received.astype(jnp.float32)).astype(jnp.bfloat16)
    pieces = lax.all_to_all(summed, "z", 0, 0)
    return jnp.sum(pieces.astype(jnp.float32), axis=0) * (1.0 / SHIFT)


def solution(mesh):
    n_dp, n_fsdp = mesh.devices.shape
    fine = Mesh(
        mesh.devices.reshape(n_dp // 2, 2, n_fsdp // 4, 2, 2), ("z", "xl", "y", "xh", "core")
    )
    dp, fsdp = ("z", "xl"), ("y", "xh", "core")
    placed = (P(fsdp, None),) * 6 + (P(fsdp, dp),) * 3
    return jax.shard_map(
        body, mesh=fine, in_specs=placed, out_specs=P(fsdp, dp), check_vma=False
    )
```

time: 277 us -> 201 us (0.73)
  the two profiles are of different devices: /device:TPU:32 before, /device:TPU:2 now
where the time goes in v1:
time: 201 us; the launch traced here: 200 us
  blocking collectives  111 us (55%)
  waiting for transfers between devices  26.8 us (13%)
  other arithmetic  17.5 us (9%)
  matrix products  16.7 us (8%)
  starting transfers between devices  14.6 us (7%)
  local copies, waits for them, and re-layouts  12.6 us (6%)
    all_gather x1, blocking collectives, body(): whole = lax.all_gather(both, ('y', 'core'), axis=0, tiled=False)  63.3 us
    all_to_all x1, blocking collectives, body(): pieces = lax.all_to_all(summed, 'z', 0, 0)  47.2 us
    ppermute x2, waiting for transfers between devices, swap(): return lax.ppermute(value, axis, [(0, 1), (1, 0)])  26.8 us
    ppermute x2, starting transfers between devices, swap(): return lax.ppermute(value, axis, [(0, 1), (1, 0)])  14.6 us
    convert_element_type x1, other arithmetic, body(): weight = whole[:, :, :, :rows].transpose(0, 2, 1, 3, 4).astype(jnp.bfloat16)  9.64 us
    dot_general x1, matrix products, body(): jnp.dot(slot_rows, weight, preferred_element_type=jnp.float32)  8.34 us
    convert_element_type x1, local copies, waits for them, and re-layouts, body(): weight = whole[:, :, :, :rows].transpose(0, 2, 1, 3, 4).astype(jnp.bfloat16)  8.29 us
    dot_general x2, matrix products, partial(): lax.dot_general(grads, part, (((1,), (1,)), ((), ())), preferred_element_...  8.11 us
  transfers between devices with their start and end apart: 2, of which 2 were waited for; matrix products, arithmetic and copies ran while one was open for 2% of the time, Pallas kernels for 0%

profile of v1, /device:TPU:2, one launch (start us, length us, event | category | flops | bytes accessed | tf_op | source)
XLA Modules:
  0.0 200.2 jit_solution(5813696462864559976)
XLA Ops:
  0.0 1.3 convert_reduce_fusion.2
  2.0 1.1 multiply_convert_fusion
  3.1 4.0 %collective-permute-start = (f16[208,768]{1,0:T(8,128)(2,1)S(1)}, f16[208,768]{1,0:T(8,128)(2,1)S(1)}, u32[]{:S(2)}, u32[]{:S(2)}) collective-permute-start(f16[208,768]{1,0:T(8,128)(2,1)S(1)} %concatenate.10), channel_id=1, source_target_pairs={{0,2},{2,0},{1,3},{3,1},{4,6},{6,4},{5,7},{7,5},{8,10},{10,8},{9,1... | collective-permute-start | bytes 958472 | tf_op jit(solution)/shard_map/ppermute | solution.py:44
  7.1 0.7 fusion.33
  7.9 0.3 reduce-window.19
  8.4 0.7 fusion.36
  9.3 0.8 reduce-window.21
  10.2 0.7 select_reduce_fusion.2
  11.1 0.2 select_reduce_fusion
  11.3 4.5 %collective-permute-done = f16[208,768]{1,0:T(8,128)(2,1)S(1)} collective-permute-done((f16[208,768]{1,0:T(8,128)(2,1)S(1)}, f16[208,768]{1,0:T(8,128)(2,1)S(1)}, u32[]{:S(2)}, u32[]{:S(2)}) %collective-permute-start) | collective-permute-done | bytes 319520 | tf_op jit(solution)/shard_map/ppermute | solution.py:44
  15.8 0.2 select_bitcast_fusion.1
  16.1 63.3 %all-gather.2 = f16[32,208,768]{2,1,0:T(8,128)(2,1)S(1)} all-gather(f16[2,208,768]{2,1,0:T(8,128)(2,1)S(1)} %pad_maximum_fusion), channel_id=2, replica_groups=mesh['z'=12,'xl'=2,'y'=8,'xh'=2,'core'=2] {'y','core'}, dimensions={0}, use_global_device_ids=true | all-gather | bytes 10862592 | tf_op jit(solution)/shard_map/all_gather | solution.py:59
  79.4 3.9 %copy-done.1 = f16[32,208,768]{2,1,0:T(8,128)(2,1)} copy-done((f16[32,208,768]{2,1,0:T(8,128)(2,1)}, f16[32,208,768]{2,1,0:T(8,128)(2,1)S(1)}, u32[]{:S(2)}) %copy-start.1) | copy-done | bytes 10223640
  83.3 0.6 fusion.29
  83.9 9.6 %fusion = bf16[8,2,2,192,768]{4,3,1,2,0:T(8,128)(2,1)} fusion(f16[8,2,2,208,768]{4,3,2,1,0:T(8,128)(2,1)} %bitcast.44), kind=kLoop, calls=%fused_computation.1 | loop fusion | flops 4718592 | bytes 18874368 | tf_op jit(solution)/shard_map/convert_element_type | solution.py:63
  93.5 8.3 %copy.19 = bf16[8,2,2,192,768]{4,3,2,1,0:T(8,128)(2,1)} copy(bf16[8,2,2,192,768]{4,3,1,2,0:T(8,128)(2,1)} %fusion) | data formatting | bytes 18874368 | tf_op jit(solution)/shard_map/convert_element_type | solution.py:63
  102.5 8.3 %convolution_multiply_fusion = f32[160,768]{1,0:T(8,128)S(1)} fusion(bf16[6144,768]{1,0:T(8,128)(2,1)} %bitcast.45, bf16[512,6144]{1,0:T(8,128)(2,1)} %param.9, s32[512]{0:T(512)S(1)} %add_bitcast_fusion, pred[512]{0:T(512)(128)(4,1)S(1)} %fusion.33), kind=kOutput, calls=%fused_computation.14 | convolution fusion | flops 2517852160 | bytes 16222720 | tf_op jit(solution)/shard_map/dot_general | solution.py:74
  110.9 0.3 fusion.22
  111.2 4.1 %fusion.13 = bf16[12,160,256]{2,1,0:T(8,128)(2,1)S(1)} fusion(bf16[12,2,256,768]{3,2,1,0:T(8,128)(2,1)} %bitcast.46, s32[]{:T(128)S(6)} %select_n.38, bf16[160,384]{1,0:T(8,128)(2,1)S(1)} %get-tuple-element.8, bf16[160,384]{1,0:T(8,128)(2,1)S(1)} %get-tuple-element.7), kind=kOutput, calls=%fused_computation.13 | convolution fusion | flops 755957760 | bytes 5947396 | tf_op jit(solution)/shard_map/dot_general | solution.py:84
  115.2 10.6 %collective-permute-start.1 = (bf16[12,160,256]{2,1,0:T(8,128)(2,1)S(1)}, bf16[12,160,256]{2,1,0:T(8,128)(2,1)S(1)}, u32[]{:S(2)}, u32[]{:S(2)}) collective-permute-start(bf16[12,160,256]{2,1,0:T(8,128)(2,1)S(1)} %fusion.13), channel_id=1, source_target_pairs={{0,32},{32,0},{1,33},{33,1},{2,34},{34,2},{3,35},{35,3},{4,36},{36... | collective-permute-start | bytes 2949128 | tf_op jit(solution)/shard_map/ppermute | solution.py:44
  125.9 22.3 %collective-permute-done.1 = bf16[12,160,256]{2,1,0:T(8,128)(2,1)S(1)} collective-permute-done((bf16[12,160,256]{2,1,0:T(8,128)(2,1)S(1)}, bf16[12,160,256]{2,1,0:T(8,128)(2,1)S(1)}, u32[]{:S(2)}, u32[]{:S(2)}) %collective-permute-start.1) | collective-permute-done | bytes 983072 | tf_op jit(solution)/shard_map/ppermute | solution.py:44
  148.1 4.1 %fusion.7 = bf16[12,160,256]{2,1,0:T(8,128)(2,1)S(1)} fusion(bf16[12,160,256]{2,1,0:T(8,128)(2,1)S(1)} %collective-permute-done.1, bf16[12,2,256,768]{3,2,1,0:T(8,128)(2,1)} %bitcast.47, s32[]{:T(128)S(6)} %select_n.37, bf16[160,384]{1,0:T(8,128)(2,1)S(1)} %get-tuple-element.8, bf16[160,384]{1,0:T(8,128)(2,1)S(1)} %get-tuple-element.7), kind=kOutput, calls=%fused_computation.10 | convolution fusion | flops 756940800 | bytes 6930436 | tf_op jit(solution)/shard_map/dot_general | solution.py:84
  152.2 47.2 %all_to_all.5 = bf16[12,160,256]{2,1,0:T(8,128)(2,1)S(1)} all-to-all(bf16[12,160,256]{2,1,0:T(8,128)(2,1)S(1)} %fusion.7), channel_id=1, replica_groups=mesh['z'=12,'xl'=2,'y'=8,'xh'=2,'core'=2] {'z'}, dimensions={0} | all-to-all | bytes 1966080 | tf_op jit(solution)/shard_map/all_to_all | solution.py:91
  199.6 0.7 broadcast_multiply_fusion
  (18 shorter events, 1.0 us)
Async XLA Ops:
  0.0 110.9 %copy-start = (bf16[512,384]{1,0:T(8,128)(2,1)S(1)}, bf16[512,384]{1,0:T(8,128)(2,1)}, u32[]{:S(2)}) copy-start(bf16[512,384]{1,0:T(8,128)(2,1)} %param.15) | copy-start | bytes 1179652
  3.1 12.7 %collective-permute-start = (f16[208,768]{1,0:T(8,128)(2,1)S(1)}, f16[208,768]{1,0:T(8,128)(2,1)S(1)}, u32[]{:S(2)}, u32[]{:S(2)}) collective-permute-start(f16[208,768]{1,0:T(8,128)(2,1)S(1)} %concatenate.10), channel_id=1, source_target_pairs={{0,2},{2,0},{1,3},{3,1},{4,6},{6,4},{5,7},{7,5},{8,10},{10,8},{9,1... | collective-permute-start | bytes 958472 | tf_op jit(solution)/shard_map/ppermute | solution.py:44
  79.4 3.9 %copy-start.1 = (f16[32,208,768]{2,1,0:T(8,128)(2,1)}, f16[32,208,768]{2,1,0:T(8,128)(2,1)S(1)}, u32[]{:S(2)}) copy-start(f16[32,208,768]{2,1,0:T(8,128)(2,1)S(1)} %all-gather.2) | copy-start | bytes 30670852
  115.2 32.9 %collective-permute-start.1 = (bf16[12,160,256]{2,1,0:T(8,128)(2,1)S(1)}, bf16[12,160,256]{2,1,0:T(8,128)(2,1)S(1)}, u32[]{:S(2)}, u32[]{:S(2)}) collective-permute-start(bf16[12,160,256]{2,1,0:T(8,128)(2,1)S(1)} %fusion.13), channel_id=1, source_target_pairs={{0,32},{32,0},{1,33},{33,1},{2,34},{34,2},{3,35},{35,3},{4,36},{36... | collective-permute-start | bytes 2949128 | tf_op jit(solution)/shard_map/ppermute | solution.py:44

commit v2 on v1

--- a/solution.py
+++ b/solution.py
@@ -44,24 +44,40 @@
     return lax.ppermute(value, axis, [(0, 1), (1, 0)])
 
 
+def half_of(value, which, axis):
+    size = value.shape[axis] // 2
+    low = lax.slice_in_dim(value, 0, size, axis=axis)
+    high = lax.slice_in_dim(value, size, 2 * size, axis=axis)
+    return jnp.where(which == 0, low, high)
+
+
+def in_order(mine, theirs, which):
+    return jnp.where(which == 0, jnp.stack([mine, theirs]), jnp.stack([theirs, mine]))
+
+
 def body(
     tokens, routes, router_prob, lengths, pair_mask, margins, hidden_grad, gate_weight, up_weight
 ):
     n_y, n_z = lax.axis_size("y"), lax.axis_size("z")
+    core, mine, z = lax.axis_index("core"), lax.axis_index("xl"), lax.axis_index("z")
     rows, units = gate_weight.shape
     pairs = margins.shape[1]
-    own = jnp.concatenate([gate_weight, up_weight], axis=1).astype(jnp.float32) * SHIFT
+    tail = 16
     count = jnp.sum(pair_mask.astype(jnp.float32))
-    own = jnp.concatenate([own, jnp.broadcast_to(count, (16, 2 * units))]).astype(jnp.float16)
-    other = swap(own, "xh")
-    first = lax.axis_index("xh") == 0
-    both = jnp.stack([jnp.where(first, own, other), jnp.where(first, other, own)])
-    whole = lax.all_gather(both, ("y", "core"), axis=0, tiled=False)
-    whole = whole.reshape(n_y, 2, 2, rows + 16, 2 * units)
-    total_pairs = jnp.sum(whole[:, :, :, rows, 0].astype(jnp.float32))
-    loss_scale = whole.shape[0] * 4 * pairs / total_pairs
-    weight = whole[:, :, :, :rows].transpose(0, 2, 1, 3, 4).astype(jnp.bfloat16)
-    weight = weight.reshape(n_y * 4 * rows, 2 * units)
+
+    def packed(which):
+        part = [half_of(gate_weight, which, 1), half_of(up_weight, which, 1)]
+        part = jnp.concatenate(part, axis=1).astype(jnp.float32) * SHIFT
+        return jnp.concatenate([part, jnp.broadcast_to(count, (tail, units))]).astype(jnp.float16)
+
+    pair = in_order(packed(core), swap(packed(1 - core), "core"), core)
+    four = in_order(pair, swap(pair, "xh"), lax.axis_index("xh"))
+    chip_count = jnp.sum(four[:, :, rows:].astype(jnp.float32), axis=(0, 1)).astype(jnp.float16)
+    sent = jnp.concatenate([four[:, :, :rows].reshape(4 * rows, units), chip_count])
+    whole = lax.all_gather(sent, "y", axis=0, tiled=False)
+    total_pairs = jnp.sum(whole[:, 4 * rows, 0].astype(jnp.float32))
+    loss_scale = n_y * 4 * pairs / total_pairs
+    weight = whole[:, : 4 * rows].astype(jnp.bfloat16).reshape(n_y * 4 * rows, units)
 
     taken = slot_matrix(routes, CAP)
     picks = taken.astype(jnp.bfloat16)
@@ -69,27 +85,48 @@
     grad_rows = jnp.dot(picks, hidden_grad, preferred_element_type=jnp.float32)
     coef_tok = token_scale(routes, router_prob, lengths[0], pair_mask[0], margins[0])
     coefficient = jnp.sum(jnp.where(taken, coef_tok[None, :], jnp.float32(0.0)), axis=1)
+    cotangent = coefficient[:, None] * grad_rows
+    slot_rows = jnp.concatenate([slot_rows, swap(slot_rows, "core")])
+    cotangent = jnp.concatenate(
+        [half_of(cotangent, core, 1), swap(half_of(cotangent, 1 - core, 1), "core")]
+    )
 
-    cotangent = (coefficient * loss_scale)[:, None] * grad_rows
     value = jnp.dot(slot_rows, weight, preferred_element_type=jnp.float32) * (1.0 / SHIFT)
-    grads = jnp.concatenate(backward(value[:, :units], value[:, units:], cotangent), axis=1)
+    grads = jnp.concatenate(
+        backward(value[:, : units // 2], value[:, units // 2 :], cotangent * loss_scale), axis=1
+    )
 
-    mine = lax.axis_index("xl")
     width = weight.shape[0] // (2 * n_z)
-    columns = weight.reshape(n_z, 2, width, 2 * units)
+    columns = weight.reshape(n_z, 2, width, units)
 
-    def partial(side):
+    def partial(left, side):
         part = lax.dynamic_index_in_dim(columns, side, 1, keepdims=False)
-        part = part.reshape(n_z * width, 2 * units)
+        part = part.reshape(n_z * width, units)
         out = lax.dot_general(
-            grads, part, (((1,), (1,)), ((), ())), preferred_element_type=jnp.float32
+            left, part, (((1,), (1,)), ((), ())), preferred_element_type=jnp.float32
         )
         return out.reshape(CAP, n_z, width).transpose(1, 0, 2)
 
-    received = swap(partial(1 - mine).astype(jnp.bfloat16), "xl")
-    summed = (partial(mine) + received.astype(jnp.float32)).astype(jnp.bfloat16)
-    pieces = lax.all_to_all(summed, "z", 0, 0)
-    return jnp.sum(pieces.astype(jnp.float32), axis=0) * (1.0 / SHIFT)
+    def chip_sum(side):
+        return swap(partial(grads[CAP:], side), "core") + partial(grads[:CAP], side)
+
+    received = swap(chip_sum(1 - mine).astype(jnp.bfloat16), "xl")
+    total = chip_sum(mine) + received.astype(jnp.float32)
+
+    place, group = z % 3, z // 3
+    total = total.reshape(n_z // 3, 3, CAP, width)
+    kept = lax.dynamic_index_in_dim(total, place, 1, keepdims=False)
+    for step in (1, 2):
+        piece = lax.dynamic_index_in_dim(total, (place + step) % 3, 1, keepdims=False)
+        route = [(i, i // 3 * 3 + (i + step) % 3) for i in range(n_z)]
+        kept += lax.ppermute(piece.astype(jnp.bfloat16), "z", route).astype(jnp.float32)
+    groups = n_z // 3
+    result = lax.dynamic_index_in_dim(kept, group, 0, keepdims=False)
+    for step in range(1, groups):
+        piece = lax.dynamic_index_in_dim(kept, (group + step) % groups, 0, keepdims=False)
+        route = [(i, (i + 3 * step) % n_z) for i in range(n_z)]
+        result += lax.ppermute(piece.astype(jnp.bfloat16), "z", route).astype(jnp.float32)
+    return result * (1.0 / SHIFT)
 
 
 def solution(mesh):

time: 201 us -> 184 us (0.915)
  the two profiles are of different devices: /device:TPU:2 before, /device:TPU:197 now
where the time goes in v2:
time: 184 us; the launch traced here: 183 us
  blocking collectives  49.8 us (27%)
  waiting for transfers between devices  46.6 us (25%)
  starting transfers between devices  44.1 us (24%)
  matrix products  21.2 us (12%)
  other arithmetic  16.7 us (9%)
  local copies, waits for them, and re-layouts  2.84 us (2%)
  between operations  1.85 us (1%)
    all_gather x1, blocking collectives, body(): whole = lax.all_gather(sent, 'y', axis=0, tiled=False)  49.8 us
    ppermute x5, starting transfers between devices, body(): lax.ppermute(piece.astype(jnp.bfloat16), 'z', route).astype(jnp.float32)  26.6 us
    ppermute x7, waiting for transfers between devices, swap(): return lax.ppermute(value, axis, [(0, 1), (1, 0)])  24.6 us
    ppermute x5, waiting for transfers between devices, body(): lax.ppermute(piece.astype(jnp.bfloat16), 'z', route).astype(jnp.float32)  22.1 us
    ppermute x7, starting transfers between devices, swap(): return lax.ppermute(value, axis, [(0, 1), (1, 0)])  17.5 us
    dot_general x4, matrix products, partial(): lax.dot_general(left, part, (((1,), (1,)), ((), ())), preferred_element_t...  11.7 us
    dot_general x1, matrix products, body(): jnp.dot(slot_rows, weight, preferred_element_type=jnp.float32)  5.27 us
    dot_general x1, matrix products, body(): jnp.dot(picks, tokens, preferred_element_type=jnp.float32)  3.98 us
  transfers between devices with their start and end apart: 12, of which 7 were waited for; matrix products, arithmetic and copies ran while one was open for 14% of the time, Pallas kernels for 0%

profile of v2, /device:TPU:197, one launch (start us, length us, event | category | flops | bytes accessed | tf_op | source)
XLA Modules:
  0.0 183.1 jit_solution(7745468893493860531)
XLA Ops:
  5.2 2.6 %collective-permute-start = (f32[160,192]{1,0:T(8,128)}, f32[160,192]{1,0:T(8,128)}, u32[]{:S(2)}, u32[]{:S(2)}) collective-permute-start(f32[160,192]{1,0:T(8,128)} %get-tuple-element.15), channel_id=1, source_target_pairs={{0,1},{1,0},{2,3},{3,2},{4,5},{5,4},{6,7},{7,6},{8,9},{9,8},{10,11... | collective-permute-start | bytes 368648 | tf_op jit(solution)/shard_map/ppermute | solution.py:44
  14.5 2.1 %collective-permute-start.2 = (f16[2,208,384]{2,1,0:T(8,128)(2,1)S(1)}, f16[2,208,384]{2,1,0:T(8,128)(2,1)S(1)}, u32[]{:S(2)}, u32[]{:S(2)}) collective-permute-start(f16[2,208,384]{2,1,0:T(8,128)(2,1)S(1)} %maximum_select_fusion.2), channel_id=1, source_target_pairs={{0,2},{2,0},{1,3},{3,1},{4,6},{6,4},{5,7},{7,5},{8,10},{10,8},{9,1... | collective-permute-start | bytes 958472 | tf_op jit(solution)/shard_map/ppermute | solution.py:44
  16.7 4.0 %convolution_convert_fusion = bf16[160,6144]{1,0:T(8,128)(2,1)S(1)} fusion(bf16[512,6144]{1,0:T(8,128)(2,1)} %param.9, s32[512]{0:T(512)S(1)} %add_bitcast_fusion, pred[512]{0:T(512)(128)(4,1)S(1)} %fusion.59), kind=kOutput, calls=%fused_computation | convolution fusion | flops 1007779840 | bytes 8260096 | tf_op jit(solution)/shard_map/dot_general | solution.py:84
  20.7 2.3 %collective-permute-start.3 = (bf16[160,6144]{1,0:T(8,128)(2,1)S(1)}, bf16[160,6144]{1,0:T(8,128)(2,1)}, u32[]{:S(2)}, u32[]{:S(2)}) collective-permute-start(bf16[160,6144]{1,0:T(8,128)(2,1)S(1)} %convolution_convert_fusion), channel_id=1, source_target_pairs={{0,1},{1,0},{2,3},{3,2},{4,5},{5,4},{6,7},{7,6},{8,9},{9,8},{10,11... | collective-permute-start | bytes 5898248 | tf_op jit(solution)/shard_map/ppermute | solution.py:44
  23.2 3.8 %collective-permute-done.2 = f16[2,208,384]{2,1,0:T(8,128)(2,1)S(1)} collective-permute-done((f16[2,208,384]{2,1,0:T(8,128)(2,1)S(1)}, f16[2,208,384]{2,1,0:T(8,128)(2,1)S(1)}, u32[]{:S(2)}, u32[]{:S(2)}) %collective-permute-start.2) | collective-permute-done | bytes 319520 | tf_op jit(solution)/shard_map/ppermute | solution.py:44
  27.5 49.8 %all-gather.2 = f16[6272,384]{1,0:T(8,128)(2,1)S(1)} all-gather(f16[784,384]{1,0:T(8,128)(2,1)S(1)} %pad_maximum_fusion), channel_id=2, replica_groups=mesh['z'=12,'xl'=2,'y'=8,'xh'=2,'core'=2] {'y'}, dimensions={0}, use_global_device_ids=true | all-gather | bytes 5419008 | tf_op jit(solution)/shard_map/all_gather | solution.py:77
  77.3 2.2 %copy-done.2 = f16[6272,384]{1,0:T(8,128)(2,1)} copy-done((f16[6272,384]{1,0:T(8,128)(2,1)}, f16[6272,384]{1,0:T(8,128)(2,1)S(1)}, u32[]{:S(2)}) %copy-start.2) | copy-done | bytes 4816920
  80.8 3.1 %slice_convert_fusion = bf16[8,768,384]{2,1,0:T(8,128)(2,1)S(1)} fusion(f16[8,784,384]{2,1,0:T(8,128)(2,1)} %bitcast.96), kind=kLoop, calls=%fused_computation.1 | loop fusion | flops 2359296 | bytes 9437184 | tf_op jit(solution)/shard_map/convert_element_type | solution.py:80
  83.9 5.3 %fusion.26 = f32[320,384]{1,0:T(8,128)S(1)} fusion(bf16[6144,384]{1,0:T(8,128)(2,1)S(1)} %bitcast.90, bf16[160,6144]{1,0:T(8,128)(2,1)} %collective-permute-done.3, bf16[160,6144]{1,0:T(8,128)(2,1)S(1)} %convolution_convert_fusion), kind=kOutput, calls=%fused_computation.24 | convolution fusion | flops 1517936640 | bytes 9142272 | tf_op jit(solution)/shard_map/dot_general | solution.py:94
  90.4 2.3 %fusion.21 = f32[12,160,256]{2,1,0:T(8,128)} fusion(bf16[12,2,256,384]{3,2,1,0:T(8,128)(2,1)S(1)} %bitcast.91, s32[]{:T(128)S(6)} %select_n.158, bf16[320,192]{1,0:T(8,128)(2,1)S(1)} %get-tuple-element.10, bf16[320,192]{1,0:T(8,128)(2,1)S(1)} %get-tuple-element.9), kind=kOutput, calls=%fused_computation.23 | convolution fusion | flops 377733120 | bytes 4653060 | tf_op jit(solution)/shard_map/dot_general | solution.py:105
  92.6 3.8 %collective-permute-start.5 = (f32[12,160,256]{2,1,0:T(8,128)}, f32[12,160,256]{2,1,0:T(8,128)}, u32[]{:S(2)}, u32[]{:S(2)}) collective-permute-start(f32[12,160,256]{2,1,0:T(8,128)} %fusion.21), channel_id=1, source_target_pairs={{0,1},{1,0},{2,3},{3,2},{4,5},{5,4},{6,7},{7,6},{8,9},{9,8},{10,11... | collective-permute-start | bytes 5898248 | tf_op jit(solution)/shard_map/ppermute | solution.py:44
  96.4 2.6 %fusion.18 = f32[12,160,256]{2,1,0:T(8,128)S(1)} fusion(bf16[12,2,256,384]{3,2,1,0:T(8,128)(2,1)} %bitcast.92, s32[]{:T(128)S(6)} %select_n.157, bf16[320,192]{1,0:T(8,128)(2,1)S(1)} %get-tuple-element.10, bf16[320,192]{1,0:T(8,128)(2,1)S(1)} %get-tuple-element.9), kind=kOutput, calls=%fused_computation.22 | convolution fusion | flops 377733120 | bytes 4571140 | tf_op jit(solution)/shard_map/dot_general | solution.py:105
  100.9 4.3 %fusion.16 = bf16[12,160,256]{2,1,0:T(8,128)(2,1)} fusion(f32[12,160,256]{2,1,0:T(8,128)} %collective-permute-done.5, bf16[12,2,256,384]{3,2,1,0:T(8,128)(2,1)} %bitcast.93, s32[]{:T(128)S(6)} %select_n.158, bf16[320,192]{1,0:T(8,128)(2,1)S(1)} %get-tuple-element.9, bf16[320,192]{1,0:T(8,128)(2,1)S(1)} %get-tuple-element.10), kind=kOutput, calls=%fused_computation.19 | convolution fusion | flops 378716160 | bytes 5554180 | tf_op jit(solution)/shard_map/dot_general | solution.py:105
  105.2 2.8 %collective-permute-start.6 = (bf16[12,160,256]{2,1,0:T(8,128)(2,1)}, bf16[12,160,256]{2,1,0:T(8,128)(2,1)}, u32[]{:S(2)}, u32[]{:S(2)}) collective-permute-start(bf16[12,160,256]{2,1,0:T(8,128)(2,1)} %fusion.16), channel_id=1, source_target_pairs={{0,32},{32,0},{1,33},{33,1},{2,34},{34,2},{3,35},{35,3},{4,36},{36... | collective-permute-start | bytes 2949128 | tf_op jit(solution)/shard_map/ppermute | solution.py:44
  108.0 2.6 %fusion.8 = f32[160,12,256]{2,0,1:T(8,128)S(1)} fusion(bf16[12,2,256,384]{3,2,1,0:T(8,128)(2,1)} %bitcast.94, s32[]{:T(128)S(6)} %select_n.157, bf16[320,192]{1,0:T(8,128)(2,1)S(1)} %get-tuple-element.9, bf16[320,192]{1,0:T(8,128)(2,1)S(1)} %get-tuple-element.10), kind=kOutput, calls=%fused_computation.10 | convolution fusion | flops 377733120 | bytes 4571140 | tf_op jit(solution)/shard_map/dot_general | solution.py:105
  110.7 19.6 %collective-permute-done.6 = bf16[12,160,256]{2,1,0:T(8,128)(2,1)} collective-permute-done((bf16[12,160,256]{2,1,0:T(8,128)(2,1)}, bf16[12,160,256]{2,1,0:T(8,128)(2,1)}, u32[]{:S(2)}, u32[]{:S(2)}) %collective-permute-start.6) | collective-permute-done | bytes 983072 | tf_op jit(solution)/shard_map/ppermute | solution.py:44
  130.2 2.1 %fusion.17 = f32[12,160,256]{2,1,0:T(8,128)S(1)} fusion(f32[12,160,256]{2,1,0:T(8,128)} %collective-permute-done.4, f32[160,12,256]{2,0,1:T(8,128)S(1)} %fusion.8, bf16[12,160,256]{2,1,0:T(8,128)(2,1)} %collective-permute-done.6), kind=kLoop, calls=%fused_computation.21 | loop fusion | flops 1474560 | bytes 6881280 | tf_op jit(solution)/shard_map/add | solution.py:114
  132.5 5.2 %collective-permute-start.7 = (bf16[4,160,256]{2,1,0:T(8,128)(2,1)S(1)}, bf16[4,160,256]{2,1,0:T(8,128)(2,1)S(1)}, u32[]{:S(2)}, u32[]{:S(2)}) collective-permute-start(bf16[4,160,256]{2,1,0:T(8,128)(2,1)S(1)} %get-tuple-element.7), channel_id=1, source_target_pairs={{0,64},{64,128},{128,0},{192,256},{256,320},{320,192},{384,448},{4... | collective-permute-start | bytes 983048 | tf_op jit(solution)/shard_map/ppermute | solution.py:122
  137.7 3.7 %collective-permute-start.8 = (bf16[4,160,256]{2,1,0:T(8,128)(2,1)S(1)}, bf16[4,160,256]{2,1,0:T(8,128)(2,1)}, u32[]{:S(2)}, u32[]{:S(2)}) collective-permute-start(bf16[4,160,256]{2,1,0:T(8,128)(2,1)S(1)} %get-tuple-element.8), channel_id=1, source_target_pairs={{0,128},{64,0},{128,64},{192,320},{256,192},{320,256},{384,512},{4... | collective-permute-start | bytes 983048 | tf_op jit(solution)/shard_map/ppermute | solution.py:122
  141.5 4.7 %collective-permute-done.7 = bf16[4,160,256]{2,1,0:T(8,128)(2,1)S(1)} collective-permute-done((bf16[4,160,256]{2,1,0:T(8,128)(2,1)S(1)}, bf16[4,160,256]{2,1,0:T(8,128)(2,1)S(1)}, u32[]{:S(2)}, u32[]{:S(2)}) %collective-permute-start.7) | collective-permute-done | bytes 327712 | tf_op jit(solution)/shard_map/ppermute | solution.py:122
  146.2 8.6 %collective-permute-done.8 = bf16[4,160,256]{2,1,0:T(8,128)(2,1)} collective-permute-done((bf16[4,160,256]{2,1,0:T(8,128)(2,1)S(1)}, bf16[4,160,256]{2,1,0:T(8,128)(2,1)}, u32[]{:S(2)}, u32[]{:S(2)}) %collective-permute-start.8) | collective-permute-done | bytes 327712 | tf_op jit(solution)/shard_map/ppermute | solution.py:122
  155.9 7.3 %collective-permute-start.9 = (bf16[160,256]{1,0:T(8,128)(2,1)S(1)}, bf16[160,256]{1,0:T(8,128)(2,1)S(1)}, u32[]{:S(2)}, u32[]{:S(2)}) collective-permute-start(bf16[160,256]{1,0:T(8,128)(2,1)S(1)} %get-tuple-element.11), channel_id=1, source_target_pairs={{0,192},{64,256},{128,320},{192,384},{256,448},{320,512},{384,576}... | collective-permute-start | bytes 245768 | tf_op jit(solution)/shard_map/ppermute | solution.py:128
  165.1 8.5 %collective-permute-start.10 = (bf16[160,256]{1,0:T(8,128)(2,1)S(1)}, bf16[160,256]{1,0:T(8,128)(2,1)S(1)}, u32[]{:S(2)}, u32[]{:S(2)}) collective-permute-start(bf16[160,256]{1,0:T(8,128)(2,1)S(1)} %get-tuple-element.13), channel_id=1, source_target_pairs={{0,384},{64,448},{128,512},{192,576},{256,640},{320,704},{384,0},{... | collective-permute-start | bytes 245768 | tf_op jit(solution)/shard_map/ppermute | solution.py:128
  174.7 7.7 %collective-permute-done.10 = bf16[160,256]{1,0:T(8,128)(2,1)S(1)} collective-permute-done((bf16[160,256]{1,0:T(8,128)(2,1)S(1)}, bf16[160,256]{1,0:T(8,128)(2,1)S(1)}, u32[]{:S(2)}, u32[]{:S(2)}) %collective-permute-start.10) | collective-permute-done | bytes 81952 | tf_op jit(solution)/shard_map/ppermute | solution.py:128
  (53 shorter events, 20.5 us)
Async XLA Ops:
  0.0 4.1 %copy-start = (bf16[512,384]{1,0:T(8,128)(2,1)S(1)}, bf16[512,384]{1,0:T(8,128)(2,1)}, u32[]{:S(2)}) copy-start(bf16[512,384]{1,0:T(8,128)(2,1)} %param.15) | copy-start | bytes 1179652
  5.2 84.0 %collective-permute-start = (f32[160,192]{1,0:T(8,128)}, f32[160,192]{1,0:T(8,128)}, u32[]{:S(2)}, u32[]{:S(2)}) collective-permute-start(f32[160,192]{1,0:T(8,128)} %get-tuple-element.15), channel_id=1, source_target_pairs={{0,1},{1,0},{2,3},{3,2},{4,5},{5,4},{6,7},{7,6},{8,9},{9,8},{10,11... | collective-permute-start | bytes 368648 | tf_op jit(solution)/shard_map/ppermute | solution.py:44
  11.1 3.3 %collective-permute-start.1 = (f16[208,384]{1,0:T(8,128)(2,1)S(1)}, f16[208,384]{1,0:T(8,128)(2,1)S(1)}, u32[]{:S(2)}, u32[]{:S(2)}) collective-permute-start(f16[208,384]{1,0:T(8,128)(2,1)S(1)} %concatenate.42), channel_id=1, source_target_pairs={{0,1},{1,0},{2,3},{3,2},{4,5},{5,4},{6,7},{7,6},{8,9},{9,8},{10,11... | collective-permute-start | bytes 479240 | tf_op jit(solution)/shard_map/ppermute | solution.py:44
  14.5 12.4 %collective-permute-start.2 = (f16[2,208,384]{2,1,0:T(8,128)(2,1)S(1)}, f16[2,208,384]{2,1,0:T(8,128)(2,1)S(1)}, u32[]{:S(2)}, u32[]{:S(2)}) collective-permute-start(f16[2,208,384]{2,1,0:T(8,128)(2,1)S(1)} %maximum_select_fusion.2), channel_id=1, source_target_pairs={{0,2},{2,0},{1,3},{3,1},{4,6},{6,4},{5,7},{7,5},{8,10},{10,8},{9,1... | collective-permute-start | bytes 958472 | tf_op jit(solution)/shard_map/ppermute | solution.py:44
  20.7 63.3 %collective-permute-start.3 = (bf16[160,6144]{1,0:T(8,128)(2,1)S(1)}, bf16[160,6144]{1,0:T(8,128)(2,1)}, u32[]{:S(2)}, u32[]{:S(2)}) collective-permute-start(bf16[160,6144]{1,0:T(8,128)(2,1)S(1)} %convolution_convert_fusion), channel_id=1, source_target_pairs={{0,1},{1,0},{2,3},{3,2},{4,5},{5,4},{6,7},{7,6},{8,9},{9,8},{10,11... | collective-permute-start | bytes 5898248 | tf_op jit(solution)/shard_map/ppermute | solution.py:44
  77.3 2.2 %copy-start.2 = (f16[6272,384]{1,0:T(8,128)(2,1)}, f16[6272,384]{1,0:T(8,128)(2,1)S(1)}, u32[]{:S(2)}) copy-start(f16[6272,384]{1,0:T(8,128)(2,1)S(1)} %all-gather.2) | copy-start | bytes 14450692
  83.9 6.4 %copy-start.1 = (bf16[8,768,384]{2,1,0:T(8,128)(2,1)}, bf16[8,768,384]{2,1,0:T(8,128)(2,1)S(1)}, u32[]{:S(2)}) copy-start(bf16[8,768,384]{2,1,0:T(8,128)(2,1)S(1)} %slice_convert_fusion) | copy-start | bytes 14155780
  92.6 8.3 %collective-permute-start.5 = (f32[12,160,256]{2,1,0:T(8,128)}, f32[12,160,256]{2,1,0:T(8,128)}, u32[]{:S(2)}, u32[]{:S(2)}) collective-permute-start(f32[12,160,256]{2,1,0:T(8,128)} %fusion.21), channel_id=1, source_target_pairs={{0,1},{1,0},{2,3},{3,2},{4,5},{5,4},{6,7},{7,6},{8,9},{9,8},{10,11... | collective-permute-start | bytes 5898248 | tf_op jit(solution)/shard_map/ppermute | solution.py:44
  99.0 11.7 %collective-permute-start.4 = (f32[12,160,256]{2,1,0:T(8,128)S(1)}, f32[12,160,256]{2,1,0:T(8,128)}, u32[]{:S(2)}, u32[]{:S(2)}) collective-permute-start(f32[12,160,256]{2,1,0:T(8,128)S(1)} %fusion.18), channel_id=1, source_target_pairs={{0,1},{1,0},{2,3},{3,2},{4,5},{5,4},{6,7},{7,6},{8,9},{9,8},{10,11... | collective-permute-start | bytes 5898248 | tf_op jit(solution)/shard_map/ppermute | solution.py:44
  105.2 25.0 %collective-permute-start.6 = (bf16[12,160,256]{2,1,0:T(8,128)(2,1)}, bf16[12,160,256]{2,1,0:T(8,128)(2,1)}, u32[]{:S(2)}, u32[]{:S(2)}) collective-permute-start(bf16[12,160,256]{2,1,0:T(8,128)(2,1)} %fusion.16), channel_id=1, source_target_pairs={{0,32},{32,0},{1,33},{33,1},{2,34},{34,2},{3,35},{35,3},{4,36},{36... | collective-permute-start | bytes 2949128 | tf_op jit(solution)/shard_map/ppermute | solution.py:44
  132.5 13.7 %collective-permute-start.7 = (bf16[4,160,256]{2,1,0:T(8,128)(2,1)S(1)}, bf16[4,160,256]{2,1,0:T(8,128)(2,1)S(1)}, u32[]{:S(2)}, u32[]{:S(2)}) collective-permute-start(bf16[4,160,256]{2,1,0:T(8,128)(2,1)S(1)} %get-tuple-element.7), channel_id=1, source_target_pairs={{0,64},{64,128},{128,0},{192,256},{256,320},{320,192},{384,448},{4... | collective-permute-start | bytes 983048 | tf_op jit(solution)/shard_map/ppermute | solution.py:122
  137.7 17.1 %collective-permute-start.8 = (bf16[4,160,256]{2,1,0:T(8,128)(2,1)S(1)}, bf16[4,160,256]{2,1,0:T(8,128)(2,1)}, u32[]{:S(2)}, u32[]{:S(2)}) collective-permute-start(bf16[4,160,256]{2,1,0:T(8,128)(2,1)S(1)} %get-tuple-element.8), channel_id=1, source_target_pairs={{0,128},{64,0},{128,64},{192,320},{256,192},{320,256},{384,512},{4... | collective-permute-start | bytes 983048 | tf_op jit(solution)/shard_map/ppermute | solution.py:122
  155.9 17.7 %collective-permute-start.9 = (bf16[160,256]{1,0:T(8,128)(2,1)S(1)}, bf16[160,256]{1,0:T(8,128)(2,1)S(1)}, u32[]{:S(2)}, u32[]{:S(2)}) collective-permute-start(bf16[160,256]{1,0:T(8,128)(2,1)S(1)} %get-tuple-element.11), channel_id=1, source_target_pairs={{0,192},{64,256},{128,320},{192,384},{256,448},{320,512},{384,576}... | collective-permute-start | bytes 245768 | tf_op jit(solution)/shard_map/ppermute | solution.py:128
  163.2 11.6 %collective-permute-start.11 = (bf16[160,256]{1,0:T(8,128)(2,1)S(1)}, bf16[160,256]{1,0:T(8,128)(2,1)S(1)}, u32[]{:S(2)}, u32[]{:S(2)}) collective-permute-start(bf16[160,256]{1,0:T(8,128)(2,1)S(1)} %get-tuple-element.12), channel_id=1, source_target_pairs={{0,576},{64,640},{128,704},{192,0},{256,64},{320,128},{384,192},{4... | collective-permute-start | bytes 245768 | tf_op jit(solution)/shard_map/ppermute | solution.py:128
  165.1 17.3 %collective-permute-start.10 = (bf16[160,256]{1,0:T(8,128)(2,1)S(1)}, bf16[160,256]{1,0:T(8,128)(2,1)S(1)}, u32[]{:S(2)}, u32[]{:S(2)}) collective-permute-start(bf16[160,256]{1,0:T(8,128)(2,1)S(1)} %get-tuple-element.13), channel_id=1, source_target_pairs={{0,384},{64,448},{128,512},{192,576},{256,640},{320,704},{384,0},{... | collective-permute-start | bytes 245768 | tf_op jit(solution)/shard_map/ppermute | solution.py:128

commit v3 on v2

v3 whole, which is shorter than its diff:
```python
import jax
import jax.numpy as jnp
from jax import lax
from jax.sharding import Mesh, PartitionSpec as P

CAP = 160
SHIFT = 2.0**19


def slot_matrix(route_rows, capacity):
    routed = jnp.any(route_rows == 0, axis=1)
    slot_of = jnp.cumsum(routed.astype(jnp.int32)) - 1
    slots = jnp.arange(capacity, dtype=jnp.int32)
    return (slot_of[None, :] == slots[:, None]) & routed[None, :]


def token_scale(route_rows, prob_rows, length_row, mask_row, margin_row):
    count_rows = route_rows.shape[0]
    seq_count = length_row.shape[0]
    seq_ends = jnp.cumsum(length_row)
    positions = jnp.arange(count_rows, dtype=jnp.int32)
    seq_index = jnp.sum((positions[:, None] >= seq_ends[None, :]).astype(jnp.int32), axis=1)
    pair_weight = mask_row.astype(jnp.float32) * jax.nn.sigmoid(-margin_row)
    per_seq = jnp.stack([-pair_weight, pair_weight], axis=1).reshape(-1)
    seq_ids = jnp.arange(seq_count, dtype=jnp.int32)
    seq_weight = jnp.sum(
        jnp.where(seq_index[:, None] == seq_ids[None, :], per_seq[None, :], jnp.float32(0.0)),
        axis=1,
    )
    router_weight = jnp.sum(jnp.where(route_rows == 0, prob_rows, jnp.float32(0.0)), axis=1)
    return seq_weight * router_weight


def backward(gate_value, up_value, cotangent):
    sigmoid_gate = jax.nn.sigmoid(gate_value)
    grad_up = (cotangent * gate_value * sigmoid_gate).astype(jnp.bfloat16)
    grad_gate = (
        cotangent * up_value * sigmoid_gate * (1.0 + gate_value * (1.0 - sigmoid_gate))
    ).astype(jnp.bfloat16)
    return (grad_gate, grad_up)


def swap(value, axis):
    return lax.ppermute(value, axis, [(0, 1), (1, 0)])


def half_of(value, which, axis):
    size = value.shape[axis] // 2
    low = lax.slice_in_dim(value, 0, size, axis=axis)
    high = lax.slice_in_dim(value, size, 2 * size, axis=axis)
    return jnp.where(which == 0, low, high)


def in_order(mine, theirs, which):
    return jnp.where(which == 0, jnp.stack([mine, theirs]), jnp.stack([theirs, mine]))


def body(
    tokens, routes, router_prob, lengths, pair_mask, margins, hidden_grad, gate_weight, up_weight
):
    n_y, n_z = lax.axis_size("y"), lax.axis_size("z")
    core, mine, z = lax.axis_index("core"), lax.axis_index("xl"), lax.axis_index("z")
    rows, units = gate_weight.shape
    pairs = margins.shape[1]
    tail = 16
    mask_rows = jnp.pad(pair_mask.astype(jnp.float16), ((0, tail - 1), (0, units - pairs)))

    def packed(which):
        low = which * (units // 2)
        part = [lax.slice_in_dim(w, low, low + units // 2, axis=1) for w in (gate_weight, up_weight)]
        part = (jnp.concatenate(part, axis=1).astype(jnp.float32) * SHIFT).astype(jnp.float16)
        return jnp.concatenate([part, mask_rows])

    own = jnp.stack([packed(0), packed(1)])
    pair = in_order(own, swap(own, "xh"), lax.axis_index("xh"))
    kept = lax.dynamic_index_in_dim(pair, core, 1, keepdims=False)
    given = lax.dynamic_index_in_dim(pair, 1 - core, 1, keepdims=False)
    four = in_order(kept, swap(given, "core"), core).transpose(1, 0, 2, 3)
    chip_mask = jnp.sum(four[:, :, rows:].astype(jnp.float32), axis=(0, 1)).astype(jnp.float16)
    sent = jnp.concatenate([four[:, :, :rows].reshape(4 * rows, units), chip_mask])

    taken = slot_matrix(routes, CAP)
    picks = taken.astype(jnp.bfloat16)
    slot_rows = jnp.dot(picks, tokens, preferred_element_type=jnp.float32).astype(jnp.bfloat16)
    grad_rows = jnp.dot(picks, hidden_grad, preferred_element_type=jnp.float32)
    coef_tok = token_scale(routes, router_prob, lengths[0], pair_mask[0], margins[0])
    coefficient = jnp.sum(jnp.where(taken, coef_tok[None, :], jnp.float32(0.0)), axis=1)
    cotangent = coefficient[:, None] * grad_rows
    their_rows = swap(slot_rows, "core")
    their_cotangent = swap(half_of(cotangent, 1 - core, 1), "core")
    cotangent = half_of(cotangent, core, 1)
    sent, slot_rows, cotangent, their_rows, their_cotangent = lax.optimization_barrier(
        (sent, slot_rows, cotangent, their_rows, their_cotangent)
    )

    whole = lax.all_gather(sent, "y", axis=0, tiled=False)
    total_pairs = jnp.sum(whole[:, 4 * rows, :pairs].astype(jnp.float32))
    loss_scale = n_y * 4 * pairs / total_pairs
    weight = whole[:, : 4 * rows].astype(jnp.bfloat16).reshape(n_y * 4 * rows, units)

    def slot_gradients(left, weight, cotangent):
        value = jnp.dot(left, weight, preferred_element_type=jnp.float32) * (1.0 / SHIFT)
        gate_value, up_value = value[:, : units // 2], value[:, units // 2 :]
        return jnp.concatenate(backward(gate_value, up_value, cotangent * loss_scale), axis=1)

    their_grads = slot_gradients(their_rows, weight, their_cotangent)

    width = weight.shape[0] // (4 * n_z)
    columns = weight.reshape(n_z, 2, 2, width, units)
    place, group, groups = z % 3, z // 3, n_z // 3

    def partial(left, part):
        out = lax.dot_general(
            left,
            part.reshape(-1, units),
            (((1,), (1,)), ((), ())),
            preferred_element_type=jnp.float32,
        )
        return out.reshape(CAP, -1, width).transpose(1, 0, 2)

    def pick(value, index, axis):
        return lax.dynamic_index_in_dim(value, index, axis, keepdims=False)

    def send(value, axis, route):
        return lax.ppermute(value.astype(jnp.bfloat16), axis, route).astype(jnp.float32)

    def three(value):
        value = value.reshape(groups, 3, *value.shape[1:])
        moved = []
        for step in (1, 2):
            route = [(i, i // 3 * 3 + (i + step) % 3) for i in range(n_z)]
            moved.append(send(pick(value, (place + step) % 3, 1), "z", route))
        return pick(value, place, 1) + moved[0] + moved[1]

    across = [(0, 1), (1, 0)]
    part = pick(columns[:, :, 0], 1 - mine, 1)
    theirs = swap(partial(their_grads, part), "core")
    own_grads = slot_gradients(slot_rows, weight, cotangent)
    leaving = (partial(own_grads, part) + theirs).astype(jnp.bfloat16)
    leaving, own_grads, their_grads = lax.optimization_barrier((leaving, own_grads, their_grads))
    arrived = send(leaving, "xl", across)
    part = columns[:, :, 1]
    second = swap(partial(their_grads, part), "core") + partial(own_grads, part)
    second = three(second.reshape(n_z, 2, CAP, width))
    part = pick(columns[:, :, 0], mine, 1)
    first = swap(partial(their_grads, part), "core") + partial(own_grads, part) + arrived
    second = pick(second, mine, 1) + send(pick(second, 1 - mine, 1), "xl", across)
    first = three(first)
    total = jnp.concatenate([first, second], axis=2)
    result = pick(total, group, 0)
    for step in range(1, groups):
        route = [(i, (i + 3 * step) % n_z) for i in range(n_z)]
        result += send(pick(total, (group + step) % groups, 0), "z", route)
    return result * (1.0 / SHIFT)


def solution(mesh):
    n_dp, n_fsdp = mesh.devices.shape
    fine = Mesh(
        mesh.devices.reshape(n_dp // 2, 2, n_fsdp // 4, 2, 2), ("z", "xl", "y", "xh", "core")
    )
    dp, fsdp = ("z", "xl"), ("y", "xh", "core")
    placed = (P(fsdp, None),) * 6 + (P(fsdp, dp),) * 3
    return jax.shard_map(
        body, mesh=fine, in_specs=placed, out_specs=P(fsdp, dp), check_vma=False
    )
```

time: 184 us -> 173 us (0.940)
  the two profiles are of different devices: /device:TPU:197 before, /device:TPU:2 now
where the time goes in v3:
time: 173 us; the launch traced here: 172 us
  starting transfers between devices  56.3 us (33%)
  blocking collectives  51.5 us (30%)
  waiting for transfers between devices  30.9 us (18%)
  matrix products  19.4 us (11%)
  other arithmetic  6.4 us (4%)
  local copies, waits for them, and re-layouts  5.96 us (3%)
    all_gather x1, blocking collectives, body(): whole = lax.all_gather(sent, 'y', axis=0, tiled=False)  51.5 us
    ppermute x9, starting transfers between devices, send(): lax.ppermute(value.astype(jnp.bfloat16), axis, route).astype(jnp.float32)  39.6 us
    ppermute x9, waiting for transfers between devices, send(): lax.ppermute(value.astype(jnp.bfloat16), axis, route).astype(jnp.float32)  20.7 us
    ppermute x7, starting transfers between devices, swap(): return lax.ppermute(value, axis, [(0, 1), (1, 0)])  16.6 us
    ppermute x7, waiting for transfers between devices, swap(): return lax.ppermute(value, axis, [(0, 1), (1, 0)])  10.2 us
    dot_general x6, matrix products, partial(): lax.dot_general(left, part.reshape(-1, units), (((1,), (1,)), ((), ())),...  9.66 us
    dot_general x2, matrix products, slot_gradients(): jnp.dot(left, weight, preferred_element_type=jnp.float32) * (1.0 / SHIFT)  5.49 us
    dot_general x1, matrix products, body(): jnp.dot(picks, tokens, preferred_element_type=jnp.float32)  4.02 us
  transfers between devices with their start and end apart: 16, of which 9 were waited for; matrix products, arithmetic and copies ran while one was open for 7% of the time, Pallas kernels for 0%

profile of v3, /device:TPU:2, one launch (start us, length us, event | category | flops | bytes accessed | tf_op | source)
XLA Modules:
  0.0 171.9 jit_solution(10793986008859121648)
XLA Ops:
  1.4 4.0 %convolution_convert_fusion = bf16[160,6144]{1,0:T(8,128)(2,1)S(1)} fusion(bf16[512,6144]{1,0:T(8,128)(2,1)} %param.9, s32[512]{0:T(512)S(1)} %add_bitcast_fusion, pred[512]{0:T(512)(128)(4,1)S(1)} %fusion.65), kind=kOutput, calls=%fused_computation | convolution fusion | flops 1007779840 | bytes 8260096 | tf_op jit(solution)/shard_map/dot_general | solution.py:84
  5.5 2.1 %collective-permute-start.2 = (bf16[160,6144]{1,0:T(8,128)(2,1)S(1)}, bf16[160,6144]{1,0:T(8,128)(2,1)}, u32[]{:S(2)}, u32[]{:S(2)}) collective-permute-start(bf16[160,6144]{1,0:T(8,128)(2,1)S(1)} %convolution_convert_fusion), channel_id=1, source_target_pairs={{0,1},{1,0},{2,3},{3,2},{4,5},{5,4},{6,7},{7,6},{8,9},{9,8},{10,11... | collective-permute-start | bytes 5898248 | tf_op jit(solution)/shard_map/ppermute | solution.py:44
  8.1 4.0 %collective-permute-start = (f16[2,208,384]{2,1,0:T(8,128)(2,1)S(1)}, f16[2,208,384]{2,1,0:T(8,128)(2,1)S(1)}, u32[]{:S(2)}, u32[]{:S(2)}) collective-permute-start(f16[2,208,384]{2,1,0:T(8,128)(2,1)S(1)} %get-tuple-element.39), channel_id=1, source_target_pairs={{0,2},{2,0},{1,3},{3,1},{4,6},{6,4},{5,7},{7,5},{8,10},{10,8},{9,1... | collective-permute-start | bytes 958472 | tf_op jit(solution)/shard_map/ppermute | solution.py:44
  12.9 8.5 %collective-permute-done = f16[2,208,384]{2,1,0:T(8,128)(2,1)S(1)} collective-permute-done((f16[2,208,384]{2,1,0:T(8,128)(2,1)S(1)}, f16[2,208,384]{2,1,0:T(8,128)(2,1)S(1)}, u32[]{:S(2)}, u32[]{:S(2)}) %collective-permute-start) | collective-permute-done | bytes 319520 | tf_op jit(solution)/shard_map/ppermute | solution.py:44
  25.5 2.4 %collective-permute-start.3 = (f32[160,192]{1,0:T(8,128)}, f32[160,192]{1,0:T(8,128)S(1)}, u32[]{:S(2)}, u32[]{:S(2)}) collective-permute-start(f32[160,192]{1,0:T(8,128)} %get-tuple-element.40), channel_id=1, source_target_pairs={{0,1},{1,0},{2,3},{3,2},{4,5},{5,4},{6,7},{7,6},{8,9},{9,8},{10,11... | collective-permute-start | bytes 368648 | tf_op jit(solution)/shard_map/ppermute | solution.py:44
  29.1 51.5 %all-gather.2 = f16[6272,384]{1,0:T(8,128)(2,1)S(1)} all-gather(f16[784,384]{1,0:T(8,128)(2,1)S(1)} %pad_maximum_fusion), channel_id=2, replica_groups=mesh['z'=12,'xl'=2,'y'=8,'xh'=2,'core'=2] {'y'}, dimensions={0}, use_global_device_ids=true | all-gather | bytes 5419008 | tf_op jit(solution)/shard_map/all_gather | solution.py:96
  82.3 2.1 %copy-done.1 = bf16[8,768,384]{2,1,0:T(8,128)(2,1)} copy-done((bf16[8,768,384]{2,1,0:T(8,128)(2,1)}, bf16[8,768,384]{2,1,0:T(8,128)(2,1)S(1)}, u32[]{:S(2)}) %copy-start.1) | copy-done | bytes 4718616
  84.4 2.0 %fusion.69 = (bf16[12,2,1,128,384]{4,3,2,1,0:T(8,128)(2,1)}, bf16[12,2,1,128,384]{4,3,2,1,0:T(8,128)(2,1)S(1)}) fusion(bf16[12,2,2,128,384]{4,3,2,1,0:T(8,128)(2,1)S(1)} %bitcast.130), kind=kLoop, calls=%fused_computation.130 | loop fusion | bytes 9437184 | tf_op jit(solution)/shard_map/slice | solution.py:142
  87.1 4.3 %convolution_multiply_fusion = f32[160,384]{1,0:T(8,128)S(1)} fusion(bf16[160,6144]{1,0:T(8,128)(2,1)} %collective-permute-done.2, bf16[6144,384]{1,0:T(8,128)(2,1)} %bitcast.131), kind=kOutput, calls=%fused_computation.16 | convolution fusion | flops 755036160 | bytes 6930432 | tf_op jit(solution)/shard_map/dot_general | solution.py:102
  92.2 1.9 %collective-permute-start.4 = (f32[12,160,128]{2,1,0:T(8,128)S(1)}, f32[12,160,128]{2,1,0:T(8,128)S(1)}, u32[]{:S(2)}, u32[]{:S(2)}) collective-permute-start(f32[12,160,128]{2,1,0:T(8,128)S(1)} %convolution_bitcast_fusion.3), channel_id=1, source_target_pairs={{0,1},{1,0},{2,3},{3,2},{4,5},{5,4},{6,7},{7,6},{8,9},{9,8},{10,11... | collective-permute-start | bytes 2949128 | tf_op jit(solution)/shard_map/ppermute | solution.py:44
  97.2 2.2 %convolution_bitcast_fusion = f32[24,160,128]{2,1,0:T(8,128)} fusion(bf16[24,128,384]{2,1,0:T(8,128)(2,1)S(1)} %bitcast.136, bf16[160,384]{1,0:T(8,128)(2,1)S(1)} %pad_maximum_fusion.3), kind=kOutput, calls=%fused_computation.3 | convolution fusion | flops 377487360 | bytes 4448256 | tf_op jit(solution)/shard_map/dot_general | solution.py:113
  99.4 2.2 %collective-permute-start.9 = (f32[24,160,128]{2,1,0:T(8,128)}, f32[24,160,128]{2,1,0:T(8,128)}, u32[]{:S(2)}, u32[]{:S(2)}) collective-permute-start(f32[24,160,128]{2,1,0:T(8,128)} %convolution_bitcast_fusion), channel_id=1, source_target_pairs={{0,1},{1,0},{2,3},{3,2},{4,5},{5,4},{6,7},{7,6},{8,9},{9,8},{10,11... | collective-permute-start | bytes 5898248 | tf_op jit(solution)/shard_map/ppermute | solution.py:44
  103.1 2.1 %collective-permute-start.5 = (f32[12,160,128]{2,1,0:T(8,128)}, f32[12,160,128]{2,1,0:T(8,128)}, u32[]{:S(2)}, u32[]{:S(2)}) collective-permute-start(f32[12,160,128]{2,1,0:T(8,128)} %convolution_bitcast_fusion.2), channel_id=1, source_target_pairs={{0,1},{1,0},{2,3},{3,2},{4,5},{5,4},{6,7},{7,6},{8,9},{9,8},{10,11... | collective-permute-start | bytes 2949128 | tf_op jit(solution)/shard_map/ppermute | solution.py:44
  105.4 9.9 %collective-permute-start.6 = (bf16[12,160,128]{2,1,0:T(8,128)(2,1)S(1)}, bf16[12,160,128]{2,1,0:T(8,128)(2,1)S(1)}, u32[]{:S(2)}, u32[]{:S(2)}) collective-permute-start(bf16[12,160,128]{2,1,0:T(8,128)(2,1)S(1)} %fusion.3), channel_id=1, source_target_pairs={{0,32},{32,0},{1,33},{33,1},{2,34},{34,2},{3,35},{35,3},{4,36},{36... | collective-permute-start | bytes 1474568 | tf_op jit(solution)/shard_map/ppermute | solution.py:125
  115.2 3.2 %bitcast_add_fusion = f32[24,160,128]{2,1,0:T(8,128)S(1)} fusion(f32[24,160,128]{2,1,0:T(8,128)} %collective-permute-done.9, bf16[24,128,384]{2,1,0:T(8,128)(2,1)} %bitcast.135, bf16[160,384]{1,0:T(8,128)(2,1)S(1)} %pad_maximum_fusion.2), kind=kOutput, calls=%fused_computation.2 | convolution fusion | flops 377978880 | bytes 6414336 | tf_op jit(solution)/shard_map/dot_general | solution.py:113
  120.5 3.9 %collective-permute-start.10 = (bf16[4,2,160,128]{3,2,0,1:T(8,128)(2,1)S(1)}, bf16[4,2,160,128]{3,2,0,1:T(8,128)(2,1)S(1)}, u32[]{:S(2)}, u32[]{:S(2)}) collective-permute-start(bf16[4,2,160,128]{3,2,0,1:T(8,128)(2,1)S(1)} %bitcast.144), channel_id=1, source_target_pairs={{0,64},{64,128},{128,0},{192,256},{256,320},{320,192},{384,448},{4... | collective-permute-start | bytes 983048 | tf_op jit(solution)/shard_map/ppermute | solution.py:125
  124.4 2.5 %collective-permute-done.6 = bf16[12,160,128]{2,1,0:T(8,128)(2,1)S(1)} collective-permute-done((bf16[12,160,128]{2,1,0:T(8,128)(2,1)S(1)}, bf16[12,160,128]{2,1,0:T(8,128)(2,1)S(1)}, u32[]{:S(2)}, u32[]{:S(2)}) %collective-permute-start.6) | collective-permute-done | bytes 491552 | tf_op jit(solution)/shard_map/ppermute | solution.py:125
  128.7 1.9 %collective-permute-start.7 = (bf16[4,160,128]{2,1,0:T(8,128)(2,1)S(1)}, bf16[4,160,128]{2,1,0:T(8,128)(2,1)S(1)}, u32[]{:S(2)}, u32[]{:S(2)}) collective-permute-start(bf16[4,160,128]{2,1,0:T(8,128)(2,1)S(1)} %get-tuple-element.27), channel_id=1, source_target_pairs={{0,64},{64,128},{128,0},{192,256},{256,320},{320,192},{384,448},{4... | collective-permute-start | bytes 491528 | tf_op jit(solution)/shard_map/ppermute | solution.py:125
  130.6 4.8 %collective-permute-start.8 = (bf16[4,160,128]{2,1,0:T(8,128)(2,1)S(1)}, bf16[4,160,128]{2,1,0:T(8,128)(2,1)S(1)}, u32[]{:S(2)}, u32[]{:S(2)}) collective-permute-start(bf16[4,160,128]{2,1,0:T(8,128)(2,1)S(1)} %get-tuple-element.28), channel_id=1, source_target_pairs={{0,128},{64,0},{128,64},{192,320},{256,192},{320,256},{384,512},{4... | collective-permute-start | bytes 491528 | tf_op jit(solution)/shard_map/ppermute | solution.py:125
  135.5 6.1 %collective-permute-done.11 = bf16[4,2,160,128]{3,2,0,1:T(8,128)(2,1)S(1)} collective-permute-done((bf16[4,2,160,128]{3,2,0,1:T(8,128)(2,1)S(1)}, bf16[4,2,160,128]{3,2,0,1:T(8,128)(2,1)S(1)}, u32[]{:S(2)}, u32[]{:S(2)}) %collective-permute-start.11) | collective-permute-done | bytes 327712 | tf_op jit(solution)/shard_map/ppermute | solution.py:125
  144.2 4.7 %collective-permute-done.12 = bf16[4,160,128]{2,1,0:T(8,128)(2,1)S(1)} collective-permute-done((bf16[4,160,128]{2,1,0:T(8,128)(2,1)S(1)}, bf16[4,160,128]{2,1,0:T(8,128)(2,1)S(1)}, u32[]{:S(2)}, u32[]{:S(2)}) %collective-permute-start.12) | collective-permute-done | bytes 163872 | tf_op jit(solution)/shard_map/ppermute | solution.py:125
  151.0 9.1 %collective-permute-start.14 = (bf16[160,256]{1,0:T(8,128)(2,1)S(1)}, bf16[160,256]{1,0:T(8,128)(2,1)S(1)}, u32[]{:S(2)}, u32[]{:S(2)}) collective-permute-start(bf16[160,256]{1,0:T(8,128)(2,1)S(1)} %get-tuple-element.30), channel_id=1, source_target_pairs={{0,384},{64,448},{128,512},{192,576},{256,640},{320,704},{384,0},{... | collective-permute-start | bytes 245768 | tf_op jit(solution)/shard_map/ppermute | solution.py:125
  160.1 4.3 %collective-permute-start.15 = (bf16[160,256]{1,0:T(8,128)(2,1)S(1)}, bf16[160,256]{1,0:T(8,128)(2,1)S(1)}, u32[]{:S(2)}, u32[]{:S(2)}) collective-permute-start(bf16[160,256]{1,0:T(8,128)(2,1)S(1)} %get-tuple-element.31), channel_id=1, source_target_pairs={{0,576},{64,640},{128,704},{192,0},{256,64},{320,128},{384,192},{4... | collective-permute-start | bytes 245768 | tf_op jit(solution)/shard_map/ppermute | solution.py:125
  165.1 6.2 %collective-permute-done.15 = bf16[160,256]{1,0:T(8,128)(2,1)S(1)} collective-permute-done((bf16[160,256]{1,0:T(8,128)(2,1)S(1)}, bf16[160,256]{1,0:T(8,128)(2,1)S(1)}, u32[]{:S(2)}, u32[]{:S(2)}) %collective-permute-start.15) | collective-permute-done | bytes 81952 | tf_op jit(solution)/shard_map/ppermute | solution.py:125
  (100 shorter events, 24.6 us)
Async XLA Ops:
  0.0 24.4 %copy-start = (bf16[512,384]{1,0:T(8,128)(2,1)S(1)}, bf16[512,384]{1,0:T(8,128)(2,1)}, u32[]{:S(2)}) copy-start(bf16[512,384]{1,0:T(8,128)(2,1)} %param.15) | copy-start | bytes 1179652
  5.4 17.1 %copy-start.3 = (bf16[160,6144]{1,0:T(8,128)(2,1)}, bf16[160,6144]{1,0:T(8,128)(2,1)S(1)}, u32[]{:S(2)}) copy-start(bf16[160,6144]{1,0:T(8,128)(2,1)S(1)} %convolution_convert_fusion) | copy-start | bytes 5898244
  5.4 6.9 %copy-start.12 = (f32[1,4]{1,0:T(1,128)S(1)}, f32[1,4]{1,0:T(1,128)}, u32[]{:S(2)}) copy-start(f32[1,4]{1,0:T(1,128)} %param.14) | copy-start | bytes 52
  5.5 7.2 %copy-start.9 = (s32[512,2]{0,1:T(2,128)S(1)}, s32[512,2]{0,1:T(2,128)}, u32[]{:S(2)}) copy-start(s32[512,2]{0,1:T(2,128)} %param.10) | copy-start | bytes 12292
  5.5 7.2 %copy-start.10 = (f32[512,2]{0,1:T(2,128)S(1)}, f32[512,2]{0,1:T(2,128)}, u32[]{:S(2)}) copy-start(f32[512,2]{0,1:T(2,128)} %param.11) | copy-start | bytes 12292
  5.5 23.7 %collective-permute-start.2 = (bf16[160,6144]{1,0:T(8,128)(2,1)S(1)}, bf16[160,6144]{1,0:T(8,128)(2,1)}, u32[]{:S(2)}, u32[]{:S(2)}) collective-permute-start(bf16[160,6144]{1,0:T(8,128)(2,1)S(1)} %convolution_convert_fusion), channel_id=1, source_target_pairs={{0,1},{1,0},{2,3},{3,2},{4,5},{5,4},{6,7},{7,6},{8,9},{9,8},{10,11... | collective-permute-start | bytes 5898248 | tf_op jit(solution)/shard_map/ppermute | solution.py:44
  8.1 13.3 %collective-permute-start = (f16[2,208,384]{2,1,0:T(8,128)(2,1)S(1)}, f16[2,208,384]{2,1,0:T(8,128)(2,1)S(1)}, u32[]{:S(2)}, u32[]{:S(2)}) collective-permute-start(f16[2,208,384]{2,1,0:T(8,128)(2,1)S(1)} %get-tuple-element.39), channel_id=1, source_target_pairs={{0,2},{2,0},{1,3},{3,1},{4,6},{6,4},{5,7},{7,5},{8,10},{10,8},{9,1... | collective-permute-start | bytes 958472 | tf_op jit(solution)/shard_map/ppermute | solution.py:44
  22.5 5.4 %collective-permute-start.1 = (f16[2,208,384]{2,1,0:T(8,128)(2,1)}, f16[2,208,384]{2,1,0:T(8,128)(2,1)S(1)}, u32[]{:S(2)}, u32[]{:S(2)}) collective-permute-start(f16[2,208,384]{2,1,0:T(8,128)(2,1)} %get-tuple-element.33), channel_id=1, source_target_pairs={{0,1},{1,0},{2,3},{3,2},{4,5},{5,4},{6,7},{7,6},{8,9},{9,8},{10,11... | collective-permute-start | bytes 958472 | tf_op jit(solution)/shard_map/ppermute | solution.py:44
  25.5 3.6 %collective-permute-start.3 = (f32[160,192]{1,0:T(8,128)}, f32[160,192]{1,0:T(8,128)S(1)}, u32[]{:S(2)}, u32[]{:S(2)}) collective-permute-start(f32[160,192]{1,0:T(8,128)} %get-tuple-element.40), channel_id=1, source_target_pairs={{0,1},{1,0},{2,3},{3,2},{4,5},{5,4},{6,7},{7,6},{8,9},{9,8},{10,11... | collective-permute-start | bytes 368648 | tf_op jit(solution)/shard_map/ppermute | solution.py:44
  29.1 51.5 %copy-start.7 = (f32[160,192]{1,0:T(8,128)}, f32[160,192]{1,0:T(8,128)S(1)}, u32[]{:S(2)}) copy-start(f32[160,192]{1,0:T(8,128)S(1)} %collective-permute-done.3) | copy-start | bytes 368644
  87.1 7.1 %slice-start = ((s8[4718592]{0:T(1024)(128)(4,1)}), s8[4194304]{0:T(1024)(128)(4,1)S(1)}, s32[]{:S(2)}) async-start(s8[4718592]{0:T(1024)(128)(4,1)} %bitcast.132), calls=%async_computation | async-start | bytes 8388608
  87.1 7.1 %slice-start.1 = ((s8[4718592]{0:T(1024)(128)(4,1)}), s8[524288]{0:T(1024)(128)(4,1)S(1)}, s32[]{:S(2)}) async-start(s8[4718592]{0:T(1024)(128)(4,1)} %bitcast.132), calls=%async_computation.1 | async-start | bytes 1048576
  92.2 4.5 %collective-permute-start.4 = (f32[12,160,128]{2,1,0:T(8,128)S(1)}, f32[12,160,128]{2,1,0:T(8,128)S(1)}, u32[]{:S(2)}, u32[]{:S(2)}) collective-permute-start(f32[12,160,128]{2,1,0:T(8,128)S(1)} %convolution_bitcast_fusion.3), channel_id=1, source_target_pairs={{0,1},{1,0},{2,3},{3,2},{4,5},{5,4},{6,7},{7,6},{8,9},{9,8},{10,11... | collective-permute-start | bytes 2949128 | tf_op jit(solution)/shard_map/ppermute | solution.py:44
  99.4 15.8 %collective-permute-start.9 = (f32[24,160,128]{2,1,0:T(8,128)}, f32[24,160,128]{2,1,0:T(8,128)}, u32[]{:S(2)}, u32[]{:S(2)}) collective-permute-start(f32[24,160,128]{2,1,0:T(8,128)} %convolution_bitcast_fusion), channel_id=1, source_target_pairs={{0,1},{1,0},{2,3},{3,2},{4,5},{5,4},{6,7},{7,6},{8,9},{9,8},{10,11... | collective-permute-start | bytes 5898248 | tf_op jit(solution)/shard_map/ppermute | solution.py:44
  103.1 23.8 %collective-permute-start.5 = (f32[12,160,128]{2,1,0:T(8,128)}, f32[12,160,128]{2,1,0:T(8,128)}, u32[]{:S(2)}, u32[]{:S(2)}) collective-permute-start(f32[12,160,128]{2,1,0:T(8,128)} %convolution_bitcast_fusion.2), channel_id=1, source_target_pairs={{0,1},{1,0},{2,3},{3,2},{4,5},{5,4},{6,7},{7,6},{8,9},{9,8},{10,11... | collective-permute-start | bytes 2949128 | tf_op jit(solution)/shard_map/ppermute | solution.py:44
  105.4 21.5 %collective-permute-start.6 = (bf16[12,160,128]{2,1,0:T(8,128)(2,1)S(1)}, bf16[12,160,128]{2,1,0:T(8,128)(2,1)S(1)}, u32[]{:S(2)}, u32[]{:S(2)}) collective-permute-start(bf16[12,160,128]{2,1,0:T(8,128)(2,1)S(1)} %fusion.3), channel_id=1, source_target_pairs={{0,32},{32,0},{1,33},{33,1},{2,34},{34,2},{3,35},{35,3},{4,36},{36... | collective-permute-start | bytes 1474568 | tf_op jit(solution)/shard_map/ppermute | solution.py:125
  118.6 23.0 %collective-permute-start.11 = (bf16[4,2,160,128]{3,2,0,1:T(8,128)(2,1)S(1)}, bf16[4,2,160,128]{3,2,0,1:T(8,128)(2,1)S(1)}, u32[]{:S(2)}, u32[]{:S(2)}) collective-permute-start(bf16[4,2,160,128]{3,2,0,1:T(8,128)(2,1)S(1)} %bitcast.145), channel_id=1, source_target_pairs={{0,128},{64,0},{128,64},{192,320},{256,192},{320,256},{384,512},{4... | collective-permute-start | bytes 983048 | tf_op jit(solution)/shard_map/ppermute | solution.py:125
  120.5 21.1 %collective-permute-start.10 = (bf16[4,2,160,128]{3,2,0,1:T(8,128)(2,1)S(1)}, bf16[4,2,160,128]{3,2,0,1:T(8,128)(2,1)S(1)}, u32[]{:S(2)}, u32[]{:S(2)}) collective-permute-start(bf16[4,2,160,128]{3,2,0,1:T(8,128)(2,1)S(1)} %bitcast.144), channel_id=1, source_target_pairs={{0,64},{64,128},{128,0},{192,256},{256,320},{320,192},{384,448},{4... | collective-permute-start | bytes 983048 | tf_op jit(solution)/shard_map/ppermute | solution.py:125
  128.7 14.9 %collective-permute-start.7 = (bf16[4,160,128]{2,1,0:T(8,128)(2,1)S(1)}, bf16[4,160,128]{2,1,0:T(8,128)(2,1)S(1)}, u32[]{:S(2)}, u32[]{:S(2)}) collective-permute-start(bf16[4,160,128]{2,1,0:T(8,128)(2,1)S(1)} %get-tuple-element.27), channel_id=1, source_target_pairs={{0,64},{64,128},{128,0},{192,256},{256,320},{320,192},{384,448},{4... | collective-permute-start | bytes 491528 | tf_op jit(solution)/shard_map/ppermute | solution.py:125
  130.6 13.5 %collective-permute-start.8 = (bf16[4,160,128]{2,1,0:T(8,128)(2,1)S(1)}, bf16[4,160,128]{2,1,0:T(8,128)(2,1)S(1)}, u32[]{:S(2)}, u32[]{:S(2)}) collective-permute-start(bf16[4,160,128]{2,1,0:T(8,128)(2,1)S(1)} %get-tuple-element.28), channel_id=1, source_target_pairs={{0,128},{64,0},{128,64},{192,320},{256,192},{320,256},{384,512},{4... | collective-permute-start | bytes 491528 | tf_op jit(solution)/shard_map/ppermute | solution.py:125
  141.7 7.2 %collective-permute-start.12 = (bf16[4,160,128]{2,1,0:T(8,128)(2,1)S(1)}, bf16[4,160,128]{2,1,0:T(8,128)(2,1)S(1)}, u32[]{:S(2)}, u32[]{:S(2)}) collective-permute-start(bf16[4,160,128]{2,1,0:T(8,128)(2,1)S(1)} %fusion.21), channel_id=1, source_target_pairs={{0,32},{32,0},{1,33},{33,1},{2,34},{34,2},{3,35},{35,3},{4,36},{36... | collective-permute-start | bytes 491528 | tf_op jit(solution)/shard_map/ppermute | solution.py:125
  149.0 15.3 %collective-permute-start.13 = (bf16[160,256]{1,0:T(8,128)(2,1)S(1)}, bf16[160,256]{1,0:T(8,128)(2,1)S(1)}, u32[]{:S(2)}, u32[]{:S(2)}) collective-permute-start(bf16[160,256]{1,0:T(8,128)(2,1)S(1)} %get-tuple-element.29), channel_id=1, source_target_pairs={{0,192},{64,256},{128,320},{192,384},{256,448},{320,512},{384,576}... | collective-permute-start | bytes 245768 | tf_op jit(solution)/shard_map/ppermute | solution.py:125
  151.0 14.1 %collective-permute-start.14 = (bf16[160,256]{1,0:T(8,128)(2,1)S(1)}, bf16[160,256]{1,0:T(8,128)(2,1)S(1)}, u32[]{:S(2)}, u32[]{:S(2)}) collective-permute-start(bf16[160,256]{1,0:T(8,128)(2,1)S(1)} %get-tuple-element.30), channel_id=1, source_target_pairs={{0,384},{64,448},{128,512},{192,576},{256,640},{320,704},{384,0},{... | collective-permute-start | bytes 245768 | tf_op jit(solution)/shard_map/ppermute | solution.py:125
  160.1 11.1 %collective-permute-start.15 = (bf16[160,256]{1,0:T(8,128)(2,1)S(1)}, bf16[160,256]{1,0:T(8,128)(2,1)S(1)}, u32[]{:S(2)}, u32[]{:S(2)}) collective-permute-start(bf16[160,256]{1,0:T(8,128)(2,1)S(1)} %get-tuple-element.31), channel_id=1, source_target_pairs={{0,576},{64,640},{128,704},{192,0},{256,64},{320,128},{384,192},{4... | collective-permute-start | bytes 245768 | tf_op jit(solution)/shard_map/ppermute | solution.py:125
  (8 other events, 36.4 us)

commit v4 on v3

--- a/solution.py
+++ b/solution.py
@@ -52,7 +52,7 @@
 
 
 def in_order(mine, theirs, which):
-    return jnp.where(which == 0, jnp.stack([mine, theirs]), jnp.stack([theirs, mine]))
+    return jnp.stack([jnp.where(which == 0, mine, theirs), jnp.where(which == 0, theirs, mine)])
 
 
 def body(
@@ -66,18 +66,18 @@
     mask_rows = jnp.pad(pair_mask.astype(jnp.float16), ((0, tail - 1), (0, units - pairs)))
 
     def packed(which):
-        low = which * (units // 2)
-        part = [lax.slice_in_dim(w, low, low + units // 2, axis=1) for w in (gate_weight, up_weight)]
+        part = [half_of(gate_weight, which, 1), half_of(up_weight, which, 1)]
         part = (jnp.concatenate(part, axis=1).astype(jnp.float32) * SHIFT).astype(jnp.float16)
         return jnp.concatenate([part, mask_rows])
 
-    own = jnp.stack([packed(0), packed(1)])
-    pair = in_order(own, swap(own, "xh"), lax.axis_index("xh"))
-    kept = lax.dynamic_index_in_dim(pair, core, 1, keepdims=False)
-    given = lax.dynamic_index_in_dim(pair, 1 - core, 1, keepdims=False)
-    four = in_order(kept, swap(given, "core"), core).transpose(1, 0, 2, 3)
-    chip_mask = jnp.sum(four[:, :, rows:].astype(jnp.float32), axis=(0, 1)).astype(jnp.float16)
-    sent = jnp.concatenate([four[:, :, :rows].reshape(4 * rows, units), chip_mask])
+    pair = in_order(packed(core), swap(packed(1 - core), "core"), core)
+    chip_rows = pair[:, :rows].reshape(2 * rows, units)
+    chip_mask = jnp.sum(pair[:, rows:].astype(jnp.float32), axis=0).astype(jnp.float16)
+    late = 2 * rows // 3
+    crossed = swap(jnp.concatenate([chip_rows[late:], chip_mask]), "xh")
+    crossed_mask = crossed[2 * rows - late :].astype(jnp.float32) + chip_mask.astype(jnp.float32)
+    crossed = jnp.concatenate([crossed[: 2 * rows - late], crossed_mask.astype(jnp.float16)])
+
 
     taken = slot_matrix(routes, CAP)
     picks = taken.astype(jnp.bfloat16)
@@ -89,14 +89,19 @@
     their_rows = swap(slot_rows, "core")
     their_cotangent = swap(half_of(cotangent, 1 - core, 1), "core")
     cotangent = half_of(cotangent, core, 1)
-    sent, slot_rows, cotangent, their_rows, their_cotangent = lax.optimization_barrier(
-        (sent, slot_rows, cotangent, their_rows, their_cotangent)
+    chip_rows, slot_rows, cotangent, their_rows, their_cotangent = lax.optimization_barrier(
+        (chip_rows, slot_rows, cotangent, their_rows, their_cotangent)
     )
 
-    whole = lax.all_gather(sent, "y", axis=0, tiled=False)
-    total_pairs = jnp.sum(whole[:, 4 * rows, :pairs].astype(jnp.float32))
+    whole = lax.all_gather(chip_rows, "y", axis=0, tiled=False)
+    crossed, whole = lax.optimization_barrier((crossed, whole))
+    after = swap(whole[:, :late], "xh")
+    before = lax.all_gather(crossed, "y", axis=0, tiled=False)
+    total_pairs = jnp.sum(before[:, 2 * rows - late, :pairs].astype(jnp.float32))
     loss_scale = n_y * 4 * pairs / total_pairs
-    weight = whole[:, : 4 * rows].astype(jnp.bfloat16).reshape(n_y * 4 * rows, units)
+    other = jnp.concatenate([after, before[:, : 2 * rows - late]], axis=1)
+    weight = in_order(whole, other, lax.axis_index("xh")).astype(jnp.bfloat16)
+    weight = weight.transpose(1, 0, 2, 3).reshape(n_y * 4 * rows, units)
 
     def slot_gradients(left, weight, cotangent):
         value = jnp.dot(left, weight, preferred_element_type=jnp.float32) * (1.0 / SHIFT)

time: 173 us -> 183 us (1.058)
  the two profiles are of different devices: /device:TPU:2 before, /device:TPU:64 now
where the time goes in v4:
time: 183 us; the launch traced here: 182 us
  starting transfers between devices  63 us (34%)
  blocking collectives  60.5 us (33%)
  waiting for transfers between devices  22.5 us (12%)
  matrix products  18.9 us (10%)
  other arithmetic  11.8 us (6%)
  local copies, waits for them, and re-layouts  3.81 us (2%)
    ppermute x9, starting transfers between devices, send(): lax.ppermute(value.astype(jnp.bfloat16), axis, route).astype(jnp.float32)  40.6 us
    all_gather x1, blocking collectives, body(): whole = lax.all_gather(chip_rows, 'y', axis=0, tiled=False)  32.4 us
    all_gather x1, blocking collectives, body(): before = lax.all_gather(crossed, 'y', axis=0, tiled=False)  28.1 us
    ppermute x8, starting transfers between devices, swap(): return lax.ppermute(value, axis, [(0, 1), (1, 0)])  22.4 us
    ppermute x9, waiting for transfers between devices, send(): lax.ppermute(value.astype(jnp.bfloat16), axis, route).astype(jnp.float32)  18.7 us
    dot_general x6, matrix products, partial(): lax.dot_general(left, part.reshape(-1, units), (((1,), (1,)), ((), ())),...  9.7 us
    dot_general x2, matrix products, slot_gradients(): jnp.dot(left, weight, preferred_element_type=jnp.float32) * (1.0 / SHIFT)  4.91 us
    dot_general x1, matrix products, body(): jnp.dot(picks, tokens, preferred_element_type=jnp.float32)  4.03 us
  transfers between devices with their start and end apart: 17, of which 7 were waited for; matrix products, arithmetic and copies ran while one was open for 10% of the time, Pallas kernels for 0%

profile of v4, /device:TPU:64, one launch (start us, length us, event | category | flops | bytes accessed | tf_op | source)
XLA Modules:
  0.0 182.0 jit_solution(2360561506938958284)
XLA Ops:
  5.3 4.0 %convolution_convert_fusion = bf16[160,6144]{1,0:T(8,128)(2,1)S(1)} fusion(bf16[512,6144]{1,0:T(8,128)(2,1)} %param.9, s32[512]{0:T(512)S(1)} %add_bitcast_fusion, pred[512]{0:T(512)(128)(4,1)S(1)} %fusion.63), kind=kOutput, calls=%fused_computation | convolution fusion | flops 1007779840 | bytes 8260096 | tf_op jit(solution)/shard_map/dot_general | solution.py:84
  9.4 2.4 %collective-permute-start.1 = (bf16[160,6144]{1,0:T(8,128)(2,1)S(1)}, bf16[160,6144]{1,0:T(8,128)(2,1)}, u32[]{:S(2)}, u32[]{:S(2)}) collective-permute-start(bf16[160,6144]{1,0:T(8,128)(2,1)S(1)} %convolution_convert_fusion), channel_id=1, source_target_pairs={{0,1},{1,0},{2,3},{3,2},{4,5},{5,4},{6,7},{7,6},{8,9},{9,8},{10,11... | collective-permute-start | bytes 5898248 | tf_op jit(solution)/shard_map/ppermute | solution.py:44
  13.2 4.9 %collective-permute-start.3 = (f16[272,384]{1,0:T(8,128)(2,1)S(1)}, f16[272,384]{1,0:T(8,128)(2,1)S(1)}, u32[]{:S(2)}, u32[]{:S(2)}) collective-permute-start(f16[272,384]{1,0:T(8,128)(2,1)S(1)} %pad_maximum_fusion.1), channel_id=1, source_target_pairs={{0,2},{2,0},{1,3},{3,1},{4,6},{6,4},{5,7},{7,5},{8,10},{10,8},{9,1... | collective-permute-start | bytes 626696 | tf_op jit(solution)/shard_map/ppermute | solution.py:44
  20.9 2.8 %collective-permute-done.3 = f16[272,384]{1,0:T(8,128)(2,1)S(1)} collective-permute-done((f16[272,384]{1,0:T(8,128)(2,1)S(1)}, f16[272,384]{1,0:T(8,128)(2,1)S(1)}, u32[]{:S(2)}, u32[]{:S(2)}) %collective-permute-start.3) | collective-permute-done | bytes 208928 | tf_op jit(solution)/shard_map/ppermute | solution.py:44
  23.9 32.4 %all-gather.4 = f16[3072,384]{1,0:T(8,128)(2,1)S(1)} all-gather(f16[384,384]{1,0:T(8,128)(2,1)S(1)} %bitcast.144), channel_id=2, replica_groups=mesh['z'=12,'xl'=2,'y'=8,'xh'=2,'core'=2] {'y'}, dimensions={0}, use_global_device_ids=true | all-gather | bytes 2654208 | tf_op jit(solution)/shard_map/all_gather | solution.py:96
  57.3 4.9 %collective-permute-start.4 = (f16[8,128,384]{2,1,0:T(8,128)(2,1)}, f16[8,128,384]{2,1,0:T(8,128)(2,1)S(1)}, u32[]{:S(2)}, u32[]{:S(2)}) collective-permute-start(f16[8,128,384]{2,1,0:T(8,128)(2,1)} %slice.88), channel_id=1, source_target_pairs={{0,2},{2,0},{1,3},{3,1},{4,6},{6,4},{5,7},{7,5},{8,10},{10,8},{9,1... | collective-permute-start | bytes 2359304 | tf_op jit(solution)/shard_map/ppermute | solution.py:44
  62.2 28.1 %all-gather.5 = f16[2176,384]{1,0:T(8,128)(2,1)S(1)} all-gather(f16[272,384]{1,0:T(8,128)(2,1)S(1)} %pad_maximum_fusion.2), channel_id=3, replica_groups=mesh['z'=12,'xl'=2,'y'=8,'xh'=2,'core'=2] {'y'}, dimensions={0}, use_global_device_ids=true | all-gather | bytes 1880064 | tf_op jit(solution)/shard_map/all_gather | solution.py:99
  93.1 2.8 %select_bitcast_fusion.1 = (f16[1,8,384,384]{3,2,0,1:T(8,128)(2,1)S(1)}, f16[1,8,384,384]{3,2,0,1:T(8,128)(2,1)S(1)}) fusion(f16[8,384,384]{2,1,0:T(8,128)(2,1)S(1)} %bitcast.136, pred[]{:T(512)S(6)} %eq.64, f16[8,256,384]{2,1,0:T(8,128)(2,1)} %slice.104, f16[8,128,384]{2,1,0:T(8,128)(2,1)S(1)} %collective-permute-done.4), kind=kLoop, calls=%fused_computation.4 | loop fusion | flops 3538944 | bytes 9437185 | tf_op jit(solution)/shard_map/stack | solution.py:55
  97.6 3.7 %convolution_multiply_fusion = f32[160,384]{1,0:T(8,128)S(1)} fusion(bf16[160,6144]{1,0:T(8,128)(2,1)} %collective-permute-done.1, bf16[6144,384]{1,0:T(8,128)(2,1)S(1)} %bitcast.131), kind=kOutput, calls=%fused_computation.19 | convolution fusion | flops 755036160 | bytes 6930432 | tf_op jit(solution)/shard_map/dot_general | solution.py:107
  108.3 2.2 %convolution_bitcast_fusion = f32[24,160,128]{2,1,0:T(8,128)} fusion(bf16[24,128,384]{2,1,0:T(8,128)(2,1)S(1)} %bitcast.133, bf16[160,384]{1,0:T(8,128)(2,1)S(1)} %pad_maximum_fusion.4), kind=kOutput, calls=%fused_computation.6 | convolution fusion | flops 377487360 | bytes 4448256 | tf_op jit(solution)/shard_map/dot_general | solution.py:118
  114.0 2.3 %collective-permute-start.6 = (f32[12,160,128]{2,1,0:T(8,128)}, f32[12,160,128]{2,1,0:T(8,128)}, u32[]{:S(2)}, u32[]{:S(2)}) collective-permute-start(f32[12,160,128]{2,1,0:T(8,128)} %convolution_bitcast_fusion.2), channel_id=1, source_target_pairs={{0,1},{1,0},{2,3},{3,2},{4,5},{5,4},{6,7},{7,6},{8,9},{9,8},{10,11... | collective-permute-start | bytes 2949128 | tf_op jit(solution)/shard_map/ppermute | solution.py:44
  116.4 2.5 %collective-permute-start.7 = (bf16[12,160,128]{2,1,0:T(8,128)(2,1)S(1)}, bf16[12,160,128]{2,1,0:T(8,128)(2,1)S(1)}, u32[]{:S(2)}, u32[]{:S(2)}) collective-permute-start(bf16[12,160,128]{2,1,0:T(8,128)(2,1)S(1)} %fusion.3), channel_id=1, source_target_pairs={{0,32},{32,0},{1,33},{33,1},{2,34},{34,2},{3,35},{35,3},{4,36},{36... | collective-permute-start | bytes 1474568 | tf_op jit(solution)/shard_map/ppermute | solution.py:130
  119.0 3.2 %bitcast_add_fusion = f32[24,160,128]{2,1,0:T(8,128)S(1)} fusion(f32[24,160,128]{2,1,0:T(8,128)} %collective-permute-done.10, bf16[24,128,384]{2,1,0:T(8,128)(2,1)} %bitcast.134, bf16[160,384]{1,0:T(8,128)(2,1)S(1)} %pad_maximum_fusion.3), kind=kOutput, calls=%fused_computation.5 | convolution fusion | flops 377978880 | bytes 6414336 | tf_op jit(solution)/shard_map/dot_general | solution.py:118
  122.3 5.4 %collective-permute-start.12 = (bf16[4,2,160,128]{3,2,0,1:T(8,128)(2,1)S(1)}, bf16[4,2,160,128]{3,2,0,1:T(8,128)(2,1)S(1)}, u32[]{:S(2)}, u32[]{:S(2)}) collective-permute-start(bf16[4,2,160,128]{3,2,0,1:T(8,128)(2,1)S(1)} %bitcast.146), channel_id=1, source_target_pairs={{0,128},{64,0},{128,64},{192,320},{256,192},{320,256},{384,512},{4... | collective-permute-start | bytes 983048 | tf_op jit(solution)/shard_map/ppermute | solution.py:130
  133.4 4.3 %collective-permute-start.8 = (bf16[4,160,128]{2,1,0:T(8,128)(2,1)S(1)}, bf16[4,160,128]{2,1,0:T(8,128)(2,1)S(1)}, u32[]{:S(2)}, u32[]{:S(2)}) collective-permute-start(bf16[4,160,128]{2,1,0:T(8,128)(2,1)S(1)} %get-tuple-element.33), channel_id=1, source_target_pairs={{0,64},{64,128},{128,0},{192,256},{256,320},{320,192},{384,448},{4... | collective-permute-start | bytes 491528 | tf_op jit(solution)/shard_map/ppermute | solution.py:130
  137.8 3.6 %collective-permute-start.9 = (bf16[4,160,128]{2,1,0:T(8,128)(2,1)S(1)}, bf16[4,160,128]{2,1,0:T(8,128)(2,1)S(1)}, u32[]{:S(2)}, u32[]{:S(2)}) collective-permute-start(bf16[4,160,128]{2,1,0:T(8,128)(2,1)S(1)} %get-tuple-element.34), channel_id=1, source_target_pairs={{0,128},{64,0},{128,64},{192,320},{256,192},{320,256},{384,512},{4... | collective-permute-start | bytes 491528 | tf_op jit(solution)/shard_map/ppermute | solution.py:130
  141.3 5.0 %collective-permute-done.12 = bf16[4,2,160,128]{3,2,0,1:T(8,128)(2,1)S(1)} collective-permute-done((bf16[4,2,160,128]{3,2,0,1:T(8,128)(2,1)S(1)}, bf16[4,2,160,128]{3,2,0,1:T(8,128)(2,1)S(1)}, u32[]{:S(2)}, u32[]{:S(2)}) %collective-permute-start.12) | collective-permute-done | bytes 327712 | tf_op jit(solution)/shard_map/ppermute | solution.py:130
  146.4 4.0 %collective-permute-start.13 = (bf16[4,160,128]{2,1,0:T(8,128)(2,1)S(1)}, bf16[4,160,128]{2,1,0:T(8,128)(2,1)S(1)}, u32[]{:S(2)}, u32[]{:S(2)}) collective-permute-start(bf16[4,160,128]{2,1,0:T(8,128)(2,1)S(1)} %fusion.21), channel_id=1, source_target_pairs={{0,32},{32,0},{1,33},{33,1},{2,34},{34,2},{3,35},{35,3},{4,36},{36... | collective-permute-start | bytes 491528 | tf_op jit(solution)/shard_map/ppermute | solution.py:130
  150.5 3.2 %collective-permute-done.13 = bf16[4,160,128]{2,1,0:T(8,128)(2,1)S(1)} collective-permute-done((bf16[4,160,128]{2,1,0:T(8,128)(2,1)S(1)}, bf16[4,160,128]{2,1,0:T(8,128)(2,1)S(1)}, u32[]{:S(2)}, u32[]{:S(2)}) %collective-permute-start.13) | collective-permute-done | bytes 163872 | tf_op jit(solution)/shard_map/ppermute | solution.py:130
  153.8 7.7 %collective-permute-start.14 = (bf16[160,256]{1,0:T(8,128)(2,1)S(1)}, bf16[160,256]{1,0:T(8,128)(2,1)S(1)}, u32[]{:S(2)}, u32[]{:S(2)}) collective-permute-start(bf16[160,256]{1,0:T(8,128)(2,1)S(1)} %get-tuple-element.35), channel_id=1, source_target_pairs={{0,192},{64,256},{128,320},{192,384},{256,448},{320,512},{384,576}... | collective-permute-start | bytes 245768 | tf_op jit(solution)/shard_map/ppermute | solution.py:130
  161.5 8.2 %collective-permute-start.15 = (bf16[160,256]{1,0:T(8,128)(2,1)S(1)}, bf16[160,256]{1,0:T(8,128)(2,1)S(1)}, u32[]{:S(2)}, u32[]{:S(2)}) collective-permute-start(bf16[160,256]{1,0:T(8,128)(2,1)S(1)} %get-tuple-element.36), channel_id=1, source_target_pairs={{0,384},{64,448},{128,512},{192,576},{256,640},{320,704},{384,0},{... | collective-permute-start | bytes 245768 | tf_op jit(solution)/shard_map/ppermute | solution.py:130
  169.8 2.9 %collective-permute-start.16 = (bf16[160,256]{1,0:T(8,128)(2,1)S(1)}, bf16[160,256]{1,0:T(8,128)(2,1)S(1)}, u32[]{:S(2)}, u32[]{:S(2)}) collective-permute-start(bf16[160,256]{1,0:T(8,128)(2,1)S(1)} %get-tuple-element.37), channel_id=1, source_target_pairs={{0,576},{64,640},{128,704},{192,0},{256,64},{320,128},{384,192},{4... | collective-permute-start | bytes 245768 | tf_op jit(solution)/shard_map/ppermute | solution.py:130
  172.7 2.8 %collective-permute-done.15 = bf16[160,256]{1,0:T(8,128)(2,1)S(1)} collective-permute-done((bf16[160,256]{1,0:T(8,128)(2,1)S(1)}, bf16[160,256]{1,0:T(8,128)(2,1)S(1)}, u32[]{:S(2)}, u32[]{:S(2)}) %collective-permute-start.15) | collective-permute-done | bytes 81952 | tf_op jit(solution)/shard_map/ppermute | solution.py:130
  175.6 5.7 %collective-permute-done.16 = bf16[160,256]{1,0:T(8,128)(2,1)S(1)} collective-permute-done((bf16[160,256]{1,0:T(8,128)(2,1)S(1)}, bf16[160,256]{1,0:T(8,128)(2,1)S(1)}, u32[]{:S(2)}, u32[]{:S(2)}) %collective-permute-start.16) | collective-permute-done | bytes 81952 | tf_op jit(solution)/shard_map/ppermute | solution.py:130
  (94 shorter events, 31.6 us)
Async XLA Ops:
  0.0 12.5 %copy-start = (bf16[512,384]{1,0:T(8,128)(2,1)S(1)}, bf16[512,384]{1,0:T(8,128)(2,1)}, u32[]{:S(2)}) copy-start(bf16[512,384]{1,0:T(8,128)(2,1)} %param.15) | copy-start | bytes 1179652
  2.0 10.9 %collective-permute-start = (f16[208,384]{1,0:T(8,128)(2,1)S(1)}, f16[208,384]{1,0:T(8,128)(2,1)S(1)}, u32[]{:S(2)}, u32[]{:S(2)}) collective-permute-start(f16[208,384]{1,0:T(8,128)(2,1)S(1)} %fusion.47), channel_id=1, source_target_pairs={{0,1},{1,0},{2,3},{3,2},{4,5},{5,4},{6,7},{7,6},{8,9},{9,8},{10,11... | collective-permute-start | bytes 479240 | tf_op jit(solution)/shard_map/ppermute | solution.py:44
  5.3 6.7 %copy-start.7 = (s32[1,4]{1,0:T(1,128)S(1)}, s32[1,4]{1,0:T(1,128)}, u32[]{:S(2)}) copy-start(s32[1,4]{1,0:T(1,128)} %param.13) | copy-start | bytes 52
  5.3 6.7 %copy-start.8 = (f32[1,4]{1,0:T(1,128)S(1)}, f32[1,4]{1,0:T(1,128)}, u32[]{:S(2)}) copy-start(f32[1,4]{1,0:T(1,128)} %param.14) | copy-start | bytes 52
  5.3 6.9 %copy-start.5 = (s32[512,2]{0,1:T(2,128)S(1)}, s32[512,2]{0,1:T(2,128)}, u32[]{:S(2)}) copy-start(s32[512,2]{0,1:T(2,128)} %param.10) | copy-start | bytes 12292
  5.3 6.9 %copy-start.6 = (f32[512,2]{0,1:T(2,128)S(1)}, f32[512,2]{0,1:T(2,128)}, u32[]{:S(2)}) copy-start(f32[512,2]{0,1:T(2,128)} %param.11) | copy-start | bytes 12292
  9.3 14.5 %copy-start.2 = (bf16[160,6144]{1,0:T(8,128)(2,1)}, bf16[160,6144]{1,0:T(8,128)(2,1)S(1)}, u32[]{:S(2)}) copy-start(bf16[160,6144]{1,0:T(8,128)(2,1)S(1)} %convolution_convert_fusion) | copy-start | bytes 5898244
  9.4 14.5 %collective-permute-start.1 = (bf16[160,6144]{1,0:T(8,128)(2,1)S(1)}, bf16[160,6144]{1,0:T(8,128)(2,1)}, u32[]{:S(2)}, u32[]{:S(2)}) collective-permute-start(bf16[160,6144]{1,0:T(8,128)(2,1)S(1)} %convolution_convert_fusion), channel_id=1, source_target_pairs={{0,1},{1,0},{2,3},{3,2},{4,5},{5,4},{6,7},{7,6},{8,9},{9,8},{10,11... | collective-permute-start | bytes 5898248 | tf_op jit(solution)/shard_map/ppermute | solution.py:44
  13.2 10.5 %collective-permute-start.3 = (f16[272,384]{1,0:T(8,128)(2,1)S(1)}, f16[272,384]{1,0:T(8,128)(2,1)S(1)}, u32[]{:S(2)}, u32[]{:S(2)}) collective-permute-start(f16[272,384]{1,0:T(8,128)(2,1)S(1)} %pad_maximum_fusion.1), channel_id=1, source_target_pairs={{0,2},{2,0},{1,3},{3,1},{4,6},{6,4},{5,7},{7,5},{8,10},{10,8},{9,1... | collective-permute-start | bytes 626696 | tf_op jit(solution)/shard_map/ppermute | solution.py:44
  19.0 4.8 %collective-permute-start.2 = (f32[160,192]{1,0:T(8,128)}, f32[160,192]{1,0:T(8,128)}, u32[]{:S(2)}, u32[]{:S(2)}) collective-permute-start(f32[160,192]{1,0:T(8,128)} %get-tuple-element.44), channel_id=1, source_target_pairs={{0,1},{1,0},{2,3},{3,2},{4,5},{5,4},{6,7},{7,6},{8,9},{9,8},{10,11... | collective-permute-start | bytes 368648 | tf_op jit(solution)/shard_map/ppermute | solution.py:44
  57.3 35.8 %collective-permute-start.4 = (f16[8,128,384]{2,1,0:T(8,128)(2,1)}, f16[8,128,384]{2,1,0:T(8,128)(2,1)S(1)}, u32[]{:S(2)}, u32[]{:S(2)}) collective-permute-start(f16[8,128,384]{2,1,0:T(8,128)(2,1)} %slice.88), channel_id=1, source_target_pairs={{0,2},{2,0},{1,3},{3,1},{4,6},{6,4},{5,7},{7,5},{8,10},{10,8},{9,1... | collective-permute-start | bytes 2359304 | tf_op jit(solution)/shard_map/ppermute | solution.py:44
  97.6 10.7 %copy-start.1 = (bf16[12,2,1,128,384]{4,3,2,1,0:T(8,128)(2,1)}, bf16[12,2,1,128,384]{4,3,2,1,0:T(8,128)(2,1)S(1)}, u32[]{:S(2)}) copy-start(bf16[12,2,1,128,384]{4,3,2,1,0:T(8,128)(2,1)S(1)} %get-tuple-element.27) | copy-start | bytes 7077892
  103.1 4.6 %collective-permute-start.5 = (f32[12,160,128]{2,1,0:T(8,128)S(1)}, f32[12,160,128]{2,1,0:T(8,128)S(1)}, u32[]{:S(2)}, u32[]{:S(2)}) collective-permute-start(f32[12,160,128]{2,1,0:T(8,128)S(1)} %convolution_bitcast_fusion.3), channel_id=1, source_target_pairs={{0,1},{1,0},{2,3},{3,2},{4,5},{5,4},{6,7},{7,6},{8,9},{9,8},{10,11... | collective-permute-start | bytes 2949128 | tf_op jit(solution)/shard_map/ppermute | solution.py:44
  110.5 8.5 %collective-permute-start.10 = (f32[24,160,128]{2,1,0:T(8,128)}, f32[24,160,128]{2,1,0:T(8,128)}, u32[]{:S(2)}, u32[]{:S(2)}) collective-permute-start(f32[24,160,128]{2,1,0:T(8,128)} %convolution_bitcast_fusion), channel_id=1, source_target_pairs={{0,1},{1,0},{2,3},{3,2},{4,5},{5,4},{6,7},{7,6},{8,9},{9,8},{10,11... | collective-permute-start | bytes 5898248 | tf_op jit(solution)/shard_map/ppermute | solution.py:44
  114.0 17.6 %collective-permute-start.6 = (f32[12,160,128]{2,1,0:T(8,128)}, f32[12,160,128]{2,1,0:T(8,128)}, u32[]{:S(2)}, u32[]{:S(2)}) collective-permute-start(f32[12,160,128]{2,1,0:T(8,128)} %convolution_bitcast_fusion.2), channel_id=1, source_target_pairs={{0,1},{1,0},{2,3},{3,2},{4,5},{5,4},{6,7},{7,6},{8,9},{9,8},{10,11... | collective-permute-start | bytes 2949128 | tf_op jit(solution)/shard_map/ppermute | solution.py:44
  116.4 15.2 %collective-permute-start.7 = (bf16[12,160,128]{2,1,0:T(8,128)(2,1)S(1)}, bf16[12,160,128]{2,1,0:T(8,128)(2,1)S(1)}, u32[]{:S(2)}, u32[]{:S(2)}) collective-permute-start(bf16[12,160,128]{2,1,0:T(8,128)(2,1)S(1)} %fusion.3), channel_id=1, source_target_pairs={{0,32},{32,0},{1,33},{33,1},{2,34},{34,2},{3,35},{35,3},{4,36},{36... | collective-permute-start | bytes 1474568 | tf_op jit(solution)/shard_map/ppermute | solution.py:130
  122.3 24.0 %collective-permute-start.12 = (bf16[4,2,160,128]{3,2,0,1:T(8,128)(2,1)S(1)}, bf16[4,2,160,128]{3,2,0,1:T(8,128)(2,1)S(1)}, u32[]{:S(2)}, u32[]{:S(2)}) collective-permute-start(bf16[4,2,160,128]{3,2,0,1:T(8,128)(2,1)S(1)} %bitcast.146), channel_id=1, source_target_pairs={{0,128},{64,0},{128,64},{192,320},{256,192},{320,256},{384,512},{4... | collective-permute-start | bytes 983048 | tf_op jit(solution)/shard_map/ppermute | solution.py:130
  127.7 18.6 %collective-permute-start.11 = (bf16[4,2,160,128]{3,2,0,1:T(8,128)(2,1)S(1)}, bf16[4,2,160,128]{3,2,0,1:T(8,128)(2,1)S(1)}, u32[]{:S(2)}, u32[]{:S(2)}) collective-permute-start(bf16[4,2,160,128]{3,2,0,1:T(8,128)(2,1)S(1)} %bitcast.145), channel_id=1, source_target_pairs={{0,64},{64,128},{128,0},{192,256},{256,320},{320,192},{384,448},{4... | collective-permute-start | bytes 983048 | tf_op jit(solution)/shard_map/ppermute | solution.py:130
  133.4 17.0 %collective-permute-start.8 = (bf16[4,160,128]{2,1,0:T(8,128)(2,1)S(1)}, bf16[4,160,128]{2,1,0:T(8,128)(2,1)S(1)}, u32[]{:S(2)}, u32[]{:S(2)}) collective-permute-start(bf16[4,160,128]{2,1,0:T(8,128)(2,1)S(1)} %get-tuple-element.33), channel_id=1, source_target_pairs={{0,64},{64,128},{128,0},{192,256},{256,320},{320,192},{384,448},{4... | collective-permute-start | bytes 491528 | tf_op jit(solution)/shard_map/ppermute | solution.py:130
  137.8 12.7 %collective-permute-start.9 = (bf16[4,160,128]{2,1,0:T(8,128)(2,1)S(1)}, bf16[4,160,128]{2,1,0:T(8,128)(2,1)S(1)}, u32[]{:S(2)}, u32[]{:S(2)}) collective-permute-start(bf16[4,160,128]{2,1,0:T(8,128)(2,1)S(1)} %get-tuple-element.34), channel_id=1, source_target_pairs={{0,128},{64,0},{128,64},{192,320},{256,192},{320,256},{384,512},{4... | collective-permute-start | bytes 491528 | tf_op jit(solution)/shard_map/ppermute | solution.py:130
  146.4 7.3 %collective-permute-start.13 = (bf16[4,160,128]{2,1,0:T(8,128)(2,1)S(1)}, bf16[4,160,128]{2,1,0:T(8,128)(2,1)S(1)}, u32[]{:S(2)}, u32[]{:S(2)}) collective-permute-start(bf16[4,160,128]{2,1,0:T(8,128)(2,1)S(1)} %fusion.21), channel_id=1, source_target_pairs={{0,32},{32,0},{1,33},{33,1},{2,34},{34,2},{3,35},{35,3},{4,36},{36... | collective-permute-start | bytes 491528 | tf_op jit(solution)/shard_map/ppermute | solution.py:130
  153.8 18.9 %collective-permute-start.14 = (bf16[160,256]{1,0:T(8,128)(2,1)S(1)}, bf16[160,256]{1,0:T(8,128)(2,1)S(1)}, u32[]{:S(2)}, u32[]{:S(2)}) collective-permute-start(bf16[160,256]{1,0:T(8,128)(2,1)S(1)} %get-tuple-element.35), channel_id=1, source_target_pairs={{0,192},{64,256},{128,320},{192,384},{256,448},{320,512},{384,576}... | collective-permute-start | bytes 245768 | tf_op jit(solution)/shard_map/ppermute | solution.py:130
  161.5 14.0 %collective-permute-start.15 = (bf16[160,256]{1,0:T(8,128)(2,1)S(1)}, bf16[160,256]{1,0:T(8,128)(2,1)S(1)}, u32[]{:S(2)}, u32[]{:S(2)}) collective-permute-start(bf16[160,256]{1,0:T(8,128)(2,1)S(1)} %get-tuple-element.36), channel_id=1, source_target_pairs={{0,384},{64,448},{128,512},{192,576},{256,640},{320,704},{384,0},{... | collective-permute-start | bytes 245768 | tf_op jit(solution)/shard_map/ppermute | solution.py:130
  169.8 11.5 %collective-permute-start.16 = (bf16[160,256]{1,0:T(8,128)(2,1)S(1)}, bf16[160,256]{1,0:T(8,128)(2,1)S(1)}, u32[]{:S(2)}, u32[]{:S(2)}) collective-permute-start(bf16[160,256]{1,0:T(8,128)(2,1)S(1)} %get-tuple-element.37), channel_id=1, source_target_pairs={{0,576},{64,640},{128,704},{192,0},{256,64},{320,128},{384,192},{4... | collective-permute-start | bytes 245768 | tf_op jit(solution)/shard_map/ppermute | solution.py:130
  (3 other events, 13.7 us)

commit v5 on v3

--- a/solution.py
+++ b/solution.py
@@ -1,6 +1,8 @@
 import jax
 import jax.numpy as jnp
 from jax import lax
+from jax.experimental import pallas as pl
+from jax.experimental.pallas import tpu as pltpu
 from jax.sharding import Mesh, PartitionSpec as P
 
 CAP = 160
@@ -44,6 +46,77 @@
     return lax.ppermute(value, axis, [(0, 1), (1, 0)])
 
 
+FREE = pl.CostEstimate(flops=0, bytes_accessed=0, transcendentals=0)
+LIMIT = pltpu.CompilerParams(vmem_limit_bytes=32 * 2**20)
+
+
+def rows_kernel(picks_ref, tokens_ref, out_ref):
+    out = jnp.dot(picks_ref[...], tokens_ref[...], preferred_element_type=jnp.float32)
+    out_ref[...] = out.astype(out_ref.dtype)
+
+
+def pick_rows(picks, tokens):
+    slots, depth = picks.shape
+    columns = tokens.shape[1]
+    block = columns // 6
+    return pl.pallas_call(
+        rows_kernel,
+        grid=(6,),
+        in_specs=[
+            pl.BlockSpec((slots, depth), lambda i: (0, 0)),
+            pl.BlockSpec((depth, block), lambda i: (0, i)),
+        ],
+        out_specs=pl.BlockSpec((slots, block), lambda i: (0, i)),
+        out_shape=jax.ShapeDtypeStruct((slots, columns), tokens.dtype),
+        cost_estimate=FREE,
+        compiler_params=LIMIT,
+    )(picks, tokens)
+
+
+def partial_kernel(side_ref, left_ref, weight_ref, *refs):
+    out_ref = refs[-1]
+    left = left_ref[...]
+    for i in range(out_ref.shape[0]):
+        for j in range(out_ref.shape[1]):
+            out = lax.dot_general(
+                left,
+                weight_ref[i, j, 0],
+                (((1,), (1,)), ((), ())),
+                preferred_element_type=jnp.float32,
+            )
+            for ref in refs[:-1]:
+                out += ref[i, j]
+            out_ref[i, j] = out.astype(out_ref.dtype)
+
+
+def partial(left, columns, side, half, addends=(), dtype=jnp.float32):
+    n_z, n_side, _, width, units = columns.shape
+    sides = n_side if side is None else 1
+    steps = 4
+    block = n_z // steps
+    slots = left.shape[0]
+    chosen = jnp.zeros((1,), jnp.int32) if side is None else side.reshape(1).astype(jnp.int32)
+    tile = pl.BlockSpec((block, sides, slots, width), lambda i, s: (i, 0, 0, 0))
+    return pl.pallas_call(
+        partial_kernel,
+        grid_spec=pltpu.PrefetchScalarGridSpec(
+            num_scalar_prefetch=1,
+            grid=(steps,),
+            in_specs=[
+                pl.BlockSpec((slots, units), lambda i, s: (0, 0)),
+                pl.BlockSpec(
+                    (block, sides, 1, width, units), lambda i, s: (i, s[0], half, 0, 0)
+                ),
+            ]
+            + [tile] * len(addends),
+            out_specs=tile,
+        ),
+        out_shape=jax.ShapeDtypeStruct((n_z, sides, slots, width), dtype),
+        cost_estimate=FREE,
+        compiler_params=LIMIT,
+    )(chosen, left, columns, *addends)
+
+
 def half_of(value, which, axis):
     size = value.shape[axis] // 2
     low = lax.slice_in_dim(value, 0, size, axis=axis)
@@ -81,17 +154,15 @@
 
     taken = slot_matrix(routes, CAP)
     picks = taken.astype(jnp.bfloat16)
-    slot_rows = jnp.dot(picks, tokens, preferred_element_type=jnp.float32).astype(jnp.bfloat16)
+    slot_rows = pick_rows(picks, tokens)
     grad_rows = jnp.dot(picks, hidden_grad, preferred_element_type=jnp.float32)
     coef_tok = token_scale(routes, router_prob, lengths[0], pair_mask[0], margins[0])
     coefficient = jnp.sum(jnp.where(taken, coef_tok[None, :], jnp.float32(0.0)), axis=1)
     cotangent = coefficient[:, None] * grad_rows
+    sent = lax.optimization_barrier((sent, slot_rows, cotangent))[0]
     their_rows = swap(slot_rows, "core")
     their_cotangent = swap(half_of(cotangent, 1 - core, 1), "core")
     cotangent = half_of(cotangent, core, 1)
-    sent, slot_rows, cotangent, their_rows, their_cotangent = lax.optimization_barrier(
-        (sent, slot_rows, cotangent, their_rows, their_cotangent)
-    )
 
     whole = lax.all_gather(sent, "y", axis=0, tiled=False)
     total_pairs = jnp.sum(whole[:, 4 * rows, :pairs].astype(jnp.float32))
@@ -108,15 +179,6 @@
     width = weight.shape[0] // (4 * n_z)
     columns = weight.reshape(n_z, 2, 2, width, units)
     place, group, groups = z % 3, z // 3, n_z // 3
-
-    def partial(left, part):
-        out = lax.dot_general(
-            left,
-            part.reshape(-1, units),
-            (((1,), (1,)), ((), ())),
-            preferred_element_type=jnp.float32,
-        )
-        return out.reshape(CAP, -1, width).transpose(1, 0, 2)
 
     def pick(value, index, axis):
         return lax.dynamic_index_in_dim(value, index, axis, keepdims=False)
@@ -133,22 +195,19 @@
         return pick(value, place, 1) + moved[0] + moved[1]
 
     across = [(0, 1), (1, 0)]
-    part = pick(columns[:, :, 0], 1 - mine, 1)
-    theirs = swap(partial(their_grads, part), "core")
+    theirs = swap(partial(their_grads, columns, 1 - mine, 0), "core")
     own_grads = slot_gradients(slot_rows, weight, cotangent)
-    leaving = (partial(own_grads, part) + theirs).astype(jnp.bfloat16)
-    leaving, own_grads, their_grads = lax.optimization_barrier((leaving, own_grads, their_grads))
+    leaving = partial(own_grads, columns, 1 - mine, 0, (theirs,), jnp.bfloat16)
     arrived = send(leaving, "xl", across)
-    part = columns[:, :, 1]
-    second = swap(partial(their_grads, part), "core") + partial(own_grads, part)
-    second = three(second.reshape(n_z, 2, CAP, width))
-    part = pick(columns[:, :, 0], mine, 1)
-    first = swap(partial(their_grads, part), "core") + partial(own_grads, part) + arrived
+    theirs = swap(partial(their_grads, columns, None, 1), "core")
+    second = three(partial(own_grads, columns, None, 1, (theirs,)))
+    theirs = swap(partial(their_grads, columns, mine, 0), "core")
+    first = partial(own_grads, columns, mine, 0, (theirs,)) + arrived
     second = pick(second, mine, 1) + send(pick(second, 1 - mine, 1), "xl", across)
-    first = three(first)
+    first = three(first)[:, 0]
     total = jnp.concatenate([first, second], axis=2)
     result = pick(total, group, 0)
-    for step in range(1, groups):
+    for step in (groups // 2, *(i for i in range(1, groups) if i != groups // 2)):
         route = [(i, (i + 3 * step) % n_z) for i in range(n_z)]
         result += send(pick(total, (group + step) % groups, 0), "z", route)
     return result * (1.0 / SHIFT)

time: 173 us -> 174 us (level)
  matrix products: 19.4 us -> 4.32 us
  Pallas kernels: 0 us -> 14.7 us
  waiting for transfers between devices: 30.9 us -> 17.4 us
  local copies, waits for them, and re-layouts: 5.96 us -> 13.6 us
  starting transfers between devices: 56.3 us -> 60.2 us
  other arithmetic: 6.4 us -> 9.69 us
    pallas_call x0 -> x7, Pallas kernels: none -> 14.7 us  [the longest x6 12.1 us: partial(): pl.pallas_call(partial_kernel, grid_spec=pltpu.PrefetchScalarGridSpec(num...]
    dot_general x7 -> x0, matrix products: 13.7 us -> none  [the longest x6 9.66 us: partial(): lax.dot_general(left, part.reshape(-1, units), (((1,), (1,)), ((), ())),...]
    ppermute x7, waiting for transfers between devices: 10.2 us -> 0.82 us  [swap(): return lax.ppermute(value, axis, [(0, 1), (1, 0)])]
    unnamed x34 -> x30, local copies, waits for them, and re-layouts: 2.24 us -> 10.7 us
    ppermute x9, waiting for transfers between devices: 20.7 us -> 16.6 us  [send(): lax.ppermute(value.astype(jnp.bfloat16), axis, route).astype(jnp.float32)]
    ppermute x9, starting transfers between devices: 39.6 us -> 43.1 us  [send(): lax.ppermute(value.astype(jnp.bfloat16), axis, route).astype(jnp.float32)]
    convert_element_type x1, other arithmetic: 0.96 us -> 3.14 us  [body(): whole[:, :4 * rows].astype(jnp.bfloat16).reshape(n_y * 4 * rows, units)]
    slice x2 -> x1, local copies, waits for them, and re-layouts: 2.08 us -> 0.07 us  [the longest x1 2.01 us: body(): part = columns[:, :, 1]]
  transfers between devices with their start and end apart: 16 -> 16, of which waited for: 9 -> 5; matrix products, arithmetic and copies ran while one was open for 7% -> 7% of each run, Pallas kernels for 0% -> 7%
where the time goes in v5:
time: 174 us; the launch traced here: 173 us
  starting transfers between devices  60.2 us (35%)
  blocking collectives  51.6 us (30%)
  waiting for transfers between devices  17.4 us (10%)
  Pallas kernels  14.7 us (8%)
  local copies, waits for them, and re-layouts  13.6 us (8%)
  other arithmetic  9.69 us (6%)
  matrix products  4.32 us (2%)
    all_gather x1, blocking collectives, body(): whole = lax.all_gather(sent, 'y', axis=0, tiled=False)  51.6 us
    ppermute x9, starting transfers between devices, send(): lax.ppermute(value.astype(jnp.bfloat16), axis, route).astype(jnp.float32)  43.1 us
    ppermute x7, starting transfers between devices, swap(): return lax.ppermute(value, axis, [(0, 1), (1, 0)])  17.1 us
    ppermute x9, waiting for transfers between devices, send(): lax.ppermute(value.astype(jnp.bfloat16), axis, route).astype(jnp.float32)  16.6 us
    pallas_call x6, Pallas kernels, partial(): pl.pallas_call(partial_kernel, grid_spec=pltpu.PrefetchScalarGridSpec(num...  12.1 us
    unnamed x30, local copies, waits for them, and re-layouts  10.7 us
    dot_general x2, matrix products, slot_gradients(): jnp.dot(left, weight, preferred_element_type=jnp.float32) * (1.0 / SHIFT)  4.07 us
  transfers between devices with their start and end apart: 16, of which 5 were waited for; matrix products, arithmetic and copies ran while one was open for 7% of the time, Pallas kernels for 7%

profile of v5, /device:TPU:2, one launch (start us, length us, event | category | flops | bytes accessed | tf_op | source)
XLA Modules:
  0.0 173.0 jit_solution(14337947284939075944)
XLA Ops:
  3.2 4.0 %collective-permute-start = (f16[2,208,384]{2,1,0:T(8,128)(2,1)S(1)}, f16[2,208,384]{2,1,0:T(8,128)(2,1)S(1)}, u32[]{:S(2)}, u32[]{:S(2)}) collective-permute-start(f16[2,208,384]{2,1,0:T(8,128)(2,1)S(1)} %get-tuple-element.23), channel_id=1, source_target_pairs={{0,2},{2,0},{1,3},{3,1},{4,6},{6,4},{5,7},{7,5},{8,10},{10,8},{9,1... | collective-permute-start | bytes 958472 | tf_op jit(solution)/shard_map/ppermute | solution.py:46
  7.9 2.8 %copy-done.6 = bf16[512,6144]{1,0:T(8,128)(2,1)S(1)} copy-done((bf16[512,6144]{1,0:T(8,128)(2,1)S(1)}, bf16[512,6144]{1,0:T(8,128)(2,1)}, u32[]{:S(2)}) %copy-start.6) | copy-done | bytes 6291480
  10.7 2.6 %shard_map.91 = bf16[160,6144]{1,0:T(8,128)(2,1)S(1)} custom-call(bf16[160,512]{1,0:T(8,128)(2,1)S(1)} %fusion.7.picks_ref, bf16[512,6144]{1,0:T(8,128)(2,1)S(1)} %copy-done.6), custom_call_target="tpu_custom_call" | custom-call | tf_op jit(solution)/shard_map/pallas_call | solution.py:62
  16.3 2.4 %collective-permute-start.1 = (f16[2,208,384]{2,1,0:T(8,128)(2,1)S(1)}, f16[2,208,384]{2,1,0:T(8,128)(2,1)S(1)}, u32[]{:S(2)}, u32[]{:S(2)}) collective-permute-start(f16[2,208,384]{2,1,0:T(8,128)(2,1)S(1)} %get-tuple-element.17), channel_id=1, source_target_pairs={{0,1},{1,0},{2,3},{3,2},{4,5},{5,4},{6,7},{7,6},{8,9},{9,8},{10,11... | collective-permute-start | bytes 958472 | tf_op jit(solution)/shard_map/ppermute | solution.py:46
  20.5 51.6 %all-gather.2 = f16[6272,384]{1,0:T(8,128)(2,1)S(1)} all-gather(f16[784,384]{1,0:T(8,128)(2,1)S(1)} %pad_maximum_fusion), channel_id=2, replica_groups=mesh['z'=12,'xl'=2,'y'=8,'xh'=2,'core'=2] {'y'}, dimensions={0}, use_global_device_ids=true | all-gather | bytes 5419008 | tf_op jit(solution)/shard_map/all_gather | solution.py:167
  72.1 2.2 %copy-done.7 = f16[6272,384]{1,0:T(8,128)(2,1)} copy-done((f16[6272,384]{1,0:T(8,128)(2,1)}, f16[6272,384]{1,0:T(8,128)(2,1)S(1)}, u32[]{:S(2)}) %copy-start.7) | copy-done | bytes 4816920
  75.5 3.1 %slice_convert_fusion = bf16[8,768,384]{2,1,0:T(8,128)(2,1)S(1)} fusion(f16[8,784,384]{2,1,0:T(8,128)(2,1)} %bitcast.97), kind=kLoop, calls=%fused_computation | loop fusion | flops 2359296 | bytes 9437184 | tf_op jit(solution)/shard_map/convert_element_type | solution.py:170
  82.8 2.8 %convolution_multiply_fusion = f32[160,384]{1,0:T(8,128)S(1)} fusion(bf16[160,6144]{1,0:T(8,128)(2,1)} %collective-permute-done.3, bf16[6144,384]{1,0:T(8,128)(2,1)S(1)} %bitcast.87), kind=kOutput, calls=%fused_computation.1 | convolution fusion | flops 755036160 | bytes 6930432 | tf_op jit(solution)/shard_map/dot_general | solution.py:173
  85.8 3.0 %shard_map.96 = f32[12,2,160,128]{3,2,1,0:T(8,128)} custom-call(s32[1]{0:T(128)} %constant.127.clone.1.side_ref, bf16[160,384]{1,0:T(8,128)(2,1)S(1)} %pad_maximum_fusion.3.left_ref, bf16[12,2,2,128,384]{4,3,2,1,0:T(8,128)(2,1)S(1)} %bitcast.88), custom_call_target="tpu_custom_call" | custom-call | tf_op jit(solution)/shard_map/pallas_call | solution.py:100
  88.8 2.4 %collective-permute-start.9 = (f32[12,2,160,128]{3,2,1,0:T(8,128)}, f32[12,2,160,128]{3,2,1,0:T(8,128)S(1)}, u32[]{:S(2)}, u32[]{:S(2)}) collective-permute-start(f32[12,2,160,128]{3,2,1,0:T(8,128)} %shard_map.96), channel_id=1, source_target_pairs={{0,1},{1,0},{2,3},{3,2},{4,5},{5,4},{6,7},{7,6},{8,9},{9,8},{10,11... | collective-permute-start | bytes 5898248 | tf_op jit(solution)/shard_map/ppermute | solution.py:46
  91.2 2.3 %copy-done.2 = bf16[8,768,384]{2,1,0:T(8,128)(2,1)S(1)} copy-done((bf16[8,768,384]{2,1,0:T(8,128)(2,1)S(1)}, bf16[8,768,384]{2,1,0:T(8,128)(2,1)}, u32[]{:S(2)}) %copy-start.2) | copy-done | bytes 4718616
  96.9 2.4 %shard_map.92 = f32[12,1,160,128]{3,2,1,0:T(8,128)} custom-call(s32[1]{0:T(128)} %bitcast.side_ref, bf16[160,384]{1,0:T(8,128)(2,1)S(1)} %pad_maximum_fusion.3.left_ref, bf16[12,2,2,128,384]{4,3,2,1,0:T(8,128)(2,1)S(1)} %bitcast.90), custom_call_target="tpu_custom_call" | custom-call | tf_op jit(solution)/shard_map/pallas_call | solution.py:100
  99.3 2.4 %collective-permute-start.4 = (f32[12,1,160,128]{3,2,1,0:T(8,128)}, f32[12,1,160,128]{3,2,1,0:T(8,128)S(1)}, u32[]{:S(2)}, u32[]{:S(2)}) collective-permute-start(f32[12,1,160,128]{3,2,1,0:T(8,128)} %shard_map.92), channel_id=1, source_target_pairs={{0,1},{1,0},{2,3},{3,2},{4,5},{5,4},{6,7},{7,6},{8,9},{9,8},{10,11... | collective-permute-start | bytes 2949128 | tf_op jit(solution)/shard_map/ppermute | solution.py:46
  101.8 2.3 %shard_map.95 = bf16[12,1,160,128]{3,2,1,0:T(8,128)(2,1)} custom-call(s32[1]{0:T(128)} %bitcast.18.side_ref, bf16[160,384]{1,0:T(8,128)(2,1)S(1)} %pad_maximum_fusion.2.left_ref, bf16[12,2,2,128,384]{4,3,2,1,0:T(8,128)(2,1)S(1)} %bitcast.91, f32[12,1,160,128]{3,2,1,0:T(8,128)S(1)} %collective-permute-done.5.refs_0_), custom_call_target="tpu_custom_call" | custom-call | tf_op jit(solution)/shard_map/pallas_call | solution.py:100
  104.1 7.8 %collective-permute-start.6 = (bf16[12,1,160,128]{3,2,1,0:T(8,128)(2,1)}, bf16[12,1,160,128]{3,2,1,0:T(8,128)(2,1)}, u32[]{:S(2)}, u32[]{:S(2)}) collective-permute-start(bf16[12,1,160,128]{3,2,1,0:T(8,128)(2,1)} %shard_map.95), channel_id=1, source_target_pairs={{0,32},{32,0},{1,33},{33,1},{2,34},{34,2},{3,35},{35,3},{4,36},{36... | collective-permute-start | bytes 1474568 | tf_op jit(solution)/shard_map/ppermute | solution.py:187
  112.1 2.3 %copy-done.4 = bf16[8,768,384]{2,1,0:T(8,128)(2,1)S(1)} copy-done((bf16[8,768,384]{2,1,0:T(8,128)(2,1)S(1)}, bf16[8,768,384]{2,1,0:T(8,128)(2,1)}, u32[]{:S(2)}) %copy-start.4) | copy-done | bytes 4718616
  120.7 3.9 %collective-permute-start.10 = (bf16[4,2,160,128]{3,2,0,1:T(8,128)(2,1)S(1)}, bf16[4,2,160,128]{3,2,0,1:T(8,128)(2,1)S(1)}, u32[]{:S(2)}, u32[]{:S(2)}) collective-permute-start(bf16[4,2,160,128]{3,2,0,1:T(8,128)(2,1)S(1)} %bitcast.102), channel_id=1, source_target_pairs={{0,64},{64,128},{128,0},{192,256},{256,320},{320,192},{384,448},{4... | collective-permute-start | bytes 983048 | tf_op jit(solution)/shard_map/ppermute | solution.py:187
  125.8 2.8 %collective-permute-start.8 = (bf16[4,1,160,128]{3,2,0,1:T(8,128)(2,1)S(1)}, bf16[4,1,160,128]{3,2,0,1:T(8,128)(2,1)S(1)}, u32[]{:S(2)}, u32[]{:S(2)}) collective-permute-start(bf16[4,1,160,128]{3,2,0,1:T(8,128)(2,1)S(1)} %get-tuple-element.12), channel_id=1, source_target_pairs={{0,128},{64,0},{128,64},{192,320},{256,192},{320,256},{384,512},{4... | collective-permute-start | bytes 491528 | tf_op jit(solution)/shard_map/ppermute | solution.py:187
  128.7 3.0 %collective-permute-start.7 = (bf16[4,1,160,128]{3,2,0,1:T(8,128)(2,1)S(1)}, bf16[4,1,160,128]{3,2,0,1:T(8,128)(2,1)S(1)}, u32[]{:S(2)}, u32[]{:S(2)}) collective-permute-start(bf16[4,1,160,128]{3,2,0,1:T(8,128)(2,1)S(1)} %get-tuple-element.11), channel_id=1, source_target_pairs={{0,64},{64,128},{128,0},{192,256},{256,320},{320,192},{384,448},{4... | collective-permute-start | bytes 491528 | tf_op jit(solution)/shard_map/ppermute | solution.py:187
  131.7 7.2 %collective-permute-done.11 = bf16[4,2,160,128]{3,2,0,1:T(8,128)(2,1)S(1)} collective-permute-done((bf16[4,2,160,128]{3,2,0,1:T(8,128)(2,1)S(1)}, bf16[4,2,160,128]{3,2,0,1:T(8,128)(2,1)S(1)}, u32[]{:S(2)}, u32[]{:S(2)}) %collective-permute-start.11) | collective-permute-done | bytes 327712 | tf_op jit(solution)/shard_map/ppermute | solution.py:187
  140.9 3.1 %collective-permute-done.8 = bf16[4,1,160,128]{3,2,0,1:T(8,128)(2,1)S(1)} collective-permute-done((bf16[4,1,160,128]{3,2,0,1:T(8,128)(2,1)S(1)}, bf16[4,1,160,128]{3,2,0,1:T(8,128)(2,1)S(1)}, u32[]{:S(2)}, u32[]{:S(2)}) %collective-permute-start.8) | collective-permute-done | bytes 163872 | tf_op jit(solution)/shard_map/ppermute | solution.py:187
  146.3 10.5 %collective-permute-start.15 = (bf16[160,256]{1,0:T(8,128)(2,1)S(1)}, bf16[160,256]{1,0:T(8,128)(2,1)S(1)}, u32[]{:S(2)}, u32[]{:S(2)}) collective-permute-start(bf16[160,256]{1,0:T(8,128)(2,1)S(1)} %get-tuple-element.15), channel_id=1, source_target_pairs={{0,576},{64,640},{128,704},{192,0},{256,64},{320,128},{384,192},{4... | collective-permute-start | bytes 245768 | tf_op jit(solution)/shard_map/ppermute | solution.py:187
  158.7 9.3 %collective-permute-start.13 = (bf16[160,256]{1,0:T(8,128)(2,1)S(1)}, bf16[160,256]{1,0:T(8,128)(2,1)S(1)}, u32[]{:S(2)}, u32[]{:S(2)}) collective-permute-start(bf16[160,256]{1,0:T(8,128)(2,1)S(1)} %get-tuple-element.13), channel_id=1, source_target_pairs={{0,384},{64,448},{128,512},{192,576},{256,640},{320,704},{384,0},{... | collective-permute-start | bytes 245768 | tf_op jit(solution)/shard_map/ppermute | solution.py:187
  168.1 4.2 %collective-permute-done.13 = bf16[160,256]{1,0:T(8,128)(2,1)S(1)} collective-permute-done((bf16[160,256]{1,0:T(8,128)(2,1)S(1)}, bf16[160,256]{1,0:T(8,128)(2,1)S(1)}, u32[]{:S(2)}, u32[]{:S(2)}) %collective-permute-start.13) | collective-permute-done | bytes 81952 | tf_op jit(solution)/shard_map/ppermute | solution.py:187
  (95 shorter events, 31.2 us)
Async XLA Ops:
  0.0 18.9 %copy-start = (bf16[512,384]{1,0:T(8,128)(2,1)S(1)}, bf16[512,384]{1,0:T(8,128)(2,1)}, u32[]{:S(2)}) copy-start(bf16[512,384]{1,0:T(8,128)(2,1)} %param.15) | copy-start | bytes 1179652
  0.0 7.2 %copy-start.9 = (s32[512,2]{0,1:T(2,128)S(1)}, s32[512,2]{0,1:T(2,128)}, u32[]{:S(2)}) copy-start(s32[512,2]{0,1:T(2,128)} %param.10) | copy-start | bytes 12292
  3.2 12.8 %collective-permute-start = (f16[2,208,384]{2,1,0:T(8,128)(2,1)S(1)}, f16[2,208,384]{2,1,0:T(8,128)(2,1)S(1)}, u32[]{:S(2)}, u32[]{:S(2)}) collective-permute-start(f16[2,208,384]{2,1,0:T(8,128)(2,1)S(1)} %get-tuple-element.23), channel_id=1, source_target_pairs={{0,2},{2,0},{1,3},{3,1},{4,6},{6,4},{5,7},{7,5},{8,10},{10,8},{9,1... | collective-permute-start | bytes 958472 | tf_op jit(solution)/shard_map/ppermute | solution.py:46
  10.7 4.6 %copy-start.11 = (s32[1,4]{1,0:T(1,128)S(1)}, s32[1,4]{1,0:T(1,128)}, u32[]{:S(2)}) copy-start(s32[1,4]{1,0:T(1,128)} %param.13) | copy-start | bytes 52
  10.7 4.6 %copy-start.12 = (f32[1,4]{1,0:T(1,128)S(1)}, f32[1,4]{1,0:T(1,128)}, u32[]{:S(2)}) copy-start(f32[1,4]{1,0:T(1,128)} %param.14) | copy-start | bytes 52
  10.7 4.8 %copy-start.13 = (s32[1,8]{1,0:T(1,128)S(1)}, s32[1,8]{1,0:T(1,128)}, u32[]{:S(2)}) copy-start(s32[1,8]{1,0:T(1,128)} %param.12) | copy-start | bytes 100
  10.7 5.0 %copy-start.10 = (f32[512,2]{0,1:T(2,128)S(1)}, f32[512,2]{0,1:T(2,128)}, u32[]{:S(2)}) copy-start(f32[512,2]{0,1:T(2,128)} %param.11) | copy-start | bytes 12292
  13.4 69.4 %collective-permute-start.3 = (bf16[160,6144]{1,0:T(8,128)(2,1)S(1)}, bf16[160,6144]{1,0:T(8,128)(2,1)}, u32[]{:S(2)}, u32[]{:S(2)}) collective-permute-start(bf16[160,6144]{1,0:T(8,128)(2,1)S(1)} %shard_map.91), channel_id=1, source_target_pairs={{0,1},{1,0},{2,3},{3,2},{4,5},{5,4},{6,7},{7,6},{8,9},{9,8},{10,11... | collective-permute-start | bytes 5898248 | tf_op jit(solution)/shard_map/ppermute | solution.py:46
  16.3 3.6 %collective-permute-start.1 = (f16[2,208,384]{2,1,0:T(8,128)(2,1)S(1)}, f16[2,208,384]{2,1,0:T(8,128)(2,1)S(1)}, u32[]{:S(2)}, u32[]{:S(2)}) collective-permute-start(f16[2,208,384]{2,1,0:T(8,128)(2,1)S(1)} %get-tuple-element.17), channel_id=1, source_target_pairs={{0,1},{1,0},{2,3},{3,2},{4,5},{5,4},{6,7},{7,6},{8,9},{9,8},{10,11... | collective-permute-start | bytes 958472 | tf_op jit(solution)/shard_map/ppermute | solution.py:46
  78.7 7.2 %copy-start.1 = (bf16[8,768,384]{2,1,0:T(8,128)(2,1)}, bf16[8,768,384]{2,1,0:T(8,128)(2,1)S(1)}, u32[]{:S(2)}) copy-start(bf16[8,768,384]{2,1,0:T(8,128)(2,1)S(1)} %slice_convert_fusion) | copy-start | bytes 14155780
  80.9 4.7 %collective-permute-start.2 = (f32[160,192]{1,0:T(8,128)S(1)}, f32[160,192]{1,0:T(8,128)S(1)}, u32[]{:S(2)}, u32[]{:S(2)}) collective-permute-start(f32[160,192]{1,0:T(8,128)S(1)} %get-tuple-element.24), channel_id=1, source_target_pairs={{0,1},{1,0},{2,3},{3,2},{4,5},{5,4},{6,7},{7,6},{8,9},{9,8},{10,11... | collective-permute-start | bytes 368648 | tf_op jit(solution)/shard_map/ppermute | solution.py:46
  88.8 26.9 %collective-permute-start.9 = (f32[12,2,160,128]{3,2,1,0:T(8,128)}, f32[12,2,160,128]{3,2,1,0:T(8,128)S(1)}, u32[]{:S(2)}, u32[]{:S(2)}) collective-permute-start(f32[12,2,160,128]{3,2,1,0:T(8,128)} %shard_map.96), channel_id=1, source_target_pairs={{0,1},{1,0},{2,3},{3,2},{4,5},{5,4},{6,7},{7,6},{8,9},{9,8},{10,11... | collective-permute-start | bytes 5898248 | tf_op jit(solution)/shard_map/ppermute | solution.py:46
  94.9 7.0 %collective-permute-start.5 = (f32[12,1,160,128]{3,2,1,0:T(8,128)S(1)}, f32[12,1,160,128]{3,2,1,0:T(8,128)S(1)}, u32[]{:S(2)}, u32[]{:S(2)}) collective-permute-start(f32[12,1,160,128]{3,2,1,0:T(8,128)S(1)} %shard_map.94), channel_id=1, source_target_pairs={{0,1},{1,0},{2,3},{3,2},{4,5},{5,4},{6,7},{7,6},{8,9},{9,8},{10,11... | collective-permute-start | bytes 2949128 | tf_op jit(solution)/shard_map/ppermute | solution.py:46
  96.9 4.8 %copy-start.8 = (bf16[160,192]{1,0:T(8,128)(2,1)S(1)}, bf16[160,192]{1,0:T(8,128)(2,1)}, u32[]{:S(2)}) copy-start(bf16[160,192]{1,0:T(8,128)(2,1)} %get-tuple-element.19) | copy-start | bytes 184324
  99.3 12.7 %collective-permute-start.4 = (f32[12,1,160,128]{3,2,1,0:T(8,128)}, f32[12,1,160,128]{3,2,1,0:T(8,128)S(1)}, u32[]{:S(2)}, u32[]{:S(2)}) collective-permute-start(f32[12,1,160,128]{3,2,1,0:T(8,128)} %shard_map.92), channel_id=1, source_target_pairs={{0,1},{1,0},{2,3},{3,2},{4,5},{5,4},{6,7},{7,6},{8,9},{9,8},{10,11... | collective-permute-start | bytes 2949128 | tf_op jit(solution)/shard_map/ppermute | solution.py:46
  104.1 20.5 %collective-permute-start.6 = (bf16[12,1,160,128]{3,2,1,0:T(8,128)(2,1)}, bf16[12,1,160,128]{3,2,1,0:T(8,128)(2,1)}, u32[]{:S(2)}, u32[]{:S(2)}) collective-permute-start(bf16[12,1,160,128]{3,2,1,0:T(8,128)(2,1)} %shard_map.95), channel_id=1, source_target_pairs={{0,32},{32,0},{1,33},{33,1},{2,34},{34,2},{3,35},{35,3},{4,36},{36... | collective-permute-start | bytes 1474568 | tf_op jit(solution)/shard_map/ppermute | solution.py:187
  118.7 20.1 %collective-permute-start.11 = (bf16[4,2,160,128]{3,2,0,1:T(8,128)(2,1)S(1)}, bf16[4,2,160,128]{3,2,0,1:T(8,128)(2,1)S(1)}, u32[]{:S(2)}, u32[]{:S(2)}) collective-permute-start(bf16[4,2,160,128]{3,2,0,1:T(8,128)(2,1)S(1)} %bitcast.101), channel_id=1, source_target_pairs={{0,128},{64,0},{128,64},{192,320},{256,192},{320,256},{384,512},{4... | collective-permute-start | bytes 983048 | tf_op jit(solution)/shard_map/ppermute | solution.py:187
  120.7 18.2 %collective-permute-start.10 = (bf16[4,2,160,128]{3,2,0,1:T(8,128)(2,1)S(1)}, bf16[4,2,160,128]{3,2,0,1:T(8,128)(2,1)S(1)}, u32[]{:S(2)}, u32[]{:S(2)}) collective-permute-start(bf16[4,2,160,128]{3,2,0,1:T(8,128)(2,1)S(1)} %bitcast.102), channel_id=1, source_target_pairs={{0,64},{64,128},{128,0},{192,256},{256,320},{320,192},{384,448},{4... | collective-permute-start | bytes 983048 | tf_op jit(solution)/shard_map/ppermute | solution.py:187
  125.8 18.2 %collective-permute-start.8 = (bf16[4,1,160,128]{3,2,0,1:T(8,128)(2,1)S(1)}, bf16[4,1,160,128]{3,2,0,1:T(8,128)(2,1)S(1)}, u32[]{:S(2)}, u32[]{:S(2)}) collective-permute-start(bf16[4,1,160,128]{3,2,0,1:T(8,128)(2,1)S(1)} %get-tuple-element.12), channel_id=1, source_target_pairs={{0,128},{64,0},{128,64},{192,320},{256,192},{320,256},{384,512},{4... | collective-permute-start | bytes 491528 | tf_op jit(solution)/shard_map/ppermute | solution.py:187
  128.7 15.4 %collective-permute-start.7 = (bf16[4,1,160,128]{3,2,0,1:T(8,128)(2,1)S(1)}, bf16[4,1,160,128]{3,2,0,1:T(8,128)(2,1)S(1)}, u32[]{:S(2)}, u32[]{:S(2)}) collective-permute-start(bf16[4,1,160,128]{3,2,0,1:T(8,128)(2,1)S(1)} %get-tuple-element.11), channel_id=1, source_target_pairs={{0,64},{64,128},{128,0},{192,256},{256,320},{320,192},{384,448},{4... | collective-permute-start | bytes 491528 | tf_op jit(solution)/shard_map/ppermute | solution.py:187
  139.0 7.2 %collective-permute-start.12 = (bf16[4,160,128]{2,1,0:T(8,128)(2,1)S(1)}, bf16[4,160,128]{2,1,0:T(8,128)(2,1)S(1)}, u32[]{:S(2)}, u32[]{:S(2)}) collective-permute-start(bf16[4,160,128]{2,1,0:T(8,128)(2,1)S(1)} %fusion.10), channel_id=1, source_target_pairs={{0,32},{32,0},{1,33},{33,1},{2,34},{34,2},{3,35},{35,3},{4,36},{36... | collective-permute-start | bytes 491528 | tf_op jit(solution)/shard_map/ppermute | solution.py:187
  146.3 21.8 %collective-permute-start.15 = (bf16[160,256]{1,0:T(8,128)(2,1)S(1)}, bf16[160,256]{1,0:T(8,128)(2,1)S(1)}, u32[]{:S(2)}, u32[]{:S(2)}) collective-permute-start(bf16[160,256]{1,0:T(8,128)(2,1)S(1)} %get-tuple-element.15), channel_id=1, source_target_pairs={{0,576},{64,640},{128,704},{192,0},{256,64},{320,128},{384,192},{4... | collective-permute-start | bytes 245768 | tf_op jit(solution)/shard_map/ppermute | solution.py:187
  156.8 11.3 %collective-permute-start.14 = (bf16[160,256]{1,0:T(8,128)(2,1)S(1)}, bf16[160,256]{1,0:T(8,128)(2,1)S(1)}, u32[]{:S(2)}, u32[]{:S(2)}) collective-permute-start(bf16[160,256]{1,0:T(8,128)(2,1)S(1)} %get-tuple-element.14), channel_id=1, source_target_pairs={{0,192},{64,256},{128,320},{192,384},{256,448},{320,512},{384,576}... | collective-permute-start | bytes 245768 | tf_op jit(solution)/shard_map/ppermute | solution.py:187
  158.7 13.5 %collective-permute-start.13 = (bf16[160,256]{1,0:T(8,128)(2,1)S(1)}, bf16[160,256]{1,0:T(8,128)(2,1)S(1)}, u32[]{:S(2)}, u32[]{:S(2)}) collective-permute-start(bf16[160,256]{1,0:T(8,128)(2,1)S(1)} %get-tuple-element.13), channel_id=1, source_target_pairs={{0,384},{64,448},{128,512},{192,576},{256,640},{320,704},{384,0},{... | collective-permute-start | bytes 245768 | tf_op jit(solution)/shard_map/ppermute | solution.py:187
  (6 other events, 15.3 us)

commit v6 on v3

--- a/solution.py
+++ b/solution.py
@@ -1,6 +1,8 @@
 import jax
 import jax.numpy as jnp
 from jax import lax
+from jax.experimental import pallas as pl
+from jax.experimental.pallas import tpu as pltpu
 from jax.sharding import Mesh, PartitionSpec as P
 
 CAP = 160
@@ -44,6 +46,33 @@
     return lax.ppermute(value, axis, [(0, 1), (1, 0)])
 
 
+FREE = pl.CostEstimate(flops=0, bytes_accessed=0, transcendentals=0)
+LIMIT = pltpu.CompilerParams(vmem_limit_bytes=32 * 2**20)
+
+
+def rows_kernel(picks_ref, tokens_ref, out_ref):
+    out = jnp.dot(picks_ref[...], tokens_ref[...], preferred_element_type=jnp.float32)
+    out_ref[...] = out.astype(out_ref.dtype)
+
+
+def pick_rows(picks, tokens):
+    slots, depth = picks.shape
+    columns = tokens.shape[1]
+    block = columns // 6
+    return pl.pallas_call(
+        rows_kernel,
+        grid=(6,),
+        in_specs=[
+            pl.BlockSpec((slots, depth), lambda i: (0, 0)),
+            pl.BlockSpec((depth, block), lambda i: (0, i)),
+        ],
+        out_specs=pl.BlockSpec((slots, block), lambda i: (0, i)),
+        out_shape=jax.ShapeDtypeStruct((slots, columns), tokens.dtype),
+        cost_estimate=FREE,
+        compiler_params=LIMIT,
+    )(picks, tokens)
+
+
 def half_of(value, which, axis):
     size = value.shape[axis] // 2
     low = lax.slice_in_dim(value, 0, size, axis=axis)
@@ -81,7 +110,7 @@
 
     taken = slot_matrix(routes, CAP)
     picks = taken.astype(jnp.bfloat16)
-    slot_rows = jnp.dot(picks, tokens, preferred_element_type=jnp.float32).astype(jnp.bfloat16)
+    slot_rows = pick_rows(picks, tokens)
     grad_rows = jnp.dot(picks, hidden_grad, preferred_element_type=jnp.float32)
     coef_tok = token_scale(routes, router_prob, lengths[0], pair_mask[0], margins[0])
     coefficient = jnp.sum(jnp.where(taken, coef_tok[None, :], jnp.float32(0.0)), axis=1)
@@ -89,8 +118,8 @@
     their_rows = swap(slot_rows, "core")
     their_cotangent = swap(half_of(cotangent, 1 - core, 1), "core")
     cotangent = half_of(cotangent, core, 1)
-    sent, slot_rows, cotangent, their_rows, their_cotangent = lax.optimization_barrier(
-        (sent, slot_rows, cotangent, their_rows, their_cotangent)
+    sent, _, cotangent, their_cotangent = lax.optimization_barrier(
+        (sent, slot_rows, cotangent, their_cotangent)
     )
 
     whole = lax.all_gather(sent, "y", axis=0, tiled=False)
@@ -141,6 +170,7 @@
     arrived = send(leaving, "xl", across)
     part = columns[:, :, 1]
     second = swap(partial(their_grads, part), "core") + partial(own_grads, part)
+    second, their_grads = lax.optimization_barrier((second, their_grads))
     second = three(second.reshape(n_z, 2, CAP, width))
     part = pick(columns[:, :, 0], mine, 1)
     first = swap(partial(their_grads, part), "core") + partial(own_grads, part) + arrived

time: 173 us -> 190 us (1.098)
  the two profiles are of different devices: /device:TPU:2 before, /device:TPU:64 now
where the time goes in v6:
time: 190 us; the launch traced here: 189 us
  starting transfers between devices  56.7 us (30%)
  blocking collectives  51.7 us (27%)
  waiting for transfers between devices  38 us (20%)
  matrix products  17 us (9%)
  local copies, waits for them, and re-layouts  11.2 us (6%)
  other arithmetic  10.7 us (6%)
  Pallas kernels  2.6 us (1%)
    all_gather x1, blocking collectives, body(): whole = lax.all_gather(sent, 'y', axis=0, tiled=False)  51.7 us
    ppermute x9, starting transfers between devices, send(): lax.ppermute(value.astype(jnp.bfloat16), axis, route).astype(jnp.float32)  39.6 us
    ppermute x9, waiting for transfers between devices, send(): lax.ppermute(value.astype(jnp.bfloat16), axis, route).astype(jnp.float32)  26.8 us
    ppermute x7, starting transfers between devices, swap(): return lax.ppermute(value, axis, [(0, 1), (1, 0)])  17.2 us
    ppermute x7, waiting for transfers between devices, swap(): return lax.ppermute(value, axis, [(0, 1), (1, 0)])  11.2 us
    dot_general x6, matrix products, partial(): lax.dot_general(left, part.reshape(-1, units), (((1,), (1,)), ((), ())),...  11.2 us
    unnamed x24, local copies, waits for them, and re-layouts  6.46 us
    dot_general x2, matrix products, slot_gradients(): jnp.dot(left, weight, preferred_element_type=jnp.float32) * (1.0 / SHIFT)  5.56 us
  transfers between devices with their start and end apart: 16, of which 8 were waited for; matrix products, arithmetic and copies ran while one was open for 8% of the time, Pallas kernels for 1%

profile of v6, /device:TPU:64, one launch (start us, length us, event | category | flops | bytes accessed | tf_op | source)
XLA Modules:
  0.0 189.3 jit_solution(9997205965201965810)
XLA Ops:
  3.2 4.9 %collective-permute-start = (f16[2,208,384]{2,1,0:T(8,128)(2,1)S(1)}, f16[2,208,384]{2,1,0:T(8,128)(2,1)S(1)}, u32[]{:S(2)}, u32[]{:S(2)}) collective-permute-start(f16[2,208,384]{2,1,0:T(8,128)(2,1)S(1)} %get-tuple-element.39), channel_id=1, source_target_pairs={{0,2},{2,0},{1,3},{3,1},{4,6},{6,4},{5,7},{7,5},{8,10},{10,8},{9,1... | collective-permute-start | bytes 958472 | tf_op jit(solution)/shard_map/ppermute | solution.py:46
  9.8 6.0 %collective-permute-done = f16[2,208,384]{2,1,0:T(8,128)(2,1)S(1)} collective-permute-done((f16[2,208,384]{2,1,0:T(8,128)(2,1)S(1)}, f16[2,208,384]{2,1,0:T(8,128)(2,1)S(1)}, u32[]{:S(2)}, u32[]{:S(2)}) %collective-permute-start) | collective-permute-done | bytes 319520 | tf_op jit(solution)/shard_map/ppermute | solution.py:46
  18.9 2.4 %collective-permute-start.2 = (f32[160,192]{1,0:T(8,128)}, f32[160,192]{1,0:T(8,128)}, u32[]{:S(2)}, u32[]{:S(2)}) collective-permute-start(f32[160,192]{1,0:T(8,128)} %get-tuple-element.40), channel_id=1, source_target_pairs={{0,1},{1,0},{2,3},{3,2},{4,5},{5,4},{6,7},{7,6},{8,9},{9,8},{10,11... | collective-permute-start | bytes 368648 | tf_op jit(solution)/shard_map/ppermute | solution.py:46
  21.4 2.8 %copy-done.1 = bf16[512,6144]{1,0:T(8,128)(2,1)S(1)} copy-done((bf16[512,6144]{1,0:T(8,128)(2,1)S(1)}, bf16[512,6144]{1,0:T(8,128)(2,1)}, u32[]{:S(2)}) %copy-start.1) | copy-done | bytes 6291480
  24.2 2.6 %shard_map.91 = bf16[160,6144]{1,0:T(8,128)(2,1)S(1)} custom-call(bf16[160,512]{1,0:T(8,128)(2,1)S(1)} %fusion.19.picks_ref, bf16[512,6144]{1,0:T(8,128)(2,1)S(1)} %copy-done.1), custom_call_target="tpu_custom_call" | custom-call | tf_op jit(solution)/shard_map/pallas_call | solution.py:62
  29.3 51.7 %all-gather.2 = f16[6272,384]{1,0:T(8,128)(2,1)S(1)} all-gather(f16[784,384]{1,0:T(8,128)(2,1)S(1)} %pad_maximum_fusion), channel_id=2, replica_groups=mesh['z'=12,'xl'=2,'y'=8,'xh'=2,'core'=2] {'y'}, dimensions={0}, use_global_device_ids=true | all-gather | bytes 5419008 | tf_op jit(solution)/shard_map/all_gather | solution.py:125
  81.0 2.2 %copy-done.5 = f16[6272,384]{1,0:T(8,128)(2,1)} copy-done((f16[6272,384]{1,0:T(8,128)(2,1)}, f16[6272,384]{1,0:T(8,128)(2,1)S(1)}, u32[]{:S(2)}) %copy-start.5) | copy-done | bytes 4816920
  84.5 3.1 %slice_convert_fusion = bf16[8,768,384]{2,1,0:T(8,128)(2,1)S(1)} fusion(f16[8,784,384]{2,1,0:T(8,128)(2,1)} %bitcast.136), kind=kLoop, calls=%fused_computation | loop fusion | flops 2359296 | bytes 9437184 | tf_op jit(solution)/shard_map/convert_element_type | solution.py:128
  88.1 4.3 %convolution_multiply_fusion = f32[160,384]{1,0:T(8,128)S(1)} fusion(bf16[160,6144]{1,0:T(8,128)(2,1)} %collective-permute-done.3, bf16[6144,384]{1,0:T(8,128)(2,1)S(1)} %bitcast.131), kind=kOutput, calls=%fused_computation.15 | convolution fusion | flops 755036160 | bytes 6930432 | tf_op jit(solution)/shard_map/dot_general | solution.py:131
  99.1 2.2 %convolution_bitcast_fusion = f32[24,160,128]{2,1,0:T(8,128)} fusion(bf16[24,128,384]{2,1,0:T(8,128)(2,1)S(1)} %bitcast.133, bf16[160,384]{1,0:T(8,128)(2,1)S(1)} %pad_maximum_fusion.3), kind=kOutput, calls=%fused_computation.2 | convolution fusion | flops 377487360 | bytes 4448256 | tf_op jit(solution)/shard_map/dot_general | solution.py:142
  101.4 2.0 %collective-permute-start.5 = (f32[24,160,128]{2,1,0:T(8,128)}, f32[24,160,128]{2,1,0:T(8,128)}, u32[]{:S(2)}, u32[]{:S(2)}) collective-permute-start(f32[24,160,128]{2,1,0:T(8,128)} %convolution_bitcast_fusion), channel_id=1, source_target_pairs={{0,1},{1,0},{2,3},{3,2},{4,5},{5,4},{6,7},{7,6},{8,9},{9,8},{10,11... | collective-permute-start | bytes 5898248 | tf_op jit(solution)/shard_map/ppermute | solution.py:46
  103.4 4.1 %collective-permute-done.5 = f32[24,160,128]{2,1,0:T(8,128)} collective-permute-done((f32[24,160,128]{2,1,0:T(8,128)}, f32[24,160,128]{2,1,0:T(8,128)}, u32[]{:S(2)}, u32[]{:S(2)}) %collective-permute-start.5) | collective-permute-done | bytes 1966112 | tf_op jit(solution)/shard_map/ppermute | solution.py:46
  107.6 4.5 %bitcast_add_fusion = f32[24,160,128]{2,1,0:T(8,128)} fusion(f32[24,160,128]{2,1,0:T(8,128)} %collective-permute-done.5, bf16[24,128,384]{2,1,0:T(8,128)(2,1)} %bitcast.134, bf16[160,384]{1,0:T(8,128)(2,1)S(1)} %pad_maximum_fusion.2), kind=kOutput, calls=%fused_computation.1 | convolution fusion | flops 377978880 | bytes 6414336 | tf_op jit(solution)/shard_map/dot_general | solution.py:142
  117.8 4.3 %collective-permute-start.10 = (bf16[4,2,160,128]{3,2,0,1:T(8,128)(2,1)}, bf16[4,2,160,128]{3,2,0,1:T(8,128)(2,1)}, u32[]{:S(2)}, u32[]{:S(2)}) collective-permute-start(bf16[4,2,160,128]{3,2,0,1:T(8,128)(2,1)} %bitcast.128), channel_id=1, source_target_pairs={{0,64},{64,128},{128,0},{192,256},{256,320},{320,192},{384,448},{4... | collective-permute-start | bytes 983048 | tf_op jit(solution)/shard_map/ppermute | solution.py:154
  122.8 4.3 %collective-permute-start.11 = (bf16[4,2,160,128]{3,2,0,1:T(8,128)(2,1)}, bf16[4,2,160,128]{3,2,0,1:T(8,128)(2,1)}, u32[]{:S(2)}, u32[]{:S(2)}) collective-permute-start(bf16[4,2,160,128]{3,2,0,1:T(8,128)(2,1)} %bitcast.129), channel_id=1, source_target_pairs={{0,128},{64,0},{128,64},{192,320},{256,192},{320,256},{384,512},{4... | collective-permute-start | bytes 983048 | tf_op jit(solution)/shard_map/ppermute | solution.py:154
  129.2 4.2 %collective-permute-done.10 = bf16[4,2,160,128]{3,2,0,1:T(8,128)(2,1)} collective-permute-done((bf16[4,2,160,128]{3,2,0,1:T(8,128)(2,1)}, bf16[4,2,160,128]{3,2,0,1:T(8,128)(2,1)}, u32[]{:S(2)}, u32[]{:S(2)}) %collective-permute-start.10) | collective-permute-done | bytes 327712 | tf_op jit(solution)/shard_map/ppermute | solution.py:154
  133.4 7.9 %collective-permute-done.11 = bf16[4,2,160,128]{3,2,0,1:T(8,128)(2,1)} collective-permute-done((bf16[4,2,160,128]{3,2,0,1:T(8,128)(2,1)}, bf16[4,2,160,128]{3,2,0,1:T(8,128)(2,1)}, u32[]{:S(2)}, u32[]{:S(2)}) %collective-permute-start.11) | collective-permute-done | bytes 327712 | tf_op jit(solution)/shard_map/ppermute | solution.py:154
  146.6 2.2 %collective-permute-start.8 = (bf16[4,160,128]{2,1,0:T(8,128)(2,1)S(1)}, bf16[4,160,128]{2,1,0:T(8,128)(2,1)S(1)}, u32[]{:S(2)}, u32[]{:S(2)}) collective-permute-start(bf16[4,160,128]{2,1,0:T(8,128)(2,1)S(1)} %get-tuple-element.27), channel_id=1, source_target_pairs={{0,64},{64,128},{128,0},{192,256},{256,320},{320,192},{384,448},{4... | collective-permute-start | bytes 491528 | tf_op jit(solution)/shard_map/ppermute | solution.py:154
  148.8 3.7 %collective-permute-start.9 = (bf16[4,160,128]{2,1,0:T(8,128)(2,1)S(1)}, bf16[4,160,128]{2,1,0:T(8,128)(2,1)S(1)}, u32[]{:S(2)}, u32[]{:S(2)}) collective-permute-start(bf16[4,160,128]{2,1,0:T(8,128)(2,1)S(1)} %get-tuple-element.28), channel_id=1, source_target_pairs={{0,128},{64,0},{128,64},{192,320},{256,192},{320,256},{384,512},{4... | collective-permute-start | bytes 491528 | tf_op jit(solution)/shard_map/ppermute | solution.py:154
  154.3 4.7 %collective-permute-done.9 = bf16[4,160,128]{2,1,0:T(8,128)(2,1)S(1)} collective-permute-done((bf16[4,160,128]{2,1,0:T(8,128)(2,1)S(1)}, bf16[4,160,128]{2,1,0:T(8,128)(2,1)S(1)}, u32[]{:S(2)}, u32[]{:S(2)}) %collective-permute-start.9) | collective-permute-done | bytes 163872 | tf_op jit(solution)/shard_map/ppermute | solution.py:154
  159.1 7.9 %collective-permute-start.13 = (bf16[160,256]{1,0:T(8,128)(2,1)S(1)}, bf16[160,256]{1,0:T(8,128)(2,1)S(1)}, u32[]{:S(2)}, u32[]{:S(2)}) collective-permute-start(bf16[160,256]{1,0:T(8,128)(2,1)S(1)} %get-tuple-element.29), channel_id=1, source_target_pairs={{0,192},{64,256},{128,320},{192,384},{256,448},{320,512},{384,576}... | collective-permute-start | bytes 245768 | tf_op jit(solution)/shard_map/ppermute | solution.py:154
  167.0 8.5 %collective-permute-start.14 = (bf16[160,256]{1,0:T(8,128)(2,1)S(1)}, bf16[160,256]{1,0:T(8,128)(2,1)S(1)}, u32[]{:S(2)}, u32[]{:S(2)}) collective-permute-start(bf16[160,256]{1,0:T(8,128)(2,1)S(1)} %get-tuple-element.30), channel_id=1, source_target_pairs={{0,384},{64,448},{128,512},{192,576},{256,640},{320,704},{384,0},{... | collective-permute-start | bytes 245768 | tf_op jit(solution)/shard_map/ppermute | solution.py:154
  175.5 4.9 %collective-permute-start.15 = (bf16[160,256]{1,0:T(8,128)(2,1)S(1)}, bf16[160,256]{1,0:T(8,128)(2,1)S(1)}, u32[]{:S(2)}, u32[]{:S(2)}) collective-permute-start(bf16[160,256]{1,0:T(8,128)(2,1)S(1)} %get-tuple-element.31), channel_id=1, source_target_pairs={{0,576},{64,640},{128,704},{192,0},{256,64},{320,128},{384,192},{4... | collective-permute-start | bytes 245768 | tf_op jit(solution)/shard_map/ppermute | solution.py:154
  180.4 8.1 %collective-permute-done.15 = bf16[160,256]{1,0:T(8,128)(2,1)S(1)} collective-permute-done((bf16[160,256]{1,0:T(8,128)(2,1)S(1)}, bf16[160,256]{1,0:T(8,128)(2,1)S(1)}, u32[]{:S(2)}, u32[]{:S(2)}) %collective-permute-start.15) | collective-permute-done | bytes 81952 | tf_op jit(solution)/shard_map/ppermute | solution.py:154
  (90 shorter events, 34.3 us)
Async XLA Ops:
  0.0 9.5 %copy-start = (bf16[512,384]{1,0:T(8,128)(2,1)S(1)}, bf16[512,384]{1,0:T(8,128)(2,1)}, u32[]{:S(2)}) copy-start(bf16[512,384]{1,0:T(8,128)(2,1)} %param.15) | copy-start | bytes 1179652
  0.0 8.8 %copy-start.8 = (s32[1,4]{1,0:T(1,128)S(1)}, s32[1,4]{1,0:T(1,128)}, u32[]{:S(2)}) copy-start(s32[1,4]{1,0:T(1,128)} %param.13) | copy-start | bytes 52
  0.0 8.8 %copy-start.9 = (f32[1,4]{1,0:T(1,128)S(1)}, f32[1,4]{1,0:T(1,128)}, u32[]{:S(2)}) copy-start(f32[1,4]{1,0:T(1,128)} %param.14) | copy-start | bytes 52
  0.0 9.0 %copy-start.10 = (s32[1,8]{1,0:T(1,128)S(1)}, s32[1,8]{1,0:T(1,128)}, u32[]{:S(2)}) copy-start(s32[1,8]{1,0:T(1,128)} %param.12) | copy-start | bytes 100
  0.0 9.2 %copy-start.7 = (f32[512,2]{0,1:T(2,128)S(1)}, f32[512,2]{0,1:T(2,128)}, u32[]{:S(2)}) copy-start(f32[512,2]{0,1:T(2,128)} %param.11) | copy-start | bytes 12292
  3.2 12.7 %collective-permute-start = (f16[2,208,384]{2,1,0:T(8,128)(2,1)S(1)}, f16[2,208,384]{2,1,0:T(8,128)(2,1)S(1)}, u32[]{:S(2)}, u32[]{:S(2)}) collective-permute-start(f16[2,208,384]{2,1,0:T(8,128)(2,1)S(1)} %get-tuple-element.39), channel_id=1, source_target_pairs={{0,2},{2,0},{1,3},{3,1},{4,6},{6,4},{5,7},{7,5},{8,10},{10,8},{9,1... | collective-permute-start | bytes 958472 | tf_op jit(solution)/shard_map/ppermute | solution.py:46
  16.2 12.5 %collective-permute-start.1 = (f16[2,208,384]{2,1,0:T(8,128)(2,1)S(1)}, f16[2,208,384]{2,1,0:T(8,128)(2,1)S(1)}, u32[]{:S(2)}, u32[]{:S(2)}) collective-permute-start(f16[2,208,384]{2,1,0:T(8,128)(2,1)S(1)} %get-tuple-element.33), channel_id=1, source_target_pairs={{0,1},{1,0},{2,3},{3,2},{4,5},{5,4},{6,7},{7,6},{8,9},{9,8},{10,11... | collective-permute-start | bytes 958472 | tf_op jit(solution)/shard_map/ppermute | solution.py:46
  18.9 10.4 %collective-permute-start.2 = (f32[160,192]{1,0:T(8,128)}, f32[160,192]{1,0:T(8,128)}, u32[]{:S(2)}, u32[]{:S(2)}) collective-permute-start(f32[160,192]{1,0:T(8,128)} %get-tuple-element.40), channel_id=1, source_target_pairs={{0,1},{1,0},{2,3},{3,2},{4,5},{5,4},{6,7},{7,6},{8,9},{9,8},{10,11... | collective-permute-start | bytes 368648 | tf_op jit(solution)/shard_map/ppermute | solution.py:46
  26.8 61.3 %collective-permute-start.3 = (bf16[160,6144]{1,0:T(8,128)(2,1)S(1)}, bf16[160,6144]{1,0:T(8,128)(2,1)}, u32[]{:S(2)}, u32[]{:S(2)}) collective-permute-start(bf16[160,6144]{1,0:T(8,128)(2,1)S(1)} %shard_map.91), channel_id=1, source_target_pairs={{0,1},{1,0},{2,3},{3,2},{4,5},{5,4},{6,7},{7,6},{8,9},{9,8},{10,11... | collective-permute-start | bytes 5898248 | tf_op jit(solution)/shard_map/ppermute | solution.py:46
  88.1 10.5 %copy-start.2 = (bf16[12,2,1,128,384]{4,3,2,1,0:T(8,128)(2,1)}, bf16[12,2,1,128,384]{4,3,2,1,0:T(8,128)(2,1)S(1)}, u32[]{:S(2)}) copy-start(bf16[12,2,1,128,384]{4,3,2,1,0:T(8,128)(2,1)S(1)} %get-tuple-element.24) | copy-start | bytes 7077892
  88.1 11.0 %copy-start.4 = (bf16[12,2,1,128,384]{4,3,2,1,0:T(8,128)(2,1)}, bf16[12,2,1,128,384]{4,3,2,1,0:T(8,128)(2,1)S(1)}, u32[]{:S(2)}) copy-start(bf16[12,2,1,128,384]{4,3,2,1,0:T(8,128)(2,1)S(1)} %get-tuple-element.23) | copy-start | bytes 7077892
  94.1 4.5 %collective-permute-start.4 = (f32[12,160,128]{2,1,0:T(8,128)S(1)}, f32[12,160,128]{2,1,0:T(8,128)S(1)}, u32[]{:S(2)}, u32[]{:S(2)}) collective-permute-start(f32[12,160,128]{2,1,0:T(8,128)S(1)} %convolution_bitcast_fusion.3), channel_id=1, source_target_pairs={{0,1},{1,0},{2,3},{3,2},{4,5},{5,4},{6,7},{7,6},{8,9},{9,8},{10,11... | collective-permute-start | bytes 2949128 | tf_op jit(solution)/shard_map/ppermute | solution.py:46
  101.4 6.2 %collective-permute-start.5 = (f32[24,160,128]{2,1,0:T(8,128)}, f32[24,160,128]{2,1,0:T(8,128)}, u32[]{:S(2)}, u32[]{:S(2)}) collective-permute-start(f32[24,160,128]{2,1,0:T(8,128)} %convolution_bitcast_fusion), channel_id=1, source_target_pairs={{0,1},{1,0},{2,3},{3,2},{4,5},{5,4},{6,7},{7,6},{8,9},{9,8},{10,11... | collective-permute-start | bytes 5898248 | tf_op jit(solution)/shard_map/ppermute | solution.py:46
  103.4 8.7 %copy-start.3 = (bf16[12,2,1,128,384]{4,3,2,1,0:T(8,128)(2,1)S(1)}, bf16[12,2,1,128,384]{4,3,2,1,0:T(8,128)(2,1)}, u32[]{:S(2)}) copy-start(bf16[12,2,1,128,384]{4,3,2,1,0:T(8,128)(2,1)} %copy-done.2) | copy-start | bytes 7077892
  113.6 31.1 %collective-permute-start.6 = (f32[12,160,128]{2,1,0:T(8,128)}, f32[12,160,128]{2,1,0:T(8,128)}, u32[]{:S(2)}, u32[]{:S(2)}) collective-permute-start(f32[12,160,128]{2,1,0:T(8,128)} %convolution_bitcast_fusion.2), channel_id=1, source_target_pairs={{0,1},{1,0},{2,3},{3,2},{4,5},{5,4},{6,7},{7,6},{8,9},{9,8},{10,11... | collective-permute-start | bytes 2949128 | tf_op jit(solution)/shard_map/ppermute | solution.py:46
  117.8 15.6 %collective-permute-start.10 = (bf16[4,2,160,128]{3,2,0,1:T(8,128)(2,1)}, bf16[4,2,160,128]{3,2,0,1:T(8,128)(2,1)}, u32[]{:S(2)}, u32[]{:S(2)}) collective-permute-start(bf16[4,2,160,128]{3,2,0,1:T(8,128)(2,1)} %bitcast.128), channel_id=1, source_target_pairs={{0,64},{64,128},{128,0},{192,256},{256,320},{320,192},{384,448},{4... | collective-permute-start | bytes 983048 | tf_op jit(solution)/shard_map/ppermute | solution.py:154
  122.8 18.4 %collective-permute-start.11 = (bf16[4,2,160,128]{3,2,0,1:T(8,128)(2,1)}, bf16[4,2,160,128]{3,2,0,1:T(8,128)(2,1)}, u32[]{:S(2)}, u32[]{:S(2)}) collective-permute-start(bf16[4,2,160,128]{3,2,0,1:T(8,128)(2,1)} %bitcast.129), channel_id=1, source_target_pairs={{0,128},{64,0},{128,64},{192,320},{256,192},{320,256},{384,512},{4... | collective-permute-start | bytes 983048 | tf_op jit(solution)/shard_map/ppermute | solution.py:154
  127.2 17.5 %collective-permute-start.7 = (bf16[12,160,128]{2,1,0:T(8,128)(2,1)S(1)}, bf16[12,160,128]{2,1,0:T(8,128)(2,1)}, u32[]{:S(2)}, u32[]{:S(2)}) collective-permute-start(bf16[12,160,128]{2,1,0:T(8,128)(2,1)S(1)} %fusion.3), channel_id=1, source_target_pairs={{0,32},{32,0},{1,33},{33,1},{2,34},{34,2},{3,35},{35,3},{4,36},{36... | collective-permute-start | bytes 1474568 | tf_op jit(solution)/shard_map/ppermute | solution.py:154
  142.7 9.7 %collective-permute-start.12 = (bf16[4,160,128]{2,1,0:T(8,128)(2,1)S(1)}, bf16[4,160,128]{2,1,0:T(8,128)(2,1)S(1)}, u32[]{:S(2)}, u32[]{:S(2)}) collective-permute-start(bf16[4,160,128]{2,1,0:T(8,128)(2,1)S(1)} %fusion.21), channel_id=1, source_target_pairs={{0,32},{32,0},{1,33},{33,1},{2,34},{34,2},{3,35},{35,3},{4,36},{36... | collective-permute-start | bytes 491528 | tf_op jit(solution)/shard_map/ppermute | solution.py:154
  146.6 7.7 %collective-permute-start.8 = (bf16[4,160,128]{2,1,0:T(8,128)(2,1)S(1)}, bf16[4,160,128]{2,1,0:T(8,128)(2,1)S(1)}, u32[]{:S(2)}, u32[]{:S(2)}) collective-permute-start(bf16[4,160,128]{2,1,0:T(8,128)(2,1)S(1)} %get-tuple-element.27), channel_id=1, source_target_pairs={{0,64},{64,128},{128,0},{192,256},{256,320},{320,192},{384,448},{4... | collective-permute-start | bytes 491528 | tf_op jit(solution)/shard_map/ppermute | solution.py:154
  148.8 10.3 %collective-permute-start.9 = (bf16[4,160,128]{2,1,0:T(8,128)(2,1)S(1)}, bf16[4,160,128]{2,1,0:T(8,128)(2,1)S(1)}, u32[]{:S(2)}, u32[]{:S(2)}) collective-permute-start(bf16[4,160,128]{2,1,0:T(8,128)(2,1)S(1)} %get-tuple-element.28), channel_id=1, source_target_pairs={{0,128},{64,0},{128,64},{192,320},{256,192},{320,256},{384,512},{4... | collective-permute-start | bytes 491528 | tf_op jit(solution)/shard_map/ppermute | solution.py:154
  159.1 21.3 %collective-permute-start.13 = (bf16[160,256]{1,0:T(8,128)(2,1)S(1)}, bf16[160,256]{1,0:T(8,128)(2,1)S(1)}, u32[]{:S(2)}, u32[]{:S(2)}) collective-permute-start(bf16[160,256]{1,0:T(8,128)(2,1)S(1)} %get-tuple-element.29), channel_id=1, source_target_pairs={{0,192},{64,256},{128,320},{192,384},{256,448},{320,512},{384,576}... | collective-permute-start | bytes 245768 | tf_op jit(solution)/shard_map/ppermute | solution.py:154
  167.0 13.4 %collective-permute-start.14 = (bf16[160,256]{1,0:T(8,128)(2,1)S(1)}, bf16[160,256]{1,0:T(8,128)(2,1)S(1)}, u32[]{:S(2)}, u32[]{:S(2)}) collective-permute-start(bf16[160,256]{1,0:T(8,128)(2,1)S(1)} %get-tuple-element.30), channel_id=1, source_target_pairs={{0,384},{64,448},{128,512},{192,576},{256,640},{320,704},{384,0},{... | collective-permute-start | bytes 245768 | tf_op jit(solution)/shard_map/ppermute | solution.py:154
  175.5 13.1 %collective-permute-start.15 = (bf16[160,256]{1,0:T(8,128)(2,1)S(1)}, bf16[160,256]{1,0:T(8,128)(2,1)S(1)}, u32[]{:S(2)}, u32[]{:S(2)}) collective-permute-start(bf16[160,256]{1,0:T(8,128)(2,1)S(1)} %get-tuple-element.31), channel_id=1, source_target_pairs={{0,576},{64,640},{128,704},{192,0},{256,64},{320,128},{384,192},{4... | collective-permute-start | bytes 245768 | tf_op jit(solution)/shard_map/ppermute | solution.py:154
  (3 other events, 13.1 us)

commit v7 on v6

--- a/solution.py
+++ b/solution.py
@@ -115,12 +115,10 @@
     coef_tok = token_scale(routes, router_prob, lengths[0], pair_mask[0], margins[0])
     coefficient = jnp.sum(jnp.where(taken, coef_tok[None, :], jnp.float32(0.0)), axis=1)
     cotangent = coefficient[:, None] * grad_rows
+    sent = lax.optimization_barrier((sent, slot_rows, cotangent))[0]
     their_rows = swap(slot_rows, "core")
     their_cotangent = swap(half_of(cotangent, 1 - core, 1), "core")
     cotangent = half_of(cotangent, core, 1)
-    sent, _, cotangent, their_cotangent = lax.optimization_barrier(
-        (sent, slot_rows, cotangent, their_cotangent)
-    )
 
     whole = lax.all_gather(sent, "y", axis=0, tiled=False)
     total_pairs = jnp.sum(whole[:, 4 * rows, :pairs].astype(jnp.float32))
@@ -164,16 +162,17 @@
     across = [(0, 1), (1, 0)]
     part = pick(columns[:, :, 0], 1 - mine, 1)
     theirs = swap(partial(their_grads, part), "core")
+    both = partial(their_grads, columns[:, :, 1])
+    last = partial(their_grads, pick(columns[:, :, 0], mine, 1))
+    slot_rows, both, last = lax.optimization_barrier((slot_rows, both, last))
     own_grads = slot_gradients(slot_rows, weight, cotangent)
     leaving = (partial(own_grads, part) + theirs).astype(jnp.bfloat16)
-    leaving, own_grads, their_grads = lax.optimization_barrier((leaving, own_grads, their_grads))
     arrived = send(leaving, "xl", across)
     part = columns[:, :, 1]
-    second = swap(partial(their_grads, part), "core") + partial(own_grads, part)
-    second, their_grads = lax.optimization_barrier((second, their_grads))
+    second = swap(both, "core") + partial(own_grads, part)
     second = three(second.reshape(n_z, 2, CAP, width))
     part = pick(columns[:, :, 0], mine, 1)
-    first = swap(partial(their_grads, part), "core") + partial(own_grads, part) + arrived
+    first = swap(last, "core") + partial(own_grads, part) + arrived
     second = pick(second, mine, 1) + send(pick(second, 1 - mine, 1), "xl", across)
     first = three(first)
     total = jnp.concatenate([first, second], axis=2)

time: 190 us -> 173 us (0.911)
  the two profiles are of different devices: /device:TPU:64 before, /device:TPU:2 now
where the time goes in v7:
time: 173 us; the launch traced here: 172 us
  starting transfers between devices  59.9 us (35%)
  blocking collectives  51.7 us (30%)
  matrix products  19 us (11%)
  waiting for transfers between devices  18.4 us (11%)
  local copies, waits for them, and re-layouts  10.8 us (6%)
  other arithmetic  8.63 us (5%)
  Pallas kernels  2.62 us (2%)
    all_gather x1, blocking collectives, body(): whole = lax.all_gather(sent, 'y', axis=0, tiled=False)  51.7 us
    ppermute x9, starting transfers between devices, send(): lax.ppermute(value.astype(jnp.bfloat16), axis, route).astype(jnp.float32)  43.3 us
    ppermute x9, waiting for transfers between devices, send(): lax.ppermute(value.astype(jnp.bfloat16), axis, route).astype(jnp.float32)  18.3 us
    ppermute x7, starting transfers between devices, swap(): return lax.ppermute(value, axis, [(0, 1), (1, 0)])  16.6 us
    dot_general x6, matrix products, partial(): lax.dot_general(left, part.reshape(-1, units), (((1,), (1,)), ((), ())),...  11.4 us
    dot_general x2, matrix products, slot_gradients(): jnp.dot(left, weight, preferred_element_type=jnp.float32) * (1.0 / SHIFT)  7.28 us
    unnamed x28, local copies, waits for them, and re-layouts  6.62 us
  transfers between devices with their start and end apart: 16, of which 7 were waited for; matrix products, arithmetic and copies ran while one was open for 13% of the time, Pallas kernels for 2%

profile of v7, /device:TPU:2, one launch (start us, length us, event | category | flops | bytes accessed | tf_op | source)
XLA Modules:
  0.0 172.4 jit_solution(14698523761232526099)
XLA Ops:
  3.1 4.0 %collective-permute-start.1 = (f16[2,208,384]{2,1,0:T(8,128)(2,1)S(1)}, f16[2,208,384]{2,1,0:T(8,128)(2,1)S(1)}, u32[]{:S(2)}, u32[]{:S(2)}) collective-permute-start(f16[2,208,384]{2,1,0:T(8,128)(2,1)S(1)} %get-tuple-element.31), channel_id=1, source_target_pairs={{0,2},{2,0},{1,3},{3,1},{4,6},{6,4},{5,7},{7,5},{8,10},{10,8},{9,1... | collective-permute-start | bytes 958472 | tf_op jit(solution)/shard_map/ppermute | solution.py:46
  7.9 2.8 %copy-done.1 = bf16[512,6144]{1,0:T(8,128)(2,1)S(1)} copy-done((bf16[512,6144]{1,0:T(8,128)(2,1)S(1)}, bf16[512,6144]{1,0:T(8,128)(2,1)}, u32[]{:S(2)}) %copy-start.1) | copy-done | bytes 6291480
  10.7 2.6 %shard_map.91 = bf16[160,6144]{1,0:T(8,128)(2,1)S(1)} custom-call(bf16[160,512]{1,0:T(8,128)(2,1)S(1)} %fusion.19.picks_ref, bf16[512,6144]{1,0:T(8,128)(2,1)S(1)} %copy-done.1), custom_call_target="tpu_custom_call" | custom-call | tf_op jit(solution)/shard_map/pallas_call | solution.py:62
  17.1 2.4 %collective-permute-start.2 = (f16[2,208,384]{2,1,0:T(8,128)(2,1)}, f16[2,208,384]{2,1,0:T(8,128)(2,1)S(1)}, u32[]{:S(2)}, u32[]{:S(2)}) collective-permute-start(f16[2,208,384]{2,1,0:T(8,128)(2,1)} %get-tuple-element.25), channel_id=1, source_target_pairs={{0,1},{1,0},{2,3},{3,2},{4,5},{5,4},{6,7},{7,6},{8,9},{9,8},{10,11... | collective-permute-start | bytes 958472 | tf_op jit(solution)/shard_map/ppermute | solution.py:46
  22.4 51.7 %all-gather.2 = f16[6272,384]{1,0:T(8,128)(2,1)S(1)} all-gather(f16[784,384]{1,0:T(8,128)(2,1)S(1)} %pad_maximum_fusion), channel_id=2, replica_groups=mesh['z'=12,'xl'=2,'y'=8,'xh'=2,'core'=2] {'y'}, dimensions={0}, use_global_device_ids=true | all-gather | bytes 5419008 | tf_op jit(solution)/shard_map/all_gather | solution.py:123
  74.1 2.2 %copy-done.7 = f16[6272,384]{1,0:T(8,128)(2,1)} copy-done((f16[6272,384]{1,0:T(8,128)(2,1)}, f16[6272,384]{1,0:T(8,128)(2,1)S(1)}, u32[]{:S(2)}) %copy-start.7) | copy-done | bytes 4816920
  77.6 3.1 %slice_convert_fusion = bf16[8,768,384]{2,1,0:T(8,128)(2,1)S(1)} fusion(f16[8,784,384]{2,1,0:T(8,128)(2,1)} %bitcast.129), kind=kLoop, calls=%fused_computation | loop fusion | flops 2359296 | bytes 9437184 | tf_op jit(solution)/shard_map/convert_element_type | solution.py:126
  82.9 3.8 %convolution_multiply_fusion.1 = f32[160,384]{1,0:T(8,128)S(1)} fusion(bf16[160,6144]{1,0:T(8,128)(2,1)} %collective-permute-done.3, bf16[6144,384]{1,0:T(8,128)(2,1)S(1)} %bitcast.124), kind=kOutput, calls=%fused_computation.16 | convolution fusion | flops 755036160 | bytes 6930432 | tf_op jit(solution)/shard_map/dot_general | solution.py:129
  87.7 2.2 %convolution_bitcast_fusion = f32[24,160,128]{2,1,0:T(8,128)} fusion(bf16[24,128,384]{2,1,0:T(8,128)(2,1)S(1)} %bitcast.126, bf16[160,192]{1,0:T(8,128)(2,1)S(1)} %get-tuple-element.29, bf16[160,192]{1,0:T(8,128)(2,1)S(1)} %get-tuple-element.28), kind=kOutput, calls=%fused_computation.2 | convolution fusion | flops 377733120 | bytes 4448256 | tf_op jit(solution)/shard_map/dot_general | solution.py:140
  93.4 2.8 %convolution_bitcast_fusion.1 = f32[12,160,128]{2,1,0:T(8,128)} fusion(bf16[12,2,1,128,384]{4,3,2,1,0:T(8,128)(2,1)} %copy-done.5, s32[]{:T(128)S(6)} %select_n.134, bf16[160,192]{1,0:T(8,128)(2,1)S(1)} %get-tuple-element.29, bf16[160,192]{1,0:T(8,128)(2,1)S(1)} %get-tuple-element.28), kind=kOutput, calls=%fused_computation.3 | convolution fusion | flops 188989440 | bytes 2285572 | tf_op jit(solution)/shard_map/dot_general | solution.py:140
  96.2 2.4 %collective-permute-start.5 = (f32[12,160,128]{2,1,0:T(8,128)}, f32[12,160,128]{2,1,0:T(8,128)}, u32[]{:S(2)}, u32[]{:S(2)}) collective-permute-start(f32[12,160,128]{2,1,0:T(8,128)} %convolution_bitcast_fusion.1), channel_id=1, source_target_pairs={{0,1},{1,0},{2,3},{3,2},{4,5},{5,4},{6,7},{7,6},{8,9},{9,8},{10,11... | collective-permute-start | bytes 2949128 | tf_op jit(solution)/shard_map/ppermute | solution.py:46
  100.8 3.5 %convolution_multiply_fusion = f32[160,384]{1,0:T(8,128)S(1)} fusion(bf16[160,6144]{1,0:T(8,128)(2,1)S(1)} %shard_map.91, bf16[6144,384]{1,0:T(8,128)(2,1)} %bitcast.125), kind=kOutput, calls=%fused_computation.15 | convolution fusion | flops 755036160 | bytes 6930432 | tf_op jit(solution)/shard_map/dot_general | solution.py:129
  106.4 7.8 %collective-permute-start.6 = (bf16[12,160,128]{2,1,0:T(8,128)(2,1)S(1)}, bf16[12,160,128]{2,1,0:T(8,128)(2,1)S(1)}, u32[]{:S(2)}, u32[]{:S(2)}) collective-permute-start(bf16[12,160,128]{2,1,0:T(8,128)(2,1)S(1)} %fusion.3), channel_id=1, source_target_pairs={{0,32},{32,0},{1,33},{33,1},{2,34},{34,2},{3,35},{35,3},{4,36},{36... | collective-permute-start | bytes 1474568 | tf_op jit(solution)/shard_map/ppermute | solution.py:152
  114.2 2.5 %bitcast_add_fusion = f32[24,160,128]{2,1,0:T(8,128)S(1)} fusion(f32[24,160,128]{2,1,0:T(8,128)} %collective-permute-done.9, bf16[24,128,384]{2,1,0:T(8,128)(2,1)S(1)} %bitcast.127, bf16[160,192]{1,0:T(8,128)(2,1)S(1)} %get-tuple-element.27, bf16[160,192]{1,0:T(8,128)(2,1)S(1)} %get-tuple-element.26), kind=kOutput, calls=%fused_computation.1 | convolution fusion | flops 378224640 | bytes 6414336 | tf_op jit(solution)/shard_map/dot_general | solution.py:140
  118.8 4.8 %collective-permute-start.11 = (bf16[4,2,160,128]{3,2,0,1:T(8,128)(2,1)S(1)}, bf16[4,2,160,128]{3,2,0,1:T(8,128)(2,1)S(1)}, u32[]{:S(2)}, u32[]{:S(2)}) collective-permute-start(bf16[4,2,160,128]{3,2,0,1:T(8,128)(2,1)S(1)} %bitcast.136), channel_id=1, source_target_pairs={{0,128},{64,0},{128,64},{192,320},{256,192},{320,256},{384,512},{4... | collective-permute-start | bytes 983048 | tf_op jit(solution)/shard_map/ppermute | solution.py:152
  123.6 2.4 %collective-permute-done.6 = bf16[12,160,128]{2,1,0:T(8,128)(2,1)S(1)} collective-permute-done((bf16[12,160,128]{2,1,0:T(8,128)(2,1)S(1)}, bf16[12,160,128]{2,1,0:T(8,128)(2,1)S(1)}, u32[]{:S(2)}, u32[]{:S(2)}) %collective-permute-start.6) | collective-permute-done | bytes 491552 | tf_op jit(solution)/shard_map/ppermute | solution.py:152
  128.6 4.8 %collective-permute-start.8 = (bf16[4,160,128]{2,1,0:T(8,128)(2,1)S(1)}, bf16[4,160,128]{2,1,0:T(8,128)(2,1)S(1)}, u32[]{:S(2)}, u32[]{:S(2)}) collective-permute-start(bf16[4,160,128]{2,1,0:T(8,128)(2,1)S(1)} %get-tuple-element.20), channel_id=1, source_target_pairs={{0,128},{64,0},{128,64},{192,320},{256,192},{320,256},{384,512},{4... | collective-permute-start | bytes 491528 | tf_op jit(solution)/shard_map/ppermute | solution.py:152
  133.4 3.8 %collective-permute-done.11 = bf16[4,2,160,128]{3,2,0,1:T(8,128)(2,1)S(1)} collective-permute-done((bf16[4,2,160,128]{3,2,0,1:T(8,128)(2,1)S(1)}, bf16[4,2,160,128]{3,2,0,1:T(8,128)(2,1)S(1)}, u32[]{:S(2)}, u32[]{:S(2)}) %collective-permute-start.11) | collective-permute-done | bytes 327712 | tf_op jit(solution)/shard_map/ppermute | solution.py:152
  140.8 2.7 %collective-permute-done.8 = bf16[4,160,128]{2,1,0:T(8,128)(2,1)S(1)} collective-permute-done((bf16[4,160,128]{2,1,0:T(8,128)(2,1)S(1)}, bf16[4,160,128]{2,1,0:T(8,128)(2,1)S(1)}, u32[]{:S(2)}, u32[]{:S(2)}) %collective-permute-start.8) | collective-permute-done | bytes 163872 | tf_op jit(solution)/shard_map/ppermute | solution.py:152
  145.3 5.9 %collective-permute-start.13 = (bf16[160,256]{1,0:T(8,128)(2,1)S(1)}, bf16[160,256]{1,0:T(8,128)(2,1)S(1)}, u32[]{:S(2)}, u32[]{:S(2)}) collective-permute-start(bf16[160,256]{1,0:T(8,128)(2,1)S(1)} %get-tuple-element.21), channel_id=1, source_target_pairs={{0,192},{64,256},{128,320},{192,384},{256,448},{320,512},{384,576}... | collective-permute-start | bytes 245768 | tf_op jit(solution)/shard_map/ppermute | solution.py:152
  151.2 10.6 %collective-permute-start.14 = (bf16[160,256]{1,0:T(8,128)(2,1)S(1)}, bf16[160,256]{1,0:T(8,128)(2,1)S(1)}, u32[]{:S(2)}, u32[]{:S(2)}) collective-permute-start(bf16[160,256]{1,0:T(8,128)(2,1)S(1)} %get-tuple-element.22), channel_id=1, source_target_pairs={{0,384},{64,448},{128,512},{192,576},{256,640},{320,704},{384,0},{... | collective-permute-start | bytes 245768 | tf_op jit(solution)/shard_map/ppermute | solution.py:152
  161.8 3.6 %collective-permute-start.15 = (bf16[160,256]{1,0:T(8,128)(2,1)S(1)}, bf16[160,256]{1,0:T(8,128)(2,1)S(1)}, u32[]{:S(2)}, u32[]{:S(2)}) collective-permute-start(bf16[160,256]{1,0:T(8,128)(2,1)S(1)} %get-tuple-element.23), channel_id=1, source_target_pairs={{0,576},{64,640},{128,704},{192,0},{256,64},{320,128},{384,192},{4... | collective-permute-start | bytes 245768 | tf_op jit(solution)/shard_map/ppermute | solution.py:152
  165.5 2.6 %collective-permute-done.14 = bf16[160,256]{1,0:T(8,128)(2,1)S(1)} collective-permute-done((bf16[160,256]{1,0:T(8,128)(2,1)S(1)}, bf16[160,256]{1,0:T(8,128)(2,1)S(1)}, u32[]{:S(2)}, u32[]{:S(2)}) %collective-permute-start.14) | collective-permute-done | bytes 81952 | tf_op jit(solution)/shard_map/ppermute | solution.py:152
  168.1 3.6 %collective-permute-done.15 = bf16[160,256]{1,0:T(8,128)(2,1)S(1)} collective-permute-done((bf16[160,256]{1,0:T(8,128)(2,1)S(1)}, bf16[160,256]{1,0:T(8,128)(2,1)S(1)}, u32[]{:S(2)}, u32[]{:S(2)}) %collective-permute-start.15) | collective-permute-done | bytes 81952 | tf_op jit(solution)/shard_map/ppermute | solution.py:152
  (92 shorter events, 32.3 us)
Async XLA Ops:
  0.0 19.5 %copy-start = (bf16[512,384]{1,0:T(8,128)(2,1)S(1)}, bf16[512,384]{1,0:T(8,128)(2,1)}, u32[]{:S(2)}) copy-start(bf16[512,384]{1,0:T(8,128)(2,1)} %param.15) | copy-start | bytes 1179652
  0.0 7.2 %copy-start.8 = (s32[512,2]{0,1:T(2,128)S(1)}, s32[512,2]{0,1:T(2,128)}, u32[]{:S(2)}) copy-start(s32[512,2]{0,1:T(2,128)} %param.10) | copy-start | bytes 12292
  3.1 12.9 %collective-permute-start.1 = (f16[2,208,384]{2,1,0:T(8,128)(2,1)S(1)}, f16[2,208,384]{2,1,0:T(8,128)(2,1)S(1)}, u32[]{:S(2)}, u32[]{:S(2)}) collective-permute-start(f16[2,208,384]{2,1,0:T(8,128)(2,1)S(1)} %get-tuple-element.31), channel_id=1, source_target_pairs={{0,2},{2,0},{1,3},{3,1},{4,6},{6,4},{5,7},{7,5},{8,10},{10,8},{9,1... | collective-permute-start | bytes 958472 | tf_op jit(solution)/shard_map/ppermute | solution.py:46
  10.7 4.8 %copy-start.12 = (s32[1,8]{1,0:T(1,128)S(1)}, s32[1,8]{1,0:T(1,128)}, u32[]{:S(2)}) copy-start(s32[1,8]{1,0:T(1,128)} %param.12) | copy-start | bytes 100
  10.7 5.1 %copy-start.9 = (f32[512,2]{0,1:T(2,128)S(1)}, f32[512,2]{0,1:T(2,128)}, u32[]{:S(2)}) copy-start(f32[512,2]{0,1:T(2,128)} %param.11) | copy-start | bytes 12292
  13.3 67.9 %collective-permute-start.3 = (bf16[160,6144]{1,0:T(8,128)(2,1)S(1)}, bf16[160,6144]{1,0:T(8,128)(2,1)}, u32[]{:S(2)}, u32[]{:S(2)}) collective-permute-start(bf16[160,6144]{1,0:T(8,128)(2,1)S(1)} %shard_map.91), channel_id=1, source_target_pairs={{0,1},{1,0},{2,3},{3,2},{4,5},{5,4},{6,7},{7,6},{8,9},{9,8},{10,11... | collective-permute-start | bytes 5898248 | tf_op jit(solution)/shard_map/ppermute | solution.py:46
  17.1 4.7 %collective-permute-start.2 = (f16[2,208,384]{2,1,0:T(8,128)(2,1)}, f16[2,208,384]{2,1,0:T(8,128)(2,1)S(1)}, u32[]{:S(2)}, u32[]{:S(2)}) collective-permute-start(f16[2,208,384]{2,1,0:T(8,128)(2,1)} %get-tuple-element.25), channel_id=1, source_target_pairs={{0,1},{1,0},{2,3},{3,2},{4,5},{5,4},{6,7},{7,6},{8,9},{9,8},{10,11... | collective-permute-start | bytes 958472 | tf_op jit(solution)/shard_map/ppermute | solution.py:46
  19.9 66.7 %collective-permute-start = (f32[160,192]{1,0:T(8,128)S(1)}, f32[160,192]{1,0:T(8,128)}, u32[]{:S(2)}, u32[]{:S(2)}) collective-permute-start(f32[160,192]{1,0:T(8,128)S(1)} %slice_select_fusion), channel_id=1, source_target_pairs={{0,1},{1,0},{2,3},{3,2},{4,5},{5,4},{6,7},{7,6},{8,9},{9,8},{10,11... | collective-permute-start | bytes 368648 | tf_op jit(solution)/shard_map/ppermute | solution.py:46
  81.2 6.5 %copy-start.3 = (bf16[12,2,1,128,384]{4,3,2,1,0:T(8,128)(2,1)}, bf16[12,2,1,128,384]{4,3,2,1,0:T(8,128)(2,1)S(1)}, u32[]{:S(2)}) copy-start(bf16[12,2,1,128,384]{4,3,2,1,0:T(8,128)(2,1)S(1)} %get-tuple-element.16) | copy-start | bytes 7077892
  81.2 8.7 %copy-start.5 = (bf16[12,2,1,128,384]{4,3,2,1,0:T(8,128)(2,1)}, bf16[12,2,1,128,384]{4,3,2,1,0:T(8,128)(2,1)S(1)}, u32[]{:S(2)}) copy-start(bf16[12,2,1,128,384]{4,3,2,1,0:T(8,128)(2,1)S(1)} %get-tuple-element.15) | copy-start | bytes 7077892
  91.4 22.8 %collective-permute-start.9 = (f32[24,160,128]{2,1,0:T(8,128)}, f32[24,160,128]{2,1,0:T(8,128)}, u32[]{:S(2)}, u32[]{:S(2)}) collective-permute-start(f32[24,160,128]{2,1,0:T(8,128)} %convolution_bitcast_fusion), channel_id=1, source_target_pairs={{0,1},{1,0},{2,3},{3,2},{4,5},{5,4},{6,7},{7,6},{8,9},{9,8},{10,11... | collective-permute-start | bytes 5898248 | tf_op jit(solution)/shard_map/ppermute | solution.py:46
  96.2 8.3 %collective-permute-start.5 = (f32[12,160,128]{2,1,0:T(8,128)}, f32[12,160,128]{2,1,0:T(8,128)}, u32[]{:S(2)}, u32[]{:S(2)}) collective-permute-start(f32[12,160,128]{2,1,0:T(8,128)} %convolution_bitcast_fusion.1), channel_id=1, source_target_pairs={{0,1},{1,0},{2,3},{3,2},{4,5},{5,4},{6,7},{7,6},{8,9},{9,8},{10,11... | collective-permute-start | bytes 2949128 | tf_op jit(solution)/shard_map/ppermute | solution.py:46
  98.7 5.8 %copy-start.6 = (bf16[12,2,1,128,384]{4,3,2,1,0:T(8,128)(2,1)S(1)}, bf16[12,2,1,128,384]{4,3,2,1,0:T(8,128)(2,1)}, u32[]{:S(2)}) copy-start(bf16[12,2,1,128,384]{4,3,2,1,0:T(8,128)(2,1)} %copy-done.5) | copy-start | bytes 7077892
  98.7 24.9 %collective-permute-start.4 = (f32[12,160,128]{2,1,0:T(8,128)}, f32[12,160,128]{2,1,0:T(8,128)S(1)}, u32[]{:S(2)}, u32[]{:S(2)}) collective-permute-start(f32[12,160,128]{2,1,0:T(8,128)} %convolution_bitcast_fusion.4), channel_id=1, source_target_pairs={{0,1},{1,0},{2,3},{3,2},{4,5},{5,4},{6,7},{7,6},{8,9},{9,8},{10,11... | collective-permute-start | bytes 2949128 | tf_op jit(solution)/shard_map/ppermute | solution.py:46
  104.3 9.9 %copy-start.4 = (bf16[12,2,1,128,384]{4,3,2,1,0:T(8,128)(2,1)S(1)}, bf16[12,2,1,128,384]{4,3,2,1,0:T(8,128)(2,1)}, u32[]{:S(2)}) copy-start(bf16[12,2,1,128,384]{4,3,2,1,0:T(8,128)(2,1)} %copy-done.3) | copy-start | bytes 7077892
  106.4 19.6 %collective-permute-start.6 = (bf16[12,160,128]{2,1,0:T(8,128)(2,1)S(1)}, bf16[12,160,128]{2,1,0:T(8,128)(2,1)S(1)}, u32[]{:S(2)}, u32[]{:S(2)}) collective-permute-start(bf16[12,160,128]{2,1,0:T(8,128)(2,1)S(1)} %fusion.3), channel_id=1, source_target_pairs={{0,32},{32,0},{1,33},{33,1},{2,34},{34,2},{3,35},{35,3},{4,36},{36... | collective-permute-start | bytes 1474568 | tf_op jit(solution)/shard_map/ppermute | solution.py:152
  116.8 16.6 %collective-permute-start.10 = (bf16[4,2,160,128]{3,2,0,1:T(8,128)(2,1)S(1)}, bf16[4,2,160,128]{3,2,0,1:T(8,128)(2,1)S(1)}, u32[]{:S(2)}, u32[]{:S(2)}) collective-permute-start(bf16[4,2,160,128]{3,2,0,1:T(8,128)(2,1)S(1)} %bitcast.135), channel_id=1, source_target_pairs={{0,64},{64,128},{128,0},{192,256},{256,320},{320,192},{384,448},{4... | collective-permute-start | bytes 983048 | tf_op jit(solution)/shard_map/ppermute | solution.py:152
  118.8 18.5 %collective-permute-start.11 = (bf16[4,2,160,128]{3,2,0,1:T(8,128)(2,1)S(1)}, bf16[4,2,160,128]{3,2,0,1:T(8,128)(2,1)S(1)}, u32[]{:S(2)}, u32[]{:S(2)}) collective-permute-start(bf16[4,2,160,128]{3,2,0,1:T(8,128)(2,1)S(1)} %bitcast.136), channel_id=1, source_target_pairs={{0,128},{64,0},{128,64},{192,320},{256,192},{320,256},{384,512},{4... | collective-permute-start | bytes 983048 | tf_op jit(solution)/shard_map/ppermute | solution.py:152
  126.7 14.1 %collective-permute-start.7 = (bf16[4,160,128]{2,1,0:T(8,128)(2,1)S(1)}, bf16[4,160,128]{2,1,0:T(8,128)(2,1)S(1)}, u32[]{:S(2)}, u32[]{:S(2)}) collective-permute-start(bf16[4,160,128]{2,1,0:T(8,128)(2,1)S(1)} %get-tuple-element.19), channel_id=1, source_target_pairs={{0,64},{64,128},{128,0},{192,256},{256,320},{320,192},{384,448},{4... | collective-permute-start | bytes 491528 | tf_op jit(solution)/shard_map/ppermute | solution.py:152
  128.6 14.9 %collective-permute-start.8 = (bf16[4,160,128]{2,1,0:T(8,128)(2,1)S(1)}, bf16[4,160,128]{2,1,0:T(8,128)(2,1)S(1)}, u32[]{:S(2)}, u32[]{:S(2)}) collective-permute-start(bf16[4,160,128]{2,1,0:T(8,128)(2,1)S(1)} %get-tuple-element.20), channel_id=1, source_target_pairs={{0,128},{64,0},{128,64},{192,320},{256,192},{320,256},{384,512},{4... | collective-permute-start | bytes 491528 | tf_op jit(solution)/shard_map/ppermute | solution.py:152
  137.4 7.8 %collective-permute-start.12 = (bf16[4,160,128]{2,1,0:T(8,128)(2,1)S(1)}, bf16[4,160,128]{2,1,0:T(8,128)(2,1)S(1)}, u32[]{:S(2)}, u32[]{:S(2)}) collective-permute-start(bf16[4,160,128]{2,1,0:T(8,128)(2,1)S(1)} %fusion.21), channel_id=1, source_target_pairs={{0,32},{32,0},{1,33},{33,1},{2,34},{34,2},{3,35},{35,3},{4,36},{36... | collective-permute-start | bytes 491528 | tf_op jit(solution)/shard_map/ppermute | solution.py:152
  145.3 20.1 %collective-permute-start.13 = (bf16[160,256]{1,0:T(8,128)(2,1)S(1)}, bf16[160,256]{1,0:T(8,128)(2,1)S(1)}, u32[]{:S(2)}, u32[]{:S(2)}) collective-permute-start(bf16[160,256]{1,0:T(8,128)(2,1)S(1)} %get-tuple-element.21), channel_id=1, source_target_pairs={{0,192},{64,256},{128,320},{192,384},{256,448},{320,512},{384,576}... | collective-permute-start | bytes 245768 | tf_op jit(solution)/shard_map/ppermute | solution.py:152
  151.2 16.9 %collective-permute-start.14 = (bf16[160,256]{1,0:T(8,128)(2,1)S(1)}, bf16[160,256]{1,0:T(8,128)(2,1)S(1)}, u32[]{:S(2)}, u32[]{:S(2)}) collective-permute-start(bf16[160,256]{1,0:T(8,128)(2,1)S(1)} %get-tuple-element.22), channel_id=1, source_target_pairs={{0,384},{64,448},{128,512},{192,576},{256,640},{320,704},{384,0},{... | collective-permute-start | bytes 245768 | tf_op jit(solution)/shard_map/ppermute | solution.py:152
  161.8 9.9 %collective-permute-start.15 = (bf16[160,256]{1,0:T(8,128)(2,1)S(1)}, bf16[160,256]{1,0:T(8,128)(2,1)S(1)}, u32[]{:S(2)}, u32[]{:S(2)}) collective-permute-start(bf16[160,256]{1,0:T(8,128)(2,1)S(1)} %get-tuple-element.23), channel_id=1, source_target_pairs={{0,576},{64,640},{128,704},{192,0},{256,64},{320,128},{384,192},{4... | collective-permute-start | bytes 245768 | tf_op jit(solution)/shard_map/ppermute | solution.py:152
  (5 other events, 16.2 us)
